TPU v7x, 256 devices: a whole 4x4x8 slice. The times are simulated.
256 devices in a mesh: dp: 8 (over x_hi, y), group: 2 (over x_lo), seq: 16 (over z, core).
Axes of the slice: x: 4 (x_hi: 2, x_lo: 2; x = x_hi * 2 + x_lo), y: 4, z: 8, core: 2. Of those that a mesh axis runs over, the one named last changes fastest.
Arguments:
- student_hidden: bfloat16 [8, 1280, 5120], P('dp', 'seq'), may hold values from -6 to 6
- student_mod: float32 [2, 5120], replicated, may hold values from -3 to 3
- student_out: bfloat16 [5120, 64], replicated, may hold values from -0.078125 to 0.078125
- score_stream: bfloat16 [2, 8, 1280, 5120], P('group', 'dp', 'seq')
- score_in: bfloat16 [2, 64, 5120], P('group'), may hold values from -0.75 to 0.75
- score_mod: float32 [2, 16, 2, 5120], P('group'), may hold values from -3 to 3
- attention_in: bfloat16 [2, 5120, 3, 4096], P('group', None, None, 'seq')
- head_out: bfloat16 [2, 32, 128, 64], P('group', 'seq'), may hold values from -6 to 6
- step_index: int32 [8], P('dp'), may hold values from 0 to 15
- lengths: int32 [8], P('dp'), may hold values from 1 to 1280, 6400 in all
- noise: bfloat16 [8, 64, 1280], P('dp', None, 'seq'), may hold values from -6 to 6
Outputs:
- latent_gradient: float32 [8, 64, 1280], P('dp', 'group', 'seq')
Inputs may be any that keep to these rules, and one draw needn't show every extreme that they name: `lengths`: one sample in every draw has all 1280 tokens valid.
All inputs are finite; a program needn't handle non-finite values. No bound on the sum of `lengths` on one device may be relied on, other than what follows from the above.
Results may differ from a plain program's by a relative error of at most 0.0045.
Values may be sent and summed in bfloat16 or wider, within the bound.
No kernel may reach another device: no remote copies, remote signals or barrier semaphores. Data moves between devices by JAX's collectives and lax.ppermute only.
A program may use at most 128 MiB of HBM per device.

v0:
```python
import jax
import jax.numpy as jnp
from jax import lax
from jax.sharding import PartitionSpec as P

epsilon = 1e-06


def from_partner(block, axis, apart):
    count = lax.axis_size(axis)
    route = []
    for low in range(count):
        high = low | 1 << apart
        if high != low and high < count:
            route += [(low, high), (high, low)]
    return lax.ppermute(block, axis, route)


def layer_norm(values):
    average = jnp.mean(values, -1, keepdims=True)
    centered = values - average
    variance = jnp.mean(centered * centered, -1, keepdims=True)
    return centered * lax.rsqrt(variance + epsilon)


def local(
    student_hidden,
    student_mod,
    student_out,
    score_stream,
    score_in,
    score_mod,
    attention_in,
    head_out,
    step_index,
    lengths,
    noise,
):
    groups = lax.axis_size("group")
    seq_count = lax.axis_size("seq")
    group_at = lax.axis_index("group")
    seq_at = lax.axis_index("seq")
    own_count = student_hidden.shape[1]
    tokens = own_count * seq_count
    patch_width = noise.shape[1]
    half_width = patch_width // groups
    level_count = score_mod.shape[1]
    heads_here = head_out.shape[1]
    head_size = head_out.shape[2]
    width = attention_in.shape[1]
    score_scale = head_size ** (-0.5)
    step_now = step_index[0]
    length = lengths[0]
    student_normed = (
        layer_norm(student_hidden[0].astype(jnp.float32)) * (1.0 + student_mod[1]) + student_mod[0]
    ).astype(jnp.bfloat16)
    latent = jnp.einsum(
        "ld,dp->pl", student_normed, student_out, preferred_element_type=jnp.float32
    )
    noise_level = (step_now.astype(jnp.float32) + 1.0) / (level_count + 1.0)
    noised_cols = (
        (1.0 - noise_level) * latent + noise_level * noise[0].astype(jnp.float32)
    ).astype(jnp.bfloat16)
    selected = jnp.arange(level_count, dtype=jnp.int32) == step_now
    modulation = jnp.sum(jnp.where(selected[:, None, None], score_mod[0], 0.0), 0)
    embed_weight = score_in[0]
    projection = attention_in[0].reshape(width, 3 * heads_here * head_size)
    head_weights = head_out[0]
    own_stream = score_stream[0, 0]

    def normalize(columns, stream_rows):
        embedded = stream_rows.astype(jnp.float32) + jnp.einsum(
            "pn,pd->nd", columns, embed_weight, preferred_element_type=jnp.float32
        )
        return (layer_norm(embedded) * (1.0 + modulation[1]) + modulation[0]).astype(jnp.bfloat16)

    def project(piece):
        return jnp.dot(piece, projection, preferred_element_type=jnp.float32).astype(jnp.bfloat16)

    all_cols, all_stream = (
        lax.all_gather(noised_cols, "seq", axis=1, tiled=True),
        lax.all_gather(own_stream, "seq", axis=0, tiled=True),
    )
    block_rows = tokens // 4

    def one_block(index):
        columns = lax.dynamic_slice_in_dim(all_cols, index * block_rows, block_rows, 1)
        stream_rows = lax.dynamic_slice_in_dim(all_stream, index * block_rows, block_rows, 0)
        return project(normalize(columns, stream_rows))

    projected = lax.map(one_block, jnp.arange(4, dtype=jnp.int32)).reshape(
        tokens, 3 * heads_here * head_size
    )
    split_heads = projected.reshape(tokens, 3, heads_here, head_size).transpose(1, 2, 0, 3)
    query_heads = split_heads[0]
    key_heads = split_heads[1]
    value_heads = split_heads[2]
    key_valid = jnp.arange(tokens, dtype=jnp.int32) < length

    def one_head(operands):
        query_rows, key_rows, value_rows, head_weight = operands
        scores = jnp.dot(query_rows, key_rows.T, preferred_element_type=jnp.float32) * score_scale
        scores = jnp.where(key_valid[None, :], scores, -1e30)
        highest = jnp.max(scores, -1, keepdims=True)
        lifted = jnp.exp(scores - highest)
        chances = (lifted / jnp.sum(lifted, -1, keepdims=True)).astype(jnp.bfloat16)
        mixture = jnp.dot(chances, value_rows, preferred_element_type=jnp.float32).astype(
            jnp.bfloat16
        )
        return jnp.dot(mixture, head_weight, preferred_element_type=jnp.float32)

    head_share = lax.psum_scatter(
        jnp.sum(lax.map(one_head, (query_heads, key_heads, value_heads, head_weights)), 0).reshape(
            lax.axis_size("seq") * (own_count // 2), 2 * patch_width
        ),
        "seq",
        scatter_dimension=0,
        tiled=True,
    )
    head_share = head_share.reshape(own_count, groups, half_width)
    mine = lax.dynamic_slice_in_dim(head_share, group_at, 1, 1)
    wanted = lax.dynamic_slice_in_dim(head_share, 1 - group_at, 1, 1)
    received = from_partner(wanted, "group", 0)
    difference = jnp.where(group_at == 0, mine - received, received - mine)
    own_places = seq_at * own_count + jnp.arange(own_count, dtype=jnp.int32)
    gradient = difference.reshape(own_count, half_width)
    gradient = jnp.where((own_places < length)[:, None], gradient, 0.0)
    return gradient.T[None]


def solution(mesh):
    return jax.shard_map(
        local,
        mesh=mesh,
        in_specs=(
            P("dp", "seq", None),
            P(),
            P(),
            P("group", "dp", "seq", None),
            P("group", None, None),
            P("group", None, None, None),
            P("group", None, None, "seq"),
            P("group", "seq", None, None),
            P("dp"),
            P("dp"),
            P("dp", None, "seq"),
        ),
        out_specs=P("dp", "group", "seq"),
        check_vma=False,
    )
```

profile of v0, /device:TPU:16, one launch (start us, length us, event | category | flops | bytes accessed | tf_op | source)
XLA Modules:
  0.0 221.1 jit_solution(1359893586088819588)
XLA Ops:
  9.3 1.5 fusion.33
  11.8 1.7 fusion.40
  13.5 21.3 %all-gather.1 = bf16[16,80,64]{1,2,0:T(8,128)(2,1)S(1)} all-gather(bf16[1,80,64]{1,2,0:T(8,128)(2,1)S(1)} %fusion.40), channel_id=1, replica_groups=mesh['dp'=8,'group'=2,'seq'=16] {'seq'}, dimensions={0}, use_global_device_ids=true | all-gather | bytes 174080 | tf_op jit(solution)/shard_map/all_gather | solution.py:81
  35.3 10.8 %copy.23 = bf16[1,5120,3,256]{1,3,2,0:T(8,128)(2,1)} copy(bf16[1,5120,3,256]{3,1,2,0:T(8,128)(2,1)} %param.21) | data formatting | bytes 15728640 | tf_op args[6]
  46.1 10.8 %copy.24 = bf16[5120,768]{1,0:T(8,128)(2,1)} copy(bf16[5120,768]{0,1:T(8,128)(2,1)} %bitcast.115) | data formatting | bytes 15728640 | tf_op jit(solution)/shard_map/while | solution.py:91
  58.5 32.3 %all-gather.4.cloned.1.call-done = bf16[1,1,1280,5120]{3,2,1,0:T(8,128)(2,1)} async-done(((bf16[1,1,80,5120]{3,2,1,0:T(8,128)(2,1)}), bf16[1,1,1280,5120]{3,2,1,0:T(8,128)(2,1)}) %all-gather.4.cloned.1.call-update) | async-done | bytes 13107216 | tf_op jit(solution)/shard_map/all_gather | solution.py:82
  90.8 34.4 %while.21 = (s32[]{:T(128)}, bf16[4,320,768]{2,1,0:T(8,128)(2,1)S(1)}, s32[4]{0:T(128)S(1)}, bf16[1280,5120]{1,0:T(8,128)(2,1)}, bf16[64,1280]{1,0:T(8,128)(2,1)...) while((s32[]{:T(128)}, ...), condition=%wide.region_6.7_spmd, body=%wide.region_3.6_spmd.sunk | while | flops 2744571136 | bytes 55728096 | solution.py:91
  92.1 3.3 %fusion.63 = (f32[320]{0:T(512)S(1)}, f32[320,5120]{1,0:T(8,128)S(1)}) fusion(bf16[64,5120]{1,0:T(8,128)(2,1)S(1)} %get-tuple-element.307, bf16[64,1280]{1,0:T(8,128)(2,1)S(1)} %get-tuple-element.306, s32[]{:T(128)S(6)} %select_n.45, bf16[1280,5120]{1,0:T(8,128)(2,1)} %get-tuple-element.305), kind=kOutput, calls=%fused_computation.68.clone.1 | convolution fusion | flops 214630080 | bytes 10537216 | tf_op jit(solution)/shard_map/while/body/eval_jaxpr/pn,pd->nd/dot_general | solution.py:72
  96.4 3.0 %fusion.64 = bf16[4,320,768]{2,1,0:T(8,128)(2,1)S(1)} fusion(bf16[4,320,768]{2,1,0:T(8,128)(2,1)S(1)} %get-tuple-element.291, s32[]{:T(128)} %get-tuple-element.290, bf16[5120,768]{1,0:T(8,128)(2,1)S(1)} %bitcast.119, f32[320,5120]{1,0:T(8,128)S(1)} %get-tuple-element.265, f32[5120]{0:T(1024)S(1)} %bitcast.123, f32[5120]{0:T(1024)S(1)} %bitcast.122, ...), kind=kOutput, calls=%fused_computation.11.clone.1 | convolution fusion | flops 2525020160 | bytes 14954500 | tf_op jit(solution)/shard_map/while/body/eval_jaxpr/dot_general | solution.py:78
  100.7 3.3 %fusion.63 = (f32[320]{0:T(512)S(1)}, f32[320,5120]{1,0:T(8,128)S(1)}) fusion(bf16[64,5120]{1,0:T(8,128)(2,1)S(1)} %get-tuple-element.307, bf16[64,1280]{1,0:T(8,128)(2,1)S(1)} %get-tuple-element.306, s32[]{:T(128)S(6)} %select_n.45, bf16[1280,5120]{1,0:T(8,128)(2,1)} %get-tuple-element.305), kind=kOutput, calls=%fused_computation.68.clone.1 | convolution fusion | flops 214630080 | bytes 10537216 | tf_op jit(solution)/shard_map/while/body/eval_jaxpr/pn,pd->nd/dot_general | solution.py:72
  105.0 3.0 %fusion.64 = bf16[4,320,768]{2,1,0:T(8,128)(2,1)S(1)} fusion(bf16[4,320,768]{2,1,0:T(8,128)(2,1)S(1)} %get-tuple-element.291, s32[]{:T(128)} %get-tuple-element.290, bf16[5120,768]{1,0:T(8,128)(2,1)S(1)} %bitcast.119, f32[320,5120]{1,0:T(8,128)S(1)} %get-tuple-element.265, f32[5120]{0:T(1024)S(1)} %bitcast.123, f32[5120]{0:T(1024)S(1)} %bitcast.122, ...), kind=kOutput, calls=%fused_computation.11.clone.1 | convolution fusion | flops 2525020160 | bytes 14954500 | tf_op jit(solution)/shard_map/while/body/eval_jaxpr/dot_general | solution.py:78
  109.3 3.3 %fusion.63 = (f32[320]{0:T(512)S(1)}, f32[320,5120]{1,0:T(8,128)S(1)}) fusion(bf16[64,5120]{1,0:T(8,128)(2,1)S(1)} %get-tuple-element.307, bf16[64,1280]{1,0:T(8,128)(2,1)S(1)} %get-tuple-element.306, s32[]{:T(128)S(6)} %select_n.45, bf16[1280,5120]{1,0:T(8,128)(2,1)} %get-tuple-element.305), kind=kOutput, calls=%fused_computation.68.clone.1 | convolution fusion | flops 214630080 | bytes 10537216 | tf_op jit(solution)/shard_map/while/body/eval_jaxpr/pn,pd->nd/dot_general | solution.py:72
  113.6 3.0 %fusion.64 = bf16[4,320,768]{2,1,0:T(8,128)(2,1)S(1)} fusion(bf16[4,320,768]{2,1,0:T(8,128)(2,1)S(1)} %get-tuple-element.291, s32[]{:T(128)} %get-tuple-element.290, bf16[5120,768]{1,0:T(8,128)(2,1)S(1)} %bitcast.119, f32[320,5120]{1,0:T(8,128)S(1)} %get-tuple-element.265, f32[5120]{0:T(1024)S(1)} %bitcast.123, f32[5120]{0:T(1024)S(1)} %bitcast.122, ...), kind=kOutput, calls=%fused_computation.11.clone.1 | convolution fusion | flops 2525020160 | bytes 14954500 | tf_op jit(solution)/shard_map/while/body/eval_jaxpr/dot_general | solution.py:78
  117.9 3.3 %fusion.63 = (f32[320]{0:T(512)S(1)}, f32[320,5120]{1,0:T(8,128)S(1)}) fusion(bf16[64,5120]{1,0:T(8,128)(2,1)S(1)} %get-tuple-element.307, bf16[64,1280]{1,0:T(8,128)(2,1)S(1)} %get-tuple-element.306, s32[]{:T(128)S(6)} %select_n.45, bf16[1280,5120]{1,0:T(8,128)(2,1)} %get-tuple-element.305), kind=kOutput, calls=%fused_computation.68.clone.1 | convolution fusion | flops 214630080 | bytes 10537216 | tf_op jit(solution)/shard_map/while/body/eval_jaxpr/pn,pd->nd/dot_general | solution.py:72
  122.2 3.0 %fusion.64 = bf16[4,320,768]{2,1,0:T(8,128)(2,1)S(1)} fusion(bf16[4,320,768]{2,1,0:T(8,128)(2,1)S(1)} %get-tuple-element.291, s32[]{:T(128)} %get-tuple-element.290, bf16[5120,768]{1,0:T(8,128)(2,1)S(1)} %bitcast.119, f32[320,5120]{1,0:T(8,128)S(1)} %get-tuple-element.265, f32[5120]{0:T(1024)S(1)} %bitcast.123, f32[5120]{0:T(1024)S(1)} %bitcast.122, ...), kind=kOutput, calls=%fused_computation.11.clone.1 | convolution fusion | flops 2525020160 | bytes 14954500 | tf_op jit(solution)/shard_map/while/body/eval_jaxpr/dot_general | solution.py:78
  126.5 3.9 %reshape_reshape.3 = bf16[1280,3,2,128]{3,2,1,0:T(2,128)(2,1)S(1)} reshape(bf16[4,320,768]{2,1,0:T(8,128)(2,1)} %copy-done.3) | data formatting | bytes 3932160 | tf_op jit(solution)/shard_map/reshape;reshape | solution.py:94
  132.9 19.4 %while.22 = (s32[]{:T(128)}, f32[2,1280,64]{1,2,0:T(8,128)S(1)}, bf16[2,1280,128]{2,1,0:T(8,128)(2,1)S(1)}, bf16[2,1280,128]{2,1,0:T(8,128)(2,1)S(1)}, bf16[2,12...) while((s32[]{:T(128)}, f32[2,1280,64]{1,2,0:T(8,128)S(1)}, ...), condition=%wide.region_10.11_spmd.clone, body=%wide.region_7.10_spmd.clone.sunk | while | flops 873102080 | bytes 47256436 | solution.py:113
  134.7 2.7 %copy-done.1 = f32[1280,1280]{0,1:T(8,128)} copy-done((f32[1280,1280]{0,1:T(8,128)}, f32[1280,1280]{0,1:T(8,128)S(1)}, u32[]{:S(2)}) %copy-start.1) | copy-done | bytes 6553624 | tf_op jit(solution)/shard_map/while
  138.4 4.2 %fusion.69 = f32[2,1280,64]{1,2,0:T(8,128)S(1)} fusion(f32[2,1280,64]{1,2,0:T(8,128)S(1)} %get-tuple-element.323, s32[]{:T(128)} %get-tuple-element.322, f32[1280,1280]{0,1:T(8,128)} %copy-done.1, f32[1280]{0:T(1024)S(1)} %fusion.68, f32[1280]{0:T(1024)S(1)} %get-tuple-element.277, bf16[2,1280,128]{2,1,0:T(8,128)(2,1)} %get-tuple-element.334, ...), kind=kOutput, calls=%fused_computation.25.clone.1 | convolution fusion | flops 445480960 | bytes 7259648 | tf_op jit(solution)/shard_map/while/body/eval_jaxpr/dot_general | solution.py:110
  144.4 2.7 %copy-done.1 = f32[1280,1280]{0,1:T(8,128)} copy-done((f32[1280,1280]{0,1:T(8,128)}, f32[1280,1280]{0,1:T(8,128)S(1)}, u32[]{:S(2)}) %copy-start.1) | copy-done | bytes 6553624 | tf_op jit(solution)/shard_map/while
  148.1 4.2 %fusion.69 = f32[2,1280,64]{1,2,0:T(8,128)S(1)} fusion(f32[2,1280,64]{1,2,0:T(8,128)S(1)} %get-tuple-element.323, s32[]{:T(128)} %get-tuple-element.322, f32[1280,1280]{0,1:T(8,128)} %copy-done.1, f32[1280]{0:T(1024)S(1)} %fusion.68, f32[1280]{0:T(1024)S(1)} %get-tuple-element.277, bf16[2,1280,128]{2,1,0:T(8,128)(2,1)} %get-tuple-element.334, ...), kind=kOutput, calls=%fused_computation.25.clone.1 | convolution fusion | flops 445480960 | bytes 7259648 | tf_op jit(solution)/shard_map/while/body/eval_jaxpr/dot_general | solution.py:110
  154.2 54.3 %reduce-scatter.4.cloned.1.call-done = f32[40,128]{1,0:T(8,128)} async-done(((f32[640,128]{1,0:T(8,128)}), f32[40,128]{1,0:T(8,128)}) %reduce-scatter.4.cloned.1.call-update) | async-done | bytes 20496
  209.4 1.7 collective-permute-start
  211.1 2.4 %collective-permute-done = f32[80,1,32]{2,1,0:T(1,128)S(1)} collective-permute-done((f32[80,1,32]{2,1,0:T(1,128)S(1)}, f32[80,1,32]{2,1,0:T(1,128)S(1)}, u32[]{:S(2)}, u32[]{:S(2)}) %collective-permute-start) | collective-permute-done | bytes 10272 | tf_op jit(solution)/shard_map/ppermute | solution.py:16
  (87 shorter events, 23.6 us)
Async XLA Ops:
  6.5 5.3 %copy-start = (bf16[5120,64]{0,1:T(8,128)(2,1)S(1)}, bf16[5120,64]{0,1:T(8,128)(2,1)}, u32[]{:S(2)}) copy-start(bf16[5120,64]{0,1:T(8,128)(2,1)} %param.17) | copy-start | bytes 1966084
  6.5 84.3 %all-gather.4.cloned.1.call-start = ((), (), s32[]{:S(2)}) async-start(), calls=%async_computation.1 | async-start | bytes 13926400 | tf_op jit(solution)/shard_map/all_gather | solution.py:82
  7.3 201.2 %reduce-scatter.4.cloned.1.call-start = ((), (), s32[]{:S(2)}) async-start(), calls=%async_computation.2 | async-start | bytes 348160
  46.1 10.8 %copy-start.5 = (bf16[1,2,128,64]{2,3,1,0:T(8,128)(2,1)S(1)}, bf16[1,2,128,64]{2,3,1,0:T(8,128)(2,1)}, u32[]{:S(2)}) copy-start(bf16[1,2,128,64]{2,3,1,0:T(8,128)(2,1)} %param.22) | copy-start | bytes 98308
  46.1 44.8 %copy-start.2 = (bf16[1,64,5120]{2,1,0:T(8,128)(2,1)S(1)}, bf16[1,64,5120]{2,1,0:T(8,128)(2,1)}, u32[]{:S(2)}) copy-start(bf16[1,64,5120]{2,1,0:T(8,128)(2,1)} %param.19) | copy-start | bytes 1966084
  92.1 4.2 %slice-start = ((s8[7864320]{0:T(1024)(128)(4,1)}), s8[4194304]{0:T(1024)(128)(4,1)S(1)}, s32[]{:S(2)}) async-start(s8[7864320]{0:T(1024)(128)(4,1)} %bitcast.118), calls=%async_computation.3 | async-start | bytes 8388608 | tf_op jit(solution)/shard_map/while
  92.1 4.3 %slice-start.1 = ((s8[7864320]{0:T(1024)(128)(4,1)}), s8[3670016]{0:T(1024)(128)(4,1)S(1)}, s32[]{:S(2)}) async-start(s8[7864320]{0:T(1024)(128)(4,1)} %bitcast.118), calls=%async_computation.4 | async-start | bytes 7340032 | tf_op jit(solution)/shard_map/while
  100.7 4.2 %slice-start = ((s8[7864320]{0:T(1024)(128)(4,1)}), s8[4194304]{0:T(1024)(128)(4,1)S(1)}, s32[]{:S(2)}) async-start(s8[7864320]{0:T(1024)(128)(4,1)} %bitcast.118), calls=%async_computation.3 | async-start | bytes 8388608 | tf_op jit(solution)/shard_map/while
  100.7 4.3 %slice-start.1 = ((s8[7864320]{0:T(1024)(128)(4,1)}), s8[3670016]{0:T(1024)(128)(4,1)S(1)}, s32[]{:S(2)}) async-start(s8[7864320]{0:T(1024)(128)(4,1)} %bitcast.118), calls=%async_computation.4 | async-start | bytes 7340032 | tf_op jit(solution)/shard_map/while
  109.3 4.2 %slice-start = ((s8[7864320]{0:T(1024)(128)(4,1)}), s8[4194304]{0:T(1024)(128)(4,1)S(1)}, s32[]{:S(2)}) async-start(s8[7864320]{0:T(1024)(128)(4,1)} %bitcast.118), calls=%async_computation.3 | async-start | bytes 8388608 | tf_op jit(solution)/shard_map/while
  109.3 4.3 %slice-start.1 = ((s8[7864320]{0:T(1024)(128)(4,1)}), s8[3670016]{0:T(1024)(128)(4,1)S(1)}, s32[]{:S(2)}) async-start(s8[7864320]{0:T(1024)(128)(4,1)} %bitcast.118), calls=%async_computation.4 | async-start | bytes 7340032 | tf_op jit(solution)/shard_map/while
  117.9 4.2 %slice-start = ((s8[7864320]{0:T(1024)(128)(4,1)}), s8[4194304]{0:T(1024)(128)(4,1)S(1)}, s32[]{:S(2)}) async-start(s8[7864320]{0:T(1024)(128)(4,1)} %bitcast.118), calls=%async_computation.3 | async-start | bytes 8388608 | tf_op jit(solution)/shard_map/while
  117.9 4.3 %slice-start.1 = ((s8[7864320]{0:T(1024)(128)(4,1)}), s8[3670016]{0:T(1024)(128)(4,1)S(1)}, s32[]{:S(2)}) async-start(s8[7864320]{0:T(1024)(128)(4,1)} %bitcast.118), calls=%async_computation.4 | async-start | bytes 7340032 | tf_op jit(solution)/shard_map/while
  125.2 1.3 copy-start.3
  126.5 6.4 %copy-start.4 = (f32[2,1280,64]{1,2,0:T(8,128)S(1)}, f32[2,1280,64]{1,2,0:T(8,128)}, u32[]{:S(2)}) copy-start(f32[2,1280,64]{1,2,0:T(8,128)} %custom-call.1) | copy-start | bytes 1966084
  134.7 2.7 %copy-start.1 = (f32[1280,1280]{0,1:T(8,128)}, f32[1280,1280]{0,1:T(8,128)S(1)}, u32[]{:S(2)}) copy-start(f32[1280,1280]{0,1:T(8,128)S(1)} %get-tuple-element.276) | copy-start | bytes 19660804 | tf_op jit(solution)/shard_map/while
  144.4 2.7 %copy-start.1 = (f32[1280,1280]{0,1:T(8,128)}, f32[1280,1280]{0,1:T(8,128)S(1)}, u32[]{:S(2)}) copy-start(f32[1280,1280]{0,1:T(8,128)S(1)} %get-tuple-element.276) | copy-start | bytes 19660804 | tf_op jit(solution)/shard_map/while
  209.4 4.1 %collective-permute-start = (f32[80,1,32]{2,1,0:T(1,128)S(1)}, f32[80,1,32]{2,1,0:T(1,128)S(1)}, u32[]{:S(2)}, u32[]{:S(2)}) collective-permute-start(f32[80,1,32]{2,1,0:T(1,128)S(1)} %constant_dynamic-slice_fusion), channel_id=1, source_target_pairs={{0,16},{16,0},{1,17},{17,1},{2,18},{18,2},{3,19},{19,3},{4,20},{20... | collective-permute-start | bytes 30728 | tf_op jit(solution)/shard_map/ppermute | solution.py:16
Sparse Core Ops, SparseCore 0:
  9.2 81.6 all-gather.3
  153.7 54.7 reduce-scatter.3
where the time goes:
time: 222 us; the launch traced here: 221 us
  waiting for transfers between devices  89.7 us (40%)
  local copies, waits for them, and re-layouts  40.9 us (18%)
  matrix products  37.6 us (17%)
  blocking collectives  21.3 us (10%)
  between operations  14.9 us (7%)
  other arithmetic  12.2 us (5%)
  loops' own time  2.77 us (1%)
    unnamed x3, waiting for transfers between devices  55 us
    all_gather x1, waiting for transfers between devices, local(): lax.all_gather(own_stream, 'seq', axis=0, tiled=True)  32.3 us
    all_gather x1, blocking collectives, local(): lax.all_gather(noised_cols, 'seq', axis=1, tiled=True)  21.3 us
    unnamed x16, local copies, waits for them, and re-layouts  13.6 us
    dot_general x4, matrix products, normalize(): jnp.einsum('pn,pd->nd', columns, embed_weight, preferred_element_type=jnp...  13.2 us
    dot_general x4, matrix products, project(): jnp.dot(piece, projection, preferred_element_type=jnp.float32)  12.1 us
    while x1, local copies, waits for them, and re-layouts, local(): lax.map(one_block, jnp.arange(4, dtype=jnp.int32))  10.8 us
    dot_general x2, matrix products, one_head(): return jnp.dot(mixture, head_weight, preferred_element_type=jnp.float32)  8.39 us
  transfers between devices with their start and end apart: 3, of which 3 were waited for; matrix products, arithmetic and copies ran while one was open for 13% of the time, Pallas kernels for 0%

commit v1 on v0

v1 whole, which is shorter than its diff:
```python
import functools

import jax
import jax.numpy as jnp
from jax import lax
from jax.experimental import pallas as pl
from jax.experimental.pallas import tpu as pltpu
from jax.sharding import PartitionSpec as P

epsilon = 1e-06
LOG2E = 1.4426950408889634
MIB = 1 << 20
NT = (((1,), (1,)), ((), ()))
TN = (((0,), (0,)), ((), ()))
NN = (((1,), (0,)), ((), ()))


def dot(a, b, dims):
    return lax.dot_general(a, b, dims, preferred_element_type=jnp.float32)


def layer_norm(values):
    average = jnp.mean(values, -1, keepdims=True)
    centered = values - average
    variance = jnp.mean(centered * centered, -1, keepdims=True)
    return centered * lax.rsqrt(variance + epsilon)


def own_rows_kernel(
    step_ref, hidden_ref, mod_ref, out_ref, noise_ref, stream_ref, embed_ref, table_ref, normed_ref, *, levels
):
    mod = mod_ref[...]
    student = (
        layer_norm(hidden_ref[...].astype(jnp.float32)) * (1.0 + mod[1:2]) + mod[0:1]
    ).astype(jnp.bfloat16)
    latent = dot(out_ref[...], student, NT)
    step = jnp.full(latent.shape, step_ref[0], jnp.int32).astype(jnp.float32)
    level = (step + 1.0) / (levels + 1.0)
    noised = ((1.0 - level) * latent + level * noise_ref[...].astype(jnp.float32)).astype(jnp.bfloat16)
    embedded = stream_ref[...].astype(jnp.float32) + dot(noised, embed_ref[...], TN)
    table = table_ref[0]
    normed_ref[...] = (layer_norm(embedded) * (1.0 + table[1:2]) + table[0:1]).astype(jnp.bfloat16)


def own_rows(step, hidden, mod, out_t, noise, stream, embed, table):
    rows, width = hidden.shape
    levels = table.shape[0]

    def whole(x):
        return pl.BlockSpec(x.shape, lambda i, s: (0,) * x.ndim)

    return pl.pallas_call(
        functools.partial(own_rows_kernel, levels=levels),
        grid_spec=pltpu.PrefetchScalarGridSpec(
            num_scalar_prefetch=1,
            grid=(1,),
            in_specs=[whole(x) for x in (hidden, mod, out_t, noise, stream, embed)]
            + [pl.BlockSpec((1, 2, width), lambda i, s: (s[0], 0, 0))],
            out_specs=pl.BlockSpec((rows, width), lambda i, s: (0, 0)),
        ),
        out_shape=jax.ShapeDtypeStruct((rows, width), jnp.bfloat16),
        compiler_params=pltpu.CompilerParams(vmem_limit_bytes=40 * MIB),
        cost_estimate=pl.CostEstimate(flops=2 * 10**8, bytes_accessed=5 * 10**6, transcendentals=0),
        name="own_rows",
    )(step, hidden, mod, out_t, noise, stream, embed, table)


def project_kernel(*refs, blocks, rows):
    x_refs = refs[:blocks]
    wa_ref, wb_ref, q_ref, kv_ref, x_buf, w_buf, x_sem, w_sem = refs[blocks:]
    x_copies = [
        pltpu.make_async_copy(x_refs[i], x_buf.at[pl.ds(i * rows, rows)], x_sem.at[i]) for i in range(blocks)
    ]
    w_copies = []
    for n in range(6):
        source = wa_ref if n < 3 else wb_ref
        w_copies.append(pltpu.make_async_copy(source.at[n % 3], w_buf.at[n], w_sem.at[n]))
    for copy in x_copies + w_copies:
        copy.start()
    for copy in x_copies:
        copy.wait()
    for n in range(6):
        w_copies[n].wait()
        value = dot(x_buf[...], w_buf[n], NN).astype(jnp.bfloat16)
        pair, kind = n // 3, n % 3
        if kind == 0:
            q_ref[pair] = value
        else:
            kv_ref[2 * pair + kind - 1] = value


def project(xs, wa, wb):
    blocks = len(xs)
    rows, width = xs[0].shape
    columns = wa.shape[2]
    total = blocks * rows
    return pl.pallas_call(
        functools.partial(project_kernel, blocks=blocks, rows=rows),
        in_specs=[pl.BlockSpec(memory_space=pl.ANY)] * (blocks + 2),
        out_specs=[pl.BlockSpec(memory_space=pltpu.VMEM)] * 2,
        out_shape=[
            jax.ShapeDtypeStruct((2, total, columns), jnp.bfloat16),
            jax.ShapeDtypeStruct((4, total, columns), jnp.bfloat16),
        ],
        scratch_shapes=[
            pltpu.VMEM((total, width), jnp.bfloat16),
            pltpu.VMEM((6, width, columns), jnp.bfloat16),
            pltpu.SemaphoreType.DMA((blocks,)),
            pltpu.SemaphoreType.DMA((6,)),
        ],
        compiler_params=pltpu.CompilerParams(vmem_limit_bytes=40 * MIB),
        cost_estimate=pl.CostEstimate(
            flops=2 * total * width * 6 * columns,
            bytes_accessed=12 * width * columns + 2 * total * width,
            transcendentals=0,
        ),
        name="project_rows",
    )(*xs, wa, wb)


def attend_kernel(
    place_ref, bias_ref, ha_ref, hb_ref, *refs, calls, rows, sizes, head_size, scale
):
    q_refs = refs[:calls]
    own_refs = refs[calls : 2 * calls]
    far_refs = refs[2 * calls : 3 * calls]
    out_ref, q_buf, k_buf, v_buf, mix = refs[3 * calls :]
    own = sum(sizes)
    at = 0
    for i, size in enumerate(sizes):
        for pair in range(2):
            q_buf[pair, pl.ds(at, size)] = q_refs[i][pair]
            k_buf[pair, pl.ds(at, size)] = own_refs[i][2 * pair]
            v_buf[pair, pl.ds(at, size)] = own_refs[i][2 * pair + 1]
            k_buf[pair, pl.ds(own + at, size)] = far_refs[i][2 * (1 - pair)]
            v_buf[pair, pl.ds(own + at, size)] = far_refs[i][2 * (1 - pair) + 1]
        at += size
    chunk = 160

    @pl.loop(0, own // chunk)
    def _(step):
        here = pl.ds(pl.multiple_of(step * chunk, chunk), chunk)
        bias = bias_ref[...]
        for pair in range(2):
            for sub in range(2):
                lanes = pl.ds(sub * head_size, head_size)
                scores = dot(q_buf[pair, here, lanes], k_buf[pair, :, lanes], NT) * scale + bias
                highest = jnp.max(scores, -1, keepdims=True)
                lifted = jnp.exp2(scores - highest)
                total = jnp.sum(lifted, -1, keepdims=True)
                mixed = dot(lifted.astype(jnp.bfloat16), v_buf[pair, :, lanes], NN) / total
                mix[here, pl.ds((2 * pair + sub) * head_size, head_size)] = mixed.astype(jnp.bfloat16)

    half = out_ref.shape[2]
    for j in range(own // rows):
        result = None
        for n in range(4):
            head_ref = ha_ref if n < 2 else hb_ref
            term = dot(head_ref[n % 2], mix[pl.ds(j * rows, rows), pl.ds(n * head_size, head_size)], NT)
            result = term if result is None else result + term
        out_ref[0, place_ref[j]] = result[:half]
        out_ref[1, place_ref[j]] = result[half:]


def attend(place, bias, ha, hb, qs, owns, fars, rows, groups, head_size):
    calls = len(qs)
    sizes = tuple(q.shape[1] for q in qs)
    own = sum(sizes)
    columns = qs[0].shape[2]
    patch = ha.shape[1]
    blocks = own // rows
    vmem = pl.BlockSpec(memory_space=pltpu.VMEM)
    return pl.pallas_call(
        functools.partial(
            attend_kernel,
            calls=calls,
            rows=rows,
            sizes=sizes,
            head_size=head_size,
            scale=head_size ** (-0.5) * LOG2E,
        ),
        in_specs=[pl.BlockSpec(memory_space=pltpu.SMEM)] + [vmem] * (3 + 3 * calls),
        out_specs=vmem,
        out_shape=jax.ShapeDtypeStruct((groups, blocks, patch // groups, rows), jnp.float32),
        scratch_shapes=[
            pltpu.VMEM((2, own, columns), jnp.bfloat16),
            pltpu.VMEM((2, 2 * own, columns), jnp.bfloat16),
            pltpu.VMEM((2, 2 * own, columns), jnp.bfloat16),
            pltpu.VMEM((own, 2 * columns), jnp.bfloat16),
        ],
        compiler_params=pltpu.CompilerParams(vmem_limit_bytes=40 * MIB),
        cost_estimate=pl.CostEstimate(
            flops=16 * own * own * columns, bytes_accessed=10**7, transcendentals=8 * own * own
        ),
        name="attend",
    )(place, bias, ha, hb, *qs, *owns, *fars)


def local(
    student_hidden,
    student_mod,
    student_out,
    score_stream,
    score_in,
    score_mod,
    attention_in,
    head_out,
    step_index,
    lengths,
    noise,
):
    groups = lax.axis_size("group")
    seq_count = lax.axis_size("seq")
    chips = seq_count // 2
    seq_at = lax.axis_index("seq")
    chip_at, core_at = seq_at // 2, seq_at % 2
    rows = student_hidden.shape[1]
    head_size = head_out.shape[2]
    length = lengths[0]

    def hop(block, sign):
        route = []
        for z in range(chips):
            for core in range(2):
                way = sign if core == 0 else -sign
                route.append((2 * z + core, 2 * ((z + way) % chips) + core))
        return lax.ppermute(block, "seq", route)

    def other_core(block):
        return lax.ppermute(block, "seq", [(i, i ^ 1) for i in range(seq_count)])

    normed = own_rows(
        step_index,
        student_hidden[0],
        student_mod,
        student_out.T,
        noise[0],
        score_stream[0, 0],
        score_in[0],
        score_mod[0],
    )
    wa = attention_in[0].transpose(1, 0, 2)
    ha = head_out[0].transpose(0, 2, 1)

    up = [hop(normed, 1)]
    down = [hop(normed, -1)]
    wb = other_core(wa)
    hb = other_core(ha)
    for _ in range(chips // 2 - 2):
        up.append(hop(up[-1], 1))
        down.append(hop(down[-1], -1))
    up.append(hop(up[-1], 1))

    sets = [[normed, up[0], down[0]]] + [[up[k], down[k]] for k in range(1, chips // 2 - 1)] + [[up[-1]]]
    qs, owns, fars = [], [], []
    for xs in sets:
        q, kv = project(xs, wa, wb)
        qs.append(q)
        owns.append(kv)
        fars.append(other_core(kv))

    order = [0]
    for k in range(1, chips // 2):
        order += [-k, k]
    order.append(-(chips // 2))
    apart = jnp.asarray(order, jnp.int32)

    def places(core):
        return (chip_at + jnp.where(core == 0, apart, -apart)) % chips

    def bias_of(core):
        tokens = (places(core) * 2 + core)[:, None] * rows + jnp.arange(rows, dtype=jnp.int32)
        return jnp.where(tokens < length, 0.0, -1e30).reshape(1, chips * rows)

    bias = jnp.concatenate([bias_of(core_at), bias_of(1 - core_at)], 1)
    terms = attend(places(core_at), bias, ha, hb, qs, owns, fars, rows, groups, head_size)

    half = terms.shape[2]
    terms = terms.reshape(groups * chips, half, rows)
    same_core = [[g * seq_count + 2 * z + c for g in range(groups) for z in range(chips)] for c in range(2)]
    terms = lax.all_to_all(terms, ("group", "seq"), 0, 0, axis_index_groups=same_core, tiled=True)
    terms = terms.reshape(groups, chips, half, rows)
    gradient = jnp.sum(terms[0], 0) - jnp.sum(terms[1], 0)
    own_places = seq_at * rows + jnp.arange(rows, dtype=jnp.int32)
    return jnp.where((own_places < length)[None, :], gradient, 0.0)[None]


def solution(mesh):
    return jax.shard_map(
        local,
        mesh=mesh,
        in_specs=(
            P("dp", "seq", None),
            P(),
            P(),
            P("group", "dp", "seq", None),
            P("group", None, None),
            P("group", None, None, None),
            P("group", None, None, "seq"),
            P("group", "seq", None, None),
            P("dp"),
            P("dp"),
            P("dp", None, "seq"),
        ),
        out_specs=P("dp", "group", "seq"),
        check_vma=False,
    )
```

time: 222 us -> 143 us (0.64)
  Pallas kernels: 0 us -> 42.1 us
  matrix products: 37.6 us -> 0 us
  local copies, waits for them, and re-layouts: 40.9 us -> 10.4 us
  waiting for transfers between devices: 89.7 us -> 59.4 us
  starting transfers between devices: 1.76 us -> 28 us
  blocking collectives: 21.3 us -> 0 us
  between operations: 14.9 us -> 1.43 us
  other arithmetic: 12.2 us -> 1.41 us
  loops' own time: 2.77 us -> 0 us
    unnamed x3 -> x0, waiting for transfers between devices: 55 us -> none
    ppermute x1 -> x13, waiting for transfers between devices: 2.36 us -> 48.8 us  [the longest x7 47.5 us: hop(): return lax.ppermute(block, 'seq', route)]
    pallas_call x0 -> x6, Pallas kernels: none -> 42.1 us  [the longest x4 30.2 us: project(): pl.pallas_call(functools.partial(project_kernel, blocks=blocks, rows=rows...]
    dot_general x13 -> x0, matrix products: 37.6 us -> none  [the longest x4 13.2 us: normalize(): jnp.einsum('pn,pd->nd', columns, embed_weight, preferred_element_type=jnp...]
    all_gather x1 -> x0, waiting for transfers between devices: 32.3 us -> none  [local(): lax.all_gather(own_stream, 'seq', axis=0, tiled=True)]
    all_gather x1 -> x0, blocking collectives: 21.3 us -> none  [local(): lax.all_gather(noised_cols, 'seq', axis=1, tiled=True)]
    while x21 -> x0, local copies, waits for them, and re-layouts: 16.7 us -> none  [the longest x1 10.8 us: local(): lax.map(one_block, jnp.arange(4, dtype=jnp.int32))]
    ppermute x1 -> x13, starting transfers between devices: 1.72 us -> 18.1 us  [the longest x7 11.8 us: hop(): return lax.ppermute(block, 'seq', route)]
  transfers between devices with their start and end apart: 3 -> 14, of which waited for: 3 -> 6; matrix products, arithmetic and copies ran while one was open for 13% -> 1% of each run, Pallas kernels for 0% -> 23%
where the time goes in v1:
time: 143 us
  waiting for transfers between devices  59.4 us (42%)
  Pallas kernels  42.1 us (29%)
  starting transfers between devices  28 us (20%)
  local copies, waits for them, and re-layouts  10.4 us (7%)
  between operations  1.43 us (1%)
    ppermute x7, waiting for transfers between devices, hop(): return lax.ppermute(block, 'seq', route)  47.5 us
    pallas_call x4, Pallas kernels, project(): pl.pallas_call(functools.partial(project_kernel, blocks=blocks, rows=rows...  30.2 us
    ppermute x7, starting transfers between devices, hop(): return lax.ppermute(block, 'seq', route)  11.8 us
    all_to_all x1, waiting for transfers between devices, local(): lax.all_to_all(terms, ('group', 'seq'), 0, 0, axis_index_groups=same_core...  10.6 us
    unnamed x20, local copies, waits for them, and re-layouts  10.3 us
    all_to_all x1, starting transfers between devices, local(): lax.all_to_all(terms, ('group', 'seq'), 0, 0, axis_index_groups=same_core...  9.86 us
    pallas_call x1, Pallas kernels, attend(): pl.pallas_call(functools.partial(attend_kernel, calls=calls, rows=rows, s...  9.65 us
    ppermute x6, starting transfers between devices, other_core(): return lax.ppermute(block, 'seq', [(i, i ^ 1) for i in range(seq_count)])  6.35 us
  transfers between devices with their start and end apart: 14, of which 6 were waited for; matrix products, arithmetic and copies ran while one was open for 1% of the time, Pallas kernels for 23%

profile of v1, /device:TPU:16, one launch (start us, length us, event | category | flops | bytes accessed | tf_op | source)
XLA Modules:
  0.0 142.8 jit_solution(17627842430139920786)
XLA Ops:
  0.7 1.1 copy-done.2
  1.8 1.1 copy-done.3
  2.9 1.1 copy-done.4
  4.0 1.1 copy-done.5
  7.7 2.3 %own_rows.1.refs_0_ = bf16[80,5120]{1,0:T(8,128)(2,1)S(1)} custom-call(s32[1]{0:T(128)S(6)} %copy.13.step_ref, bf16[80,5120]{1,0:T(8,128)(2,1)S(1)} %bitcast.23, f32[2,5120]{1,0:T(2,128)S(1)} %copy-done.7, bf16[64,5120]{1,0:T(8,128)(2,1)S(1)} %bitcast.25, bf16[64,80]{1,0:T(8,128)(2,1)S(1)} %bitcast.28, bf16[80,5120]{1,0:T(8,128)(2,1)S(1)} %bitcast.24, ...), custom_call_target="tpu_custom_call" | custom-call | flops 200000000 | bytes 5000000 | tf_op jit(solution)/shard_map/own_rows/pallas_call | solution.py:52
  10.0 2.0 %collective-permute-start.1 = (bf16[80,5120]{1,0:T(8,128)(2,1)S(1)}, bf16[80,5120]{1,0:T(8,128)(2,1)S(1)}, u32[]{:S(2)}, u32[]{:S(2)}) collective-permute-start(bf16[80,5120]{1,0:T(8,128)(2,1)S(1)} %own_rows.1.refs_0_), channel_id=1, source_target_pairs={{0,2},{1,15},{2,4},{3,1},{4,6},{5,3},{6,8},{7,5},{8,10},{9,7},{10,... | collective-permute-start | bytes 2457608 | tf_op jit(solution)/shard_map/ppermute | solution.py:227
  12.0 4.0 %collective-permute-start.2 = (bf16[80,5120]{1,0:T(8,128)(2,1)S(1)}, bf16[80,5120]{1,0:T(8,128)(2,1)}, u32[]{:S(2)}, u32[]{:S(2)}) collective-permute-start(bf16[80,5120]{1,0:T(8,128)(2,1)S(1)} %own_rows.1.refs_0_), channel_id=1, source_target_pairs={{0,14},{1,3},{2,0},{3,5},{4,2},{5,7},{6,4},{7,9},{8,6},{9,11},{10,... | collective-permute-start | bytes 2457608 | tf_op jit(solution)/shard_map/ppermute | solution.py:227
  16.0 16.4 %collective-permute-done.1.refs_1_ = bf16[80,5120]{1,0:T(8,128)(2,1)S(1)} collective-permute-done((bf16[80,5120]{1,0:T(8,128)(2,1)S(1)}, bf16[80,5120]{1,0:T(8,128)(2,1)S(1)}, u32[]{:S(2)}, u32[]{:S(2)}) %collective-permute-start.1) | collective-permute-done | bytes 819232 | tf_op jit(solution)/shard_map/ppermute | solution.py:227
  32.4 1.7 %collective-permute-done.2.refs_2_ = bf16[80,5120]{1,0:T(8,128)(2,1)} collective-permute-done((bf16[80,5120]{1,0:T(8,128)(2,1)S(1)}, bf16[80,5120]{1,0:T(8,128)(2,1)}, u32[]{:S(2)}, u32[]{:S(2)}) %collective-permute-start.2) | collective-permute-done | bytes 819232 | tf_op jit(solution)/shard_map/ppermute | solution.py:227
  34.1 3.8 %collective-permute-start.5 = (bf16[80,5120]{1,0:T(8,128)(2,1)}, bf16[80,5120]{1,0:T(8,128)(2,1)}, u32[]{:S(2)}, u32[]{:S(2)}) collective-permute-start(bf16[80,5120]{1,0:T(8,128)(2,1)} %collective-permute-done.2.refs_2_), channel_id=1, source_target_pairs={{0,14},{1,3},{2,0},{3,5},{4,2},{5,7},{6,4},{7,9},{8,6},{9,11},{10,... | collective-permute-start | bytes 2457608 | tf_op jit(solution)/shard_map/ppermute | solution.py:227
  37.9 14.9 %collective-permute-done.4.refs_0_ = bf16[80,5120]{1,0:T(8,128)(2,1)S(1)} collective-permute-done((bf16[80,5120]{1,0:T(8,128)(2,1)S(1)}, bf16[80,5120]{1,0:T(8,128)(2,1)S(1)}, u32[]{:S(2)}, u32[]{:S(2)}) %collective-permute-start.4) | collective-permute-done | bytes 819232 | tf_op jit(solution)/shard_map/ppermute | solution.py:227
  53.0 4.2 %collective-permute-start = (bf16[2,64,128]{2,1,0:T(8,128)(2,1)}, bf16[2,64,128]{2,1,0:T(8,128)(2,1)S(1)}, u32[]{:S(2)}, u32[]{:S(2)}) collective-permute-start(bf16[2,64,128]{2,1,0:T(8,128)(2,1)} %bitcast.29), channel_id=1, source_target_pairs={{0,1},{1,0},{2,3},{3,2},{4,5},{5,4},{6,7},{7,6},{8,9},{9,8},{10,11... | collective-permute-start | bytes 98312 | tf_op jit(solution)/shard_map/ppermute | solution.py:230
  57.2 1.8 %collective-permute-start.7 = (bf16[80,5120]{1,0:T(8,128)(2,1)}, bf16[80,5120]{1,0:T(8,128)(2,1)}, u32[]{:S(2)}, u32[]{:S(2)}) collective-permute-start(bf16[80,5120]{1,0:T(8,128)(2,1)} %collective-permute-done.5.refs_1_), channel_id=1, source_target_pairs={{0,14},{1,3},{2,0},{3,5},{4,2},{5,7},{6,4},{7,9},{8,6},{9,11},{10,... | collective-permute-start | bytes 2457608 | tf_op jit(solution)/shard_map/ppermute | solution.py:227
  60.6 14.5 %collective-permute-done.6.refs_0_ = bf16[80,5120]{1,0:T(8,128)(2,1)S(1)} collective-permute-done((bf16[80,5120]{1,0:T(8,128)(2,1)S(1)}, bf16[80,5120]{1,0:T(8,128)(2,1)S(1)}, u32[]{:S(2)}, u32[]{:S(2)}) %collective-permute-start.6) | collective-permute-done | bytes 819232 | tf_op jit(solution)/shard_map/ppermute | solution.py:227
  75.0 3.2 %copy-done = bf16[1,5120,3,256]{3,1,2,0:T(8,128)(2,1)S(1)} copy-done((bf16[1,5120,3,256]{3,1,2,0:T(8,128)(2,1)S(1)}, bf16[1,5120,3,256]{3,1,2,0:T(8,128)(2,1)}, u32[]{:S(2)}) %copy-start) | copy-done | bytes 7864344
  78.3 10.0 %project_rows.4 = (bf16[2,240,256]{2,1,0:T(8,128)(2,1)S(1)}, bf16[4,240,256]{2,1,0:T(8,128)(2,1)S(1)}) custom-call(bf16[80,5120]{1,0:T(8,128)(2,1)S(1)} %own_rows.1.refs_0_, bf16[80,5120]{1,0:T(8,128)(2,1)S(1)} %collective-permute-done.1.refs_1_, bf16[80,5120]{1,0:T(8,128)(2,1)} %collective-permute-done.2.refs_2_, bf16[3,5120,256]{2,1,0:T(8,128)(2,1)S(1)} %bitcast.19, ...), custom_call_target="tpu_custom_call" | custom-call | flops 3774873600 | bytes 18186240 | tf_op jit(solution)/shard_map/project_rows/pallas_call | solution.py:97
  88.3 1.1 collective-permute-start.9
  89.4 7.3 %project_rows.5 = (bf16[2,160,256]{2,1,0:T(8,128)(2,1)S(1)}, bf16[4,160,256]{2,1,0:T(8,128)(2,1)S(1)}) custom-call(bf16[80,5120]{1,0:T(8,128)(2,1)S(1)} %collective-permute-done.4.refs_0_, bf16[80,5120]{1,0:T(8,128)(2,1)} %collective-permute-done.5.refs_1_, bf16[3,5120,256]{2,1,0:T(8,128)(2,1)S(1)} %bitcast.20, ...), custom_call_target="tpu_custom_call" | custom-call | flops 2516582400 | bytes 17367040 | tf_op jit(solution)/shard_map/project_rows/pallas_call | solution.py:97
  97.0 7.3 %project_rows.6 = (bf16[2,160,256]{2,1,0:T(8,128)(2,1)S(1)}, bf16[4,160,256]{2,1,0:T(8,128)(2,1)S(1)}) custom-call(bf16[80,5120]{1,0:T(8,128)(2,1)S(1)} %collective-permute-done.6.refs_0_, bf16[80,5120]{1,0:T(8,128)(2,1)} %collective-permute-done.7.refs_1_, bf16[3,5120,256]{2,1,0:T(8,128)(2,1)S(1)} %bitcast.21, ...), custom_call_target="tpu_custom_call" | custom-call | flops 2516582400 | bytes 17367040 | tf_op jit(solution)/shard_map/project_rows/pallas_call | solution.py:97
  104.9 5.6 %project_rows.7 = (bf16[2,80,256]{2,1,0:T(8,128)(2,1)S(1)}, bf16[4,80,256]{2,1,0:T(8,128)(2,1)S(1)}) custom-call(bf16[80,5120]{1,0:T(8,128)(2,1)S(1)} %collective-permute-done.8.refs_0_, bf16[3,5120,256]{2,1,0:T(8,128)(2,1)S(1)} %bitcast.22, bf16[3,5120,256]{2,1,0:T(8,128)(2,1)} %collective-permute-done.3.refs_4_.refs_3_.refs_2_), custom_call_target="tpu_custom_call" | custom-call | flops 1258291200 | bytes 16547840 | tf_op jit(solution)/shard_map/project_rows/pallas_call | solution.py:97
  110.6 1.4 collective-permute-done.12.refs_11_
  112.0 9.7 %attend.1 = f32[2,8,32,80]{3,2,1,0:T(8,128)} custom-call(s32[8]{0:T(128)S(1)} %get-tuple-element.24.place_ref, f32[1,1280]{1,0:T(1,128)S(1)} %pad_maximum_fusion.bias_ref, bf16[2,64,128]{2,1,0:T(8,128)(2,1)S(1)} %bitcast.30, bf16[2,64,128]{2,1,0:T(8,128)(2,1)S(1)} %collective-permute-done.hb_ref, bf16[2,240,256]{2,1,0:T(8,128)(2,1)S(1)} %get-tuple-element.13.refs_0_, ...), custom_call_target="tpu_custom_call" | custom-call | flops 1677721600 | bytes 10000000 | tf_op jit(solution)/shard_map/attend/pallas_call | solution.py:173
  121.6 9.9 %all-to-all-start = ((f32[16,32,80]{2,1,0:T(8,128)}), f32[16,32,80]{2,1,0:T(8,128)S(1)}, u32[]{:S(2)}, u32[]{:S(2)}) async-start(f32[16,32,80]{2,1,0:T(8,128)} %bitcast.13), calls=%async_computation | async-start | bytes 524288 | tf_op jit(solution)/shard_map/all_to_all | solution.py:281
  131.5 10.6 %all-to-all-done = f32[16,32,80]{2,1,0:T(8,128)S(1)} async-done(((f32[16,32,80]{2,1,0:T(8,128)}), f32[16,32,80]{2,1,0:T(8,128)S(1)}, u32[]{:S(2)}, u32[]{:S(2)}) %all-to-all-start) | async-done | bytes 163872 | tf_op jit(solution)/shard_map/all_to_all | solution.py:281
  (38 shorter events, 5.4 us)
Async XLA Ops:
  0.0 75.0 %collective-permute-start.3 = (bf16[3,5120,256]{2,1,0:T(8,128)(2,1)}, bf16[3,5120,256]{2,1,0:T(8,128)(2,1)}, u32[]{:S(2)}, u32[]{:S(2)}) collective-permute-start(bf16[3,5120,256]{2,1,0:T(8,128)(2,1)} %bitcast.18), channel_id=1, source_target_pairs={{0,1},{1,0},{2,3},{3,2},{4,5},{5,4},{6,7},{7,6},{8,9},{9,8},{10,11... | collective-permute-start | bytes 23592968 | tf_op jit(solution)/shard_map/ppermute | solution.py:230
  0.7 1.1 copy-start.2
  1.8 1.1 copy-start.3
  2.9 1.1 copy-start.4
  4.0 1.1 copy-start.5
  5.1 1.1 copy-start.6
  6.2 0.8 copy-start.7
  7.0 0.7 copy-start.8
  10.0 22.5 %collective-permute-start.1 = (bf16[80,5120]{1,0:T(8,128)(2,1)S(1)}, bf16[80,5120]{1,0:T(8,128)(2,1)S(1)}, u32[]{:S(2)}, u32[]{:S(2)}) collective-permute-start(bf16[80,5120]{1,0:T(8,128)(2,1)S(1)} %own_rows.1.refs_0_), channel_id=1, source_target_pairs={{0,2},{1,15},{2,4},{3,1},{4,6},{5,3},{6,8},{7,5},{8,10},{9,7},{10,... | collective-permute-start | bytes 2457608 | tf_op jit(solution)/shard_map/ppermute | solution.py:227
  12.0 22.1 %collective-permute-start.2 = (bf16[80,5120]{1,0:T(8,128)(2,1)S(1)}, bf16[80,5120]{1,0:T(8,128)(2,1)}, u32[]{:S(2)}, u32[]{:S(2)}) collective-permute-start(bf16[80,5120]{1,0:T(8,128)(2,1)S(1)} %own_rows.1.refs_0_), channel_id=1, source_target_pairs={{0,14},{1,3},{2,0},{3,5},{4,2},{5,7},{6,4},{7,9},{8,6},{9,11},{10,... | collective-permute-start | bytes 2457608 | tf_op jit(solution)/shard_map/ppermute | solution.py:227
  32.4 20.4 %collective-permute-start.4 = (bf16[80,5120]{1,0:T(8,128)(2,1)S(1)}, bf16[80,5120]{1,0:T(8,128)(2,1)S(1)}, u32[]{:S(2)}, u32[]{:S(2)}) collective-permute-start(bf16[80,5120]{1,0:T(8,128)(2,1)S(1)} %collective-permute-done.1.refs_1_), channel_id=1, source_target_pairs={{0,2},{1,15},{2,4},{3,1},{4,6},{5,3},{6,8},{7,5},{8,10},{9,7},{10,... | collective-permute-start | bytes 2457608 | tf_op jit(solution)/shard_map/ppermute | solution.py:227
  34.1 23.1 %collective-permute-start.5 = (bf16[80,5120]{1,0:T(8,128)(2,1)}, bf16[80,5120]{1,0:T(8,128)(2,1)}, u32[]{:S(2)}, u32[]{:S(2)}) collective-permute-start(bf16[80,5120]{1,0:T(8,128)(2,1)} %collective-permute-done.2.refs_2_), channel_id=1, source_target_pairs={{0,14},{1,3},{2,0},{3,5},{4,2},{5,7},{6,4},{7,9},{8,6},{9,11},{10,... | collective-permute-start | bytes 2457608 | tf_op jit(solution)/shard_map/ppermute | solution.py:227
  52.8 22.2 %collective-permute-start.6 = (bf16[80,5120]{1,0:T(8,128)(2,1)S(1)}, bf16[80,5120]{1,0:T(8,128)(2,1)S(1)}, u32[]{:S(2)}, u32[]{:S(2)}) collective-permute-start(bf16[80,5120]{1,0:T(8,128)(2,1)S(1)} %collective-permute-done.4.refs_0_), channel_id=1, source_target_pairs={{0,2},{1,15},{2,4},{3,1},{4,6},{5,3},{6,8},{7,5},{8,10},{9,7},{10,... | collective-permute-start | bytes 2457608 | tf_op jit(solution)/shard_map/ppermute | solution.py:227
  53.0 57.6 %collective-permute-start = (bf16[2,64,128]{2,1,0:T(8,128)(2,1)}, bf16[2,64,128]{2,1,0:T(8,128)(2,1)S(1)}, u32[]{:S(2)}, u32[]{:S(2)}) collective-permute-start(bf16[2,64,128]{2,1,0:T(8,128)(2,1)} %bitcast.29), channel_id=1, source_target_pairs={{0,1},{1,0},{2,3},{3,2},{4,5},{5,4},{6,7},{7,6},{8,9},{9,8},{10,11... | collective-permute-start | bytes 98312 | tf_op jit(solution)/shard_map/ppermute | solution.py:230
  57.2 39.8 %collective-permute-start.7 = (bf16[80,5120]{1,0:T(8,128)(2,1)}, bf16[80,5120]{1,0:T(8,128)(2,1)}, u32[]{:S(2)}, u32[]{:S(2)}) collective-permute-start(bf16[80,5120]{1,0:T(8,128)(2,1)} %collective-permute-done.5.refs_1_), channel_id=1, source_target_pairs={{0,14},{1,3},{2,0},{3,5},{4,2},{5,7},{6,4},{7,9},{8,6},{9,11},{10,... | collective-permute-start | bytes 2457608 | tf_op jit(solution)/shard_map/ppermute | solution.py:227
  75.0 29.9 %collective-permute-start.8 = (bf16[80,5120]{1,0:T(8,128)(2,1)S(1)}, bf16[80,5120]{1,0:T(8,128)(2,1)S(1)}, u32[]{:S(2)}, u32[]{:S(2)}) collective-permute-start(bf16[80,5120]{1,0:T(8,128)(2,1)S(1)} %collective-permute-done.6.refs_0_), channel_id=1, source_target_pairs={{0,2},{1,15},{2,4},{3,1},{4,6},{5,3},{6,8},{7,5},{8,10},{9,7},{10,... | collective-permute-start | bytes 2457608 | tf_op jit(solution)/shard_map/ppermute | solution.py:227
  75.0 3.2 %copy-start = (bf16[1,5120,3,256]{3,1,2,0:T(8,128)(2,1)S(1)}, bf16[1,5120,3,256]{3,1,2,0:T(8,128)(2,1)}, u32[]{:S(2)}) copy-start(bf16[1,5120,3,256]{3,1,2,0:T(8,128)(2,1)} %param.18) | copy-start | bytes 23592964
  78.3 11.2 %copy-start.1 = (bf16[1,5120,3,256]{3,1,2,0:T(8,128)(2,1)S(1)}, bf16[1,5120,3,256]{3,1,2,0:T(8,128)(2,1)}, u32[]{:S(2)}) copy-start(bf16[1,5120,3,256]{3,1,2,0:T(8,128)(2,1)} %param.18) | copy-start | bytes 23592964
  88.3 23.7 %collective-permute-start.9 = (bf16[4,240,256]{2,1,0:T(8,128)(2,1)S(1)}, bf16[4,240,256]{2,1,0:T(8,128)(2,1)S(1)}, u32[]{:S(2)}, u32[]{:S(2)}) collective-permute-start(bf16[4,240,256]{2,1,0:T(8,128)(2,1)S(1)} %get-tuple-element.17.refs_4_), channel_id=1, source_target_pairs={{0,1},{1,0},{2,3},{3,2},{4,5},{5,4},{6,7},{7,6},{8,9},{9,8},{10,11... | collective-permute-start | bytes 1474568 | tf_op jit(solution)/shard_map/ppermute | solution.py:230
  96.7 15.3 %collective-permute-start.10 = (bf16[4,160,256]{2,1,0:T(8,128)(2,1)S(1)}, bf16[4,160,256]{2,1,0:T(8,128)(2,1)S(1)}, u32[]{:S(2)}, u32[]{:S(2)}) collective-permute-start(bf16[4,160,256]{2,1,0:T(8,128)(2,1)S(1)} %get-tuple-element.18.refs_5_), channel_id=1, source_target_pairs={{0,1},{1,0},{2,3},{3,2},{4,5},{5,4},{6,7},{7,6},{8,9},{9,8},{10,11... | collective-permute-start | bytes 983048 | tf_op jit(solution)/shard_map/ppermute | solution.py:230
  104.3 7.7 %copy-start.9 = (bf16[1,2,128,64]{2,3,1,0:T(8,128)(2,1)S(1)}, bf16[1,2,128,64]{2,3,1,0:T(8,128)(2,1)}, u32[]{:S(2)}) copy-start(bf16[1,2,128,64]{2,3,1,0:T(8,128)(2,1)} %param.19) | copy-start | bytes 98308
  104.3 7.7 %collective-permute-start.11 = (bf16[4,160,256]{2,1,0:T(8,128)(2,1)S(1)}, bf16[4,160,256]{2,1,0:T(8,128)(2,1)S(1)}, u32[]{:S(2)}, u32[]{:S(2)}) collective-permute-start(bf16[4,160,256]{2,1,0:T(8,128)(2,1)S(1)} %get-tuple-element.19.refs_6_), channel_id=1, source_target_pairs={{0,1},{1,0},{2,3},{3,2},{4,5},{5,4},{6,7},{7,6},{8,9},{9,8},{10,11... | collective-permute-start | bytes 983048 | tf_op jit(solution)/shard_map/ppermute | solution.py:230
  110.5 1.5 %collective-permute-start.12 = (bf16[4,80,256]{2,1,0:T(8,128)(2,1)S(1)}, bf16[4,80,256]{2,1,0:T(8,128)(2,1)S(1)}, u32[]{:S(2)}, u32[]{:S(2)}) collective-permute-start(bf16[4,80,256]{2,1,0:T(8,128)(2,1)S(1)} %get-tuple-element.20.refs_7_), channel_id=1, source_target_pairs={{0,1},{1,0},{2,3},{3,2},{4,5},{5,4},{6,7},{7,6},{8,9},{9,8},{10,11... | collective-permute-start | bytes 491528 | tf_op jit(solution)/shard_map/ppermute | solution.py:230
  121.6 20.5 %all-to-all-start = ((f32[16,32,80]{2,1,0:T(8,128)}), f32[16,32,80]{2,1,0:T(8,128)S(1)}, u32[]{:S(2)}, u32[]{:S(2)}) async-start(f32[16,32,80]{2,1,0:T(8,128)} %bitcast.13), calls=%async_computation | async-start | bytes 524288 | tf_op jit(solution)/shard_map/all_to_all | solution.py:281

commit v2 on v1

v2 whole, which is shorter than its diff:
```python
import functools

import jax
import jax.numpy as jnp
from jax import lax
from jax.experimental import pallas as pl
from jax.experimental.pallas import tpu as pltpu
from jax.sharding import PartitionSpec as P

epsilon = 1e-06
LOG2E = 1.4426950408889634
MIB = 1 << 20
NT = (((1,), (1,)), ((), ()))
TN = (((0,), (0,)), ((), ()))
NN = (((1,), (0,)), ((), ()))


def dot(a, b, dims):
    return lax.dot_general(a, b, dims, preferred_element_type=jnp.float32)


def layer_norm(values):
    average = jnp.mean(values, -1, keepdims=True)
    centered = values - average
    variance = jnp.mean(centered * centered, -1, keepdims=True)
    return centered * lax.rsqrt(variance + epsilon)


def own_rows_kernel(
    step_ref, hidden_any, mod_any, out_any, noise_any, stream_any, embed_any, table_any, *refs, levels, cuts
):
    normed_refs = refs[: len(cuts)]
    hidden_ref, mod_ref, out_ref, noise_ref, stream_ref, embed_ref, table_ref, sems = refs[len(cuts) :]
    pairs = [
        (hidden_any, hidden_ref),
        (mod_any, mod_ref),
        (out_any, out_ref),
        (noise_any, noise_ref),
        (stream_any, stream_ref),
        (embed_any, embed_ref),
        (table_any.at[step_ref[0]], table_ref),
    ]
    copies = [pltpu.make_async_copy(a, b, sems.at[i]) for i, (a, b) in enumerate(pairs)]
    for copy in copies:
        copy.start()
    copies[0].wait()
    copies[1].wait()
    mod = mod_ref[...]
    student = (
        layer_norm(hidden_ref[...].astype(jnp.float32)) * (1.0 + mod[1:2]) + mod[0:1]
    ).astype(jnp.bfloat16)
    copies[2].wait()
    latent = dot(out_ref[...], student, NT)
    step = jnp.full(latent.shape, step_ref[0], jnp.int32).astype(jnp.float32)
    level = (step + 1.0) / (levels + 1.0)
    copies[3].wait()
    noised = ((1.0 - level) * latent + level * noise_ref[...].astype(jnp.float32)).astype(jnp.bfloat16)
    for copy in copies[4:]:
        copy.wait()
    embedded = stream_ref[...].astype(jnp.float32) + dot(noised, embed_ref[...], TN)
    table = table_ref[...]
    normed = (layer_norm(embedded) * (1.0 + table[1:2]) + table[0:1]).astype(jnp.bfloat16)
    at = 0
    for ref, size in zip(normed_refs, cuts):
        ref[...] = normed[at : at + size]
        at += size


def own_rows(step, hidden, mod, out_t, noise, stream, embed, table, cuts):
    width = hidden.shape[1]
    levels = table.shape[0]
    arrays = (hidden, mod, out_t, noise, stream, embed)
    return pl.pallas_call(
        functools.partial(own_rows_kernel, levels=levels, cuts=cuts),
        in_specs=[pl.BlockSpec(memory_space=pltpu.SMEM)] + [pl.BlockSpec(memory_space=pl.ANY)] * 7,
        out_specs=[pl.BlockSpec(memory_space=pltpu.VMEM)] * len(cuts),
        out_shape=[jax.ShapeDtypeStruct((size, width), jnp.bfloat16) for size in cuts],
        scratch_shapes=[pltpu.VMEM(x.shape, x.dtype) for x in arrays]
        + [pltpu.VMEM((2, width), jnp.float32), pltpu.SemaphoreType.DMA((7,))],
        compiler_params=pltpu.CompilerParams(vmem_limit_bytes=58 * MIB),
        cost_estimate=pl.CostEstimate(flops=2 * 10**8, bytes_accessed=5 * 10**6, transcendentals=0),
        name="own_rows",
    )(step, hidden, mod, out_t, noise, stream, embed, table)


def project_kernel(*refs, sizes, fetch, keep, before):
    refs = list(refs)
    x_refs = [refs.pop(0) for _ in sizes]
    w_any = [refs.pop(0) for _ in range(2 if fetch else 1)]
    q_before, kv_before = (refs.pop(0), refs.pop(0)) if before else (None, None)
    q_ref, kv_ref = refs.pop(0), refs.pop(0)
    w_ref = refs.pop(0) if fetch else w_any[0]
    x_buf = refs.pop(0)
    copies = []
    if fetch:
        sems = refs.pop(0)
        copies = [
            pltpu.make_async_copy(w_any[n // 3].at[n % 3], w_ref.at[n], sems.at[n]) for n in range(6)
        ]
        for copy in copies[:3]:
            copy.start()
    at = 0
    for ref, size in zip(x_refs, sizes):
        x_buf[pl.ds(at, size)] = ref[...]
        at += size
    size = q_ref.shape[2]
    if before:
        q_ref[:, pl.ds(0, before)] = q_before[...]
        kv_ref[:, pl.ds(0, before)] = kv_before[...]
    here = pl.ds(before, sum(sizes))
    for n in range(6):
        if fetch:
            copies[n].wait()
            if n + 3 < 6:
                copies[n + 3].start()
        value = dot(x_buf[...], w_ref[n], NN).astype(jnp.bfloat16)
        pair, kind = n // 3, n % 3
        for sub in range(2):
            part = value[:, sub * size : (sub + 1) * size]
            if kind == 0:
                q_ref[2 * pair + sub, here] = part
            else:
                kv_ref[4 * pair + 2 * (kind - 1) + sub, here] = part


def project(xs, weights, head_size, keep=False, earlier=()):
    fetch = len(weights) == 2
    sizes = tuple(x.shape[0] for x in xs)
    width = xs[0].shape[1]
    columns = weights[0].shape[2]
    total = sum(sizes)
    before = earlier[0].shape[1] if earlier else 0
    vmem = pl.BlockSpec(memory_space=pltpu.VMEM)
    out_shape = [
        jax.ShapeDtypeStruct((4, before + total, head_size), jnp.bfloat16),
        jax.ShapeDtypeStruct((8, before + total, head_size), jnp.bfloat16),
    ]
    scratch = [pltpu.VMEM((total, width), jnp.bfloat16)]
    if keep:
        out_shape.append(jax.ShapeDtypeStruct((6, width, columns), jnp.bfloat16))
    elif fetch:
        scratch.insert(0, pltpu.VMEM((6, width, columns), jnp.bfloat16))
    if fetch:
        scratch.append(pltpu.SemaphoreType.DMA((6,)))
    return pl.pallas_call(
        functools.partial(project_kernel, sizes=sizes, fetch=fetch, keep=keep, before=before),
        in_specs=[vmem] * len(xs)
        + [pl.BlockSpec(memory_space=pl.ANY) if fetch else vmem] * len(weights)
        + [vmem] * len(earlier),
        out_specs=[vmem] * len(out_shape),
        out_shape=out_shape,
        scratch_shapes=scratch,
        compiler_params=pltpu.CompilerParams(vmem_limit_bytes=(10 if keep or not fetch else 40) * MIB),
        cost_estimate=pl.CostEstimate(
            flops=2 * total * width * 6 * columns,
            bytes_accessed=12 * width * columns if fetch else 2 * total * width,
            transcendentals=0,
        ),
        name="project_rows",
    )(*xs, *weights, *earlier)


def attend_kernel(place_ref, bias_ref, ha_ref, hb_ref, *refs, calls, rows, sizes, scale):
    q_refs = refs[:calls]
    own_refs = refs[calls : 2 * calls]
    far_refs = refs[2 * calls : 3 * calls]
    out_ref, q_buf, kv_buf, mix, heads, sems = refs[3 * calls :]
    own = sum(sizes)
    size = q_buf.shape[2]
    pairs = []
    at = 0
    for i, count in enumerate(sizes):
        here, there = pl.ds(at, count), pl.ds(own + at, count)
        pairs += [
            (q_refs[i], q_buf.at[:, here]),
            (own_refs[i].at[pl.ds(0, 8)], kv_buf.at[:, here]),
            (far_refs[i].at[pl.ds(4, 4)], kv_buf.at[pl.ds(0, 4), there]),
            (far_refs[i].at[pl.ds(0, 4)], kv_buf.at[pl.ds(4, 4), there]),
        ]
        at += count
    copies = [pltpu.make_async_copy(a, b, sems.at[j]) for j, (a, b) in enumerate(pairs)]
    for copy in copies:
        copy.start()
    for copy in copies:
        copy.wait()
    bias = bias_ref[...]
    for n in range(4):
        key = 4 * (n // 2) + n % 2
        scores = dot(q_buf[n], kv_buf[key], NT) * scale + bias
        highest = jnp.max(scores, -1, keepdims=True)
        lifted = jnp.exp2(scores - highest)
        total = jnp.sum(lifted, -1, keepdims=True)
        mixed = dot(lifted.astype(jnp.bfloat16), kv_buf[key + 2], NN) * (1.0 / total)
        mix[:, pl.ds(n * size, size)] = mixed.astype(jnp.bfloat16)
    for n in range(4):
        heads[:, pl.ds(n * size, size)] = (ha_ref if n < 2 else hb_ref)[n % 2]
    half = out_ref.shape[2]
    for j in range(own // rows):
        result = dot(heads[...], mix[pl.ds(j * rows, rows)], NT)
        out_ref[0, place_ref[j]] = result[:half]
        out_ref[1, place_ref[j]] = result[half:]


def attend(place, bias, ha, hb, qs, owns, fars, rows, groups, scale):
    calls = len(qs)
    sizes = tuple(q.shape[1] for q in qs)
    own = sum(sizes)
    head_size = qs[0].shape[2]
    patch = ha.shape[1]
    vmem = pl.BlockSpec(memory_space=pltpu.VMEM)
    return pl.pallas_call(
        functools.partial(attend_kernel, calls=calls, rows=rows, sizes=sizes, scale=scale),
        in_specs=[pl.BlockSpec(memory_space=pltpu.SMEM), vmem, vmem, vmem]
        + [pl.BlockSpec(memory_space=pl.ANY)] * (3 * calls),
        out_specs=vmem,
        out_shape=jax.ShapeDtypeStruct((groups, own // rows, patch // groups, rows), jnp.float32),
        scratch_shapes=[
            pltpu.VMEM((4, own, head_size), jnp.bfloat16),
            pltpu.VMEM((8, 2 * own, head_size), jnp.bfloat16),
            pltpu.VMEM((own, 4 * head_size), jnp.bfloat16),
            pltpu.VMEM((patch, 4 * head_size), jnp.bfloat16),
            pltpu.SemaphoreType.DMA((4 * calls,)),
        ],
        compiler_params=pltpu.CompilerParams(vmem_limit_bytes=58 * MIB),
        cost_estimate=pl.CostEstimate(
            flops=32 * own * own * head_size, bytes_accessed=10**7, transcendentals=8 * own * own
        ),
        name="attend",
    )(place, bias, ha, hb, *qs, *owns, *fars)


def local(
    student_hidden,
    student_mod,
    student_out,
    score_stream,
    score_in,
    score_mod,
    attention_in,
    head_out,
    step_index,
    lengths,
    noise,
):
    groups = lax.axis_size("group")
    seq_count = lax.axis_size("seq")
    chips = seq_count // 2
    seq_at = lax.axis_index("seq")
    chip_at, core_at = seq_at // 2, seq_at % 2
    rows = student_hidden.shape[1]
    head_size = head_out.shape[2]
    scale = head_size ** (-0.5) * LOG2E
    length = lengths[0]

    def hop(block, sign):
        route = []
        for z in range(chips):
            for core in range(2):
                way = sign if core == 0 else -sign
                route.append((2 * z + core, 2 * ((z + way) % chips) + core))
        return lax.ppermute(block, "seq", route)

    def other_core(block):
        return lax.ppermute(block, "seq", [(i, i ^ 1) for i in range(seq_count)])

    half_way = chips // 2
    apart = [0, -1]
    for k in range(1, half_way):
        apart += [k, -k - 1]
    apart = jnp.asarray(apart, jnp.int32)

    def places(core):
        return (chip_at + jnp.where(core == 0, apart, -apart)) % chips

    def bias_of(core):
        tokens = (places(core) * 2 + core)[:, None] * rows + jnp.arange(rows, dtype=jnp.int32)
        return jnp.where(tokens < length, 0.0, -1e30)

    normed, *_ = own_rows(
        step_index,
        student_hidden[0],
        student_mod,
        student_out.T,
        noise[0],
        score_stream[0, 0],
        score_in[0],
        score_mod[0],
        (rows,),
    )
    wa = attention_in[0].transpose(1, 0, 2)
    ha = head_out[0].transpose(0, 2, 1)

    up, down = [normed], [normed]
    up.append(hop(up[-1], 1))
    begun, _ = lax.optimization_barrier((ha, normed))
    hb = other_core(begun)
    later, fetched, hb = lax.optimization_barrier((normed, wa, hb))
    down.append(hop(later, -1))
    wb = other_core(fetched)
    bias = jnp.concatenate([bias_of(core_at), bias_of(1 - core_at)]).reshape(1, -1)
    up.append(hop(up[-1], 1))

    place = places(core_at)
    qs, owns, fars = [], [], []
    weights, earlier = [wa, wb], ()
    for k in range(half_way):
        nearer, further = down[k], up[k + 1]
        if k + 1 < half_way:
            nearer, down[k + 1] = lax.optimization_barrier((nearer, down[k + 1]))
        if k + 2 < half_way:
            down.append(hop(down[k + 1], -1))
        q, kv, *kept = project(
            [nearer, further], weights, head_size, keep=k == half_way - 2, earlier=earlier
        )
        weights = kept or weights
        if k + 2 <= half_way:
            up[k + 2], q, kv, fars, bias, place = lax.optimization_barrier((up[k + 2], q, kv, fars, bias, place))
        if k + 3 <= half_way:
            up.append(hop(up[k + 2], 1))
        if k == half_way - 2:
            earlier = (q, kv)
        else:
            qs.append(q)
            owns.append(kv)
            fars.append(other_core(kv))
    terms = attend(place, bias, ha, hb, qs, owns, fars, rows, groups, scale)

    half = terms.shape[2]
    terms = terms.reshape(groups * chips, half, rows)
    same_core = [[g * seq_count + 2 * z + c for g in range(groups) for z in range(chips)] for c in range(2)]
    terms = lax.all_to_all(terms, ("group", "seq"), 0, 0, axis_index_groups=same_core, tiled=True)
    terms = terms.reshape(groups, chips, half, rows)
    gradient = jnp.sum(terms[0], 0) - jnp.sum(terms[1], 0)
    own_places = seq_at * rows + jnp.arange(rows, dtype=jnp.int32)
    return jnp.where((own_places < length)[None, :], gradient, 0.0)[None]


def solution(mesh):
    return jax.shard_map(
        local,
        mesh=mesh,
        in_specs=(
            P("dp", "seq", None),
            P(),
            P(),
            P("group", "dp", "seq", None),
            P("group", None, None),
            P("group", None, None, None),
            P("group", None, None, "seq"),
            P("group", "seq", None, None),
            P("dp"),
            P("dp"),
            P("dp", None, "seq"),
        ),
        out_specs=P("dp", "group", "seq"),
        check_vma=False,
    )
```

time: 143 us -> 122 us (0.85)
  waiting for transfers between devices: 59.4 us -> 46.1 us
  Pallas kernels: 42.1 us -> 36.4 us
  local copies, waits for them, and re-layouts: 10.4 us -> 8 us
    ppermute x7, waiting for transfers between devices: 47.5 us -> 32.2 us  [hop(): return lax.ppermute(block, 'seq', route)]
    pallas_call x5, Pallas kernels: 32.4 us -> 27.5 us  [the longest x4 22.6 us: project(): pl.pallas_call(functools.partial(project_kernel, sizes=sizes, fetch=fetch...]
    unnamed x20 -> x28, local copies, waits for them, and re-layouts: 10.3 us -> 7.32 us
    ppermute x6 -> x5, starting transfers between devices: 6.35 us -> 3.84 us  [other_core(): return lax.ppermute(block, 'seq', [(i, i ^ 1) for i in range(seq_count)])]
    ppermute x6 -> x5, waiting for transfers between devices: 1.37 us -> 3.51 us  [other_core(): return lax.ppermute(block, 'seq', [(i, i ^ 1) for i in range(seq_count)])]
    ppermute x7, starting transfers between devices: 11.8 us -> 13.8 us  [hop(): return lax.ppermute(block, 'seq', route)]
  transfers between devices with their start and end apart: 14 -> 13, of which waited for: 6 -> 7; matrix products, arithmetic and copies ran while one was open for 1% -> 2% of each run, Pallas kernels for 23% -> 16%
where the time goes in v2:
time: 122 us
  waiting for transfers between devices  46.1 us (38%)
  Pallas kernels  36.4 us (30%)
  starting transfers between devices  28 us (23%)
  local copies, waits for them, and re-layouts  8 us (7%)
  other arithmetic  1.93 us (2%)
  between operations  1.5 us (1%)
    ppermute x7, waiting for transfers between devices, hop(): return lax.ppermute(block, 'seq', route)  32.2 us
    pallas_call x4, Pallas kernels, project(): pl.pallas_call(functools.partial(project_kernel, sizes=sizes, fetch=fetch...  22.6 us
    ppermute x7, starting transfers between devices, hop(): return lax.ppermute(block, 'seq', route)  13.8 us
    all_to_all x1, waiting for transfers between devices, local(): lax.all_to_all(terms, ('group', 'seq'), 0, 0, axis_index_groups=same_core...  10.4 us
    all_to_all x1, starting transfers between devices, local(): lax.all_to_all(terms, ('group', 'seq'), 0, 0, axis_index_groups=same_core...  10.3 us
    pallas_call x1, Pallas kernels, attend(): pl.pallas_call(functools.partial(attend_kernel, calls=calls, rows=rows, s...  8.98 us
    unnamed x28, local copies, waits for them, and re-layouts  7.32 us
    pallas_call x1, Pallas kernels, own_rows(): pl.pallas_call(functools.partial(own_rows_kernel, levels=levels, cuts=cut...  4.86 us
  transfers between devices with their start and end apart: 13, of which 7 were waited for; matrix products, arithmetic and copies ran while one was open for 2% of the time, Pallas kernels for 16%

profile of v2, /device:TPU:16, one launch (start us, length us, event | category | flops | bytes accessed | tf_op | source)
XLA Modules:
  0.0 122.0 jit_solution(14920928119953970126)
XLA Ops:
  0.7 4.9 %own_rows.1.refs_0_ = bf16[80,5120]{1,0:T(8,128)(2,1)} custom-call(s32[1]{0:T(128)S(6)} %copy.13.step_ref, bf16[80,5120]{1,0:T(8,128)(2,1)} %bitcast.24, f32[2,5120]{1,0:T(2,128)} %mod_any.1, bf16[64,5120]{1,0:T(8,128)(2,1)} %bitcast.26, bf16[64,80]{1,0:T(8,128)(2,1)} %bitcast.30, bf16[80,5120]{1,0:T(8,128)(2,1)} %bitcast.25, bf16[64,5120]{1,0:T(8,128)(2,1)} %bitcast.27, ...), custom_call_target="tpu_custom_call" | custom-call | flops 200000000 | bytes 5000000 | tf_op jit(solution)/shard_map/own_rows/pallas_call | solution.py:73
  5.6 1.4 %collective-permute-done.2.hb_ref = bf16[2,64,128]{2,1,0:T(8,128)(2,1)S(1)} collective-permute-done((bf16[2,64,128]{2,1,0:T(8,128)(2,1)}, bf16[2,64,128]{2,1,0:T(8,128)(2,1)S(1)}, u32[]{:S(2)}, u32[]{:S(2)}) %collective-permute-start.2) | collective-permute-done | bytes 32800 | tf_op jit(solution)/shard_map/ppermute | solution.py:264
  7.2 1.9 %collective-permute-start = (bf16[80,5120]{1,0:T(8,128)(2,1)}, bf16[80,5120]{1,0:T(8,128)(2,1)S(1)}, u32[]{:S(2)}, u32[]{:S(2)}) collective-permute-start(bf16[80,5120]{1,0:T(8,128)(2,1)} %own_rows.1.refs_0_), channel_id=1, source_target_pairs={{0,2},{1,15},{2,4},{3,1},{4,6},{5,3},{6,8},{7,5},{8,10},{9,7},{10,... | collective-permute-start | bytes 2457608 | tf_op jit(solution)/shard_map/ppermute | solution.py:261
  9.1 3.9 %collective-permute-start.3 = (bf16[80,5120]{1,0:T(8,128)(2,1)}, bf16[80,5120]{1,0:T(8,128)(2,1)S(1)}, u32[]{:S(2)}, u32[]{:S(2)}) collective-permute-start(bf16[80,5120]{1,0:T(8,128)(2,1)} %own_rows.1.refs_0_), channel_id=1, source_target_pairs={{0,14},{1,3},{2,0},{3,5},{4,2},{5,7},{6,4},{7,9},{8,6},{9,11},{10,... | collective-permute-start | bytes 2457608 | tf_op jit(solution)/shard_map/ppermute | solution.py:261
  13.0 16.9 %collective-permute-done.refs_1_ = bf16[80,5120]{1,0:T(8,128)(2,1)S(1)} collective-permute-done((bf16[80,5120]{1,0:T(8,128)(2,1)}, bf16[80,5120]{1,0:T(8,128)(2,1)S(1)}, u32[]{:S(2)}, u32[]{:S(2)}) %collective-permute-start) | collective-permute-done | bytes 819232 | tf_op jit(solution)/shard_map/ppermute | solution.py:261
  30.6 1.2 add_multiply_fusion
  31.9 0.7 reshape.56.bias_ref
  32.6 4.3 %collective-permute-start.6 = (bf16[80,5120]{1,0:T(8,128)(2,1)S(1)}, bf16[80,5120]{1,0:T(8,128)(2,1)S(1)}, u32[]{:S(2)}, u32[]{:S(2)}) collective-permute-start(bf16[80,5120]{1,0:T(8,128)(2,1)S(1)} %collective-permute-done.3.refs_0_), channel_id=1, source_target_pairs={{0,14},{1,3},{2,0},{3,5},{4,2},{5,7},{6,4},{7,9},{8,6},{9,11},{10,... | collective-permute-start | bytes 2457608 | tf_op jit(solution)/shard_map/ppermute | solution.py:261
  36.9 3.2 %copy-done = bf16[1,5120,3,256]{3,1,2,0:T(8,128)(2,1)S(1)} copy-done((bf16[1,5120,3,256]{3,1,2,0:T(8,128)(2,1)S(1)}, bf16[1,5120,3,256]{3,1,2,0:T(8,128)(2,1)}, u32[]{:S(2)}) %copy-start) | copy-done | bytes 7864344
  40.1 1.1 copy-done.1
  41.3 6.6 %project_rows.4 = (bf16[4,160,128]{2,1,0:T(8,128)(2,1)S(1)}, bf16[8,160,128]{2,1,0:T(8,128)(2,1)S(1)}) custom-call(bf16[80,5120]{1,0:T(8,128)(2,1)S(1)} %copy-done.1, bf16[80,5120]{1,0:T(8,128)(2,1)S(1)} %collective-permute-done.refs_1_, bf16[3,5120,256]{2,1,0:T(8,128)(2,1)S(1)} %bitcast.19, bf16[3,5120,256]{2,1,0:T(8,128)(2,1)} %collective-permute-done.4.refs_3_), custom_call_target="tpu_custom_call" | custom-call | flops 2516582400 | bytes 15728640 | tf_op jit(solution)/shard_map/project_rows/pallas_call | solution.py:145
  48.7 3.6 %collective-permute-start.7 = (bf16[8,160,128]{2,1,0:T(8,128)(2,1)S(1)}, bf16[8,160,128]{2,1,0:T(8,128)(2,1)S(1)}, u32[]{:S(2)}, u32[]{:S(2)}) collective-permute-start(bf16[8,160,128]{2,1,0:T(8,128)(2,1)S(1)} %get-tuple-element.53.refs_3_), channel_id=1, source_target_pairs={{0,1},{1,0},{2,3},{3,2},{4,5},{5,4},{6,7},{7,6},{8,9},{9,8},{10,11... | collective-permute-start | bytes 983048 | tf_op jit(solution)/shard_map/ppermute | solution.py:264
  52.3 3.6 %collective-permute-start.9 = (bf16[80,5120]{1,0:T(8,128)(2,1)S(1)}, bf16[80,5120]{1,0:T(8,128)(2,1)S(1)}, u32[]{:S(2)}, u32[]{:S(2)}) collective-permute-start(bf16[80,5120]{1,0:T(8,128)(2,1)S(1)} %collective-permute-done.6.refs_0_), channel_id=1, source_target_pairs={{0,14},{1,3},{2,0},{3,5},{4,2},{5,7},{6,4},{7,9},{8,6},{9,11},{10,... | collective-permute-start | bytes 2457608 | tf_op jit(solution)/shard_map/ppermute | solution.py:261
  55.9 6.6 %project_rows.5 = (bf16[4,160,128]{2,1,0:T(8,128)(2,1)S(1)}, bf16[8,160,128]{2,1,0:T(8,128)(2,1)S(1)}) custom-call(bf16[80,5120]{1,0:T(8,128)(2,1)S(1)} %collective-permute-done.3.refs_0_, bf16[80,5120]{1,0:T(8,128)(2,1)S(1)} %collective-permute-done.1.refs_1_, bf16[3,5120,256]{2,1,0:T(8,128)(2,1)S(1)} %bitcast.20, ...), custom_call_target="tpu_custom_call" | custom-call | flops 2516582400 | bytes 15728640 | tf_op jit(solution)/shard_map/project_rows/pallas_call | solution.py:145
  63.2 7.2 %collective-permute-done.5.refs_1_ = bf16[80,5120]{1,0:T(8,128)(2,1)S(1)} collective-permute-done((bf16[80,5120]{1,0:T(8,128)(2,1)S(1)}, bf16[80,5120]{1,0:T(8,128)(2,1)S(1)}, u32[]{:S(2)}, u32[]{:S(2)}) %collective-permute-start.5) | collective-permute-done | bytes 819232 | tf_op jit(solution)/shard_map/ppermute | solution.py:261
  70.6 6.6 %project_rows.6 = (bf16[4,160,128]{2,1,0:T(8,128)(2,1)S(1)}, bf16[8,160,128]{2,1,0:T(8,128)(2,1)S(1)}, bf16[6,5120,256]{2,1,0:T(8,128)(2,1)S(1)}) custom-call(bf16[80,5120]{1,0:T(8,128)(2,1)S(1)} %collective-permute-done.6.refs_0_, bf16[80,5120]{1,0:T(8,128)(2,1)S(1)} %collective-permute-done.5.refs_1_, bf16[3,5120,256]{2,1,0:T(8,128)(2,1)S(1)} %bitcast.23, ...), custom_call_target="tpu_custom_call" | custom-call | flops 2516582400 | bytes 15728640 | tf_op jit(solution)/shard_map/project_rows/pallas_call | solution.py:145
  77.3 7.9 %collective-permute-done.8.refs_1_ = bf16[80,5120]{1,0:T(8,128)(2,1)S(1)} collective-permute-done((bf16[80,5120]{1,0:T(8,128)(2,1)S(1)}, bf16[80,5120]{1,0:T(8,128)(2,1)S(1)}, u32[]{:S(2)}, u32[]{:S(2)}) %collective-permute-start.8) | collective-permute-done | bytes 819232 | tf_op jit(solution)/shard_map/ppermute | solution.py:261
  85.2 2.7 %project_rows.7 = (bf16[4,320,128]{2,1,0:T(8,128)(2,1)S(1)}, bf16[8,320,128]{2,1,0:T(8,128)(2,1)S(1)}) custom-call(bf16[80,5120]{1,0:T(8,128)(2,1)S(1)} %collective-permute-done.9.refs_0_, bf16[80,5120]{1,0:T(8,128)(2,1)S(1)} %collective-permute-done.8.refs_1_, bf16[6,5120,256]{2,1,0:T(8,128)(2,1)S(1)} %get-tuple-element.72.refs_2_, ...), custom_call_target="tpu_custom_call" | custom-call | flops 2516582400 | bytes 1638400 | tf_op jit(solution)/shard_map/project_rows/pallas_call | solution.py:145
  87.9 0.7 copy-done.5
  88.6 2.1 %collective-permute-done.11.refs_8_ = bf16[8,320,128]{2,1,0:T(8,128)(2,1)S(1)} collective-permute-done((bf16[8,320,128]{2,1,0:T(8,128)(2,1)S(1)}, bf16[8,320,128]{2,1,0:T(8,128)(2,1)S(1)}, u32[]{:S(2)}, u32[]{:S(2)}) %collective-permute-start.11) | collective-permute-done | bytes 655392 | tf_op jit(solution)/shard_map/ppermute | solution.py:264
  90.7 0.9 copy-done.8
  91.6 9.0 %attend.1 = f32[2,8,32,80]{3,2,1,0:T(8,128)} custom-call(s32[8]{0:T(128)} %get-tuple-element.65.place_ref, f32[1,1280]{1,0:T(1,128)} %reshape.56.bias_ref, bf16[2,64,128]{2,1,0:T(8,128)(2,1)} %bitcast.32, bf16[2,64,128]{2,1,0:T(8,128)(2,1)} %copy-done.11, bf16[4,160,128]{2,1,0:T(8,128)(2,1)} %copy-done.6, bf16[4,160,128]{2,1,0:T(8,128)(2,1)} %copy-done.7, ...), custom_call_target="tpu_custom_call" | custom-call | flops 1677721600 | bytes 10000000 | tf_op jit(solution)/shard_map/attend/pallas_call | solution.py:211
  100.6 10.3 %all-to-all-start = ((f32[16,32,80]{2,1,0:T(8,128)}), f32[16,32,80]{2,1,0:T(8,128)S(1)}, u32[]{:S(2)}, u32[]{:S(2)}) async-start(f32[16,32,80]{2,1,0:T(8,128)} %bitcast.29), calls=%async_computation | async-start | bytes 524288 | tf_op jit(solution)/shard_map/all_to_all | solution.py:331
  111.0 10.4 %all-to-all-done = f32[16,32,80]{2,1,0:T(8,128)S(1)} async-done(((f32[16,32,80]{2,1,0:T(8,128)}), f32[16,32,80]{2,1,0:T(8,128)S(1)}, u32[]{:S(2)}, u32[]{:S(2)}) %all-to-all-start) | async-done | bytes 163872 | tf_op jit(solution)/shard_map/all_to_all | solution.py:331
  (44 shorter events, 2.6 us)
Async XLA Ops:
  5.5 1.5 %collective-permute-start.2 = (bf16[2,64,128]{2,1,0:T(8,128)(2,1)}, bf16[2,64,128]{2,1,0:T(8,128)(2,1)S(1)}, u32[]{:S(2)}, u32[]{:S(2)}) collective-permute-start(bf16[2,64,128]{2,1,0:T(8,128)(2,1)} %bitcast.31), channel_id=1, source_target_pairs={{0,1},{1,0},{2,3},{3,2},{4,5},{5,4},{6,7},{7,6},{8,9},{9,8},{10,11... | collective-permute-start | bytes 98312 | tf_op jit(solution)/shard_map/ppermute | solution.py:264
  7.0 40.9 %copy-start.11 = (bf16[2,64,128]{2,1,0:T(8,128)(2,1)}, bf16[2,64,128]{2,1,0:T(8,128)(2,1)S(1)}, u32[]{:S(2)}) copy-start(bf16[2,64,128]{2,1,0:T(8,128)(2,1)S(1)} %collective-permute-done.2.hb_ref) | copy-start | bytes 98308
  7.0 29.9 %collective-permute-start.4 = (bf16[3,5120,256]{2,1,0:T(8,128)(2,1)}, bf16[3,5120,256]{2,1,0:T(8,128)(2,1)}, u32[]{:S(2)}, u32[]{:S(2)}) collective-permute-start(bf16[3,5120,256]{2,1,0:T(8,128)(2,1)} %bitcast.18), channel_id=1, source_target_pairs={{0,1},{1,0},{2,3},{3,2},{4,5},{5,4},{6,7},{7,6},{8,9},{9,8},{10,11... | collective-permute-start | bytes 23592968 | tf_op jit(solution)/shard_map/ppermute | solution.py:264
  7.2 22.8 %collective-permute-start = (bf16[80,5120]{1,0:T(8,128)(2,1)}, bf16[80,5120]{1,0:T(8,128)(2,1)S(1)}, u32[]{:S(2)}, u32[]{:S(2)}) collective-permute-start(bf16[80,5120]{1,0:T(8,128)(2,1)} %own_rows.1.refs_0_), channel_id=1, source_target_pairs={{0,2},{1,15},{2,4},{3,1},{4,6},{5,3},{6,8},{7,5},{8,10},{9,7},{10,... | collective-permute-start | bytes 2457608 | tf_op jit(solution)/shard_map/ppermute | solution.py:261
  9.1 23.5 %collective-permute-start.3 = (bf16[80,5120]{1,0:T(8,128)(2,1)}, bf16[80,5120]{1,0:T(8,128)(2,1)S(1)}, u32[]{:S(2)}, u32[]{:S(2)}) collective-permute-start(bf16[80,5120]{1,0:T(8,128)(2,1)} %own_rows.1.refs_0_), channel_id=1, source_target_pairs={{0,14},{1,3},{2,0},{3,5},{4,2},{5,7},{6,4},{7,9},{8,6},{9,11},{10,... | collective-permute-start | bytes 2457608 | tf_op jit(solution)/shard_map/ppermute | solution.py:261
  29.9 18.7 %collective-permute-start.1 = (bf16[80,5120]{1,0:T(8,128)(2,1)S(1)}, bf16[80,5120]{1,0:T(8,128)(2,1)S(1)}, u32[]{:S(2)}, u32[]{:S(2)}) collective-permute-start(bf16[80,5120]{1,0:T(8,128)(2,1)S(1)} %collective-permute-done.refs_1_), channel_id=1, source_target_pairs={{0,2},{1,15},{2,4},{3,1},{4,6},{5,3},{6,8},{7,5},{8,10},{9,7},{10,... | collective-permute-start | bytes 2457608 | tf_op jit(solution)/shard_map/ppermute | solution.py:261
  32.6 19.7 %collective-permute-start.6 = (bf16[80,5120]{1,0:T(8,128)(2,1)S(1)}, bf16[80,5120]{1,0:T(8,128)(2,1)S(1)}, u32[]{:S(2)}, u32[]{:S(2)}) collective-permute-start(bf16[80,5120]{1,0:T(8,128)(2,1)S(1)} %collective-permute-done.3.refs_0_), channel_id=1, source_target_pairs={{0,14},{1,3},{2,0},{3,5},{4,2},{5,7},{6,4},{7,9},{8,6},{9,11},{10,... | collective-permute-start | bytes 2457608 | tf_op jit(solution)/shard_map/ppermute | solution.py:261
  36.9 3.2 %copy-start = (bf16[1,5120,3,256]{3,1,2,0:T(8,128)(2,1)S(1)}, bf16[1,5120,3,256]{3,1,2,0:T(8,128)(2,1)}, u32[]{:S(2)}) copy-start(bf16[1,5120,3,256]{3,1,2,0:T(8,128)(2,1)} %param.18) | copy-start | bytes 23592964
  40.1 1.1 copy-start.1
  48.6 13.9 %copy-start.3 = (bf16[8,160,128]{2,1,0:T(8,128)(2,1)}, bf16[8,160,128]{2,1,0:T(8,128)(2,1)S(1)}, u32[]{:S(2)}) copy-start(bf16[8,160,128]{2,1,0:T(8,128)(2,1)S(1)} %get-tuple-element.53.refs_3_) | copy-start | bytes 983044
  48.6 22.0 %slice-start = ((s8[7864320]{0:T(1024)(128)(4,1)}), s8[4194304]{0:T(1024)(128)(4,1)S(1)}, s32[]{:S(2)}) async-start(s8[7864320]{0:T(1024)(128)(4,1)} %bitcast.21), calls=%async_computation.1 | async-start | bytes 8388608
  48.6 22.0 %slice-start.1 = ((s8[7864320]{0:T(1024)(128)(4,1)}), s8[3670016]{0:T(1024)(128)(4,1)S(1)}, s32[]{:S(2)}) async-start(s8[7864320]{0:T(1024)(128)(4,1)} %bitcast.21), calls=%async_computation.2 | async-start | bytes 7340032
  48.6 21.8 %collective-permute-start.5 = (bf16[80,5120]{1,0:T(8,128)(2,1)S(1)}, bf16[80,5120]{1,0:T(8,128)(2,1)S(1)}, u32[]{:S(2)}, u32[]{:S(2)}) collective-permute-start(bf16[80,5120]{1,0:T(8,128)(2,1)S(1)} %collective-permute-done.1.refs_1_), channel_id=1, source_target_pairs={{0,2},{1,15},{2,4},{3,1},{4,6},{5,3},{6,8},{7,5},{8,10},{9,7},{10,... | collective-permute-start | bytes 2457608 | tf_op jit(solution)/shard_map/ppermute | solution.py:261
  48.7 14.5 %collective-permute-start.7 = (bf16[8,160,128]{2,1,0:T(8,128)(2,1)S(1)}, bf16[8,160,128]{2,1,0:T(8,128)(2,1)S(1)}, u32[]{:S(2)}, u32[]{:S(2)}) collective-permute-start(bf16[8,160,128]{2,1,0:T(8,128)(2,1)S(1)} %get-tuple-element.53.refs_3_), channel_id=1, source_target_pairs={{0,1},{1,0},{2,3},{3,2},{4,5},{5,4},{6,7},{7,6},{8,9},{9,8},{10,11... | collective-permute-start | bytes 983048 | tf_op jit(solution)/shard_map/ppermute | solution.py:264
  52.3 18.3 %collective-permute-start.9 = (bf16[80,5120]{1,0:T(8,128)(2,1)S(1)}, bf16[80,5120]{1,0:T(8,128)(2,1)S(1)}, u32[]{:S(2)}, u32[]{:S(2)}) collective-permute-start(bf16[80,5120]{1,0:T(8,128)(2,1)S(1)} %collective-permute-done.6.refs_0_), channel_id=1, source_target_pairs={{0,14},{1,3},{2,0},{3,5},{4,2},{5,7},{6,4},{7,9},{8,6},{9,11},{10,... | collective-permute-start | bytes 2457608 | tf_op jit(solution)/shard_map/ppermute | solution.py:261
  63.2 14.1 %copy-start.4 = (bf16[8,160,128]{2,1,0:T(8,128)(2,1)}, bf16[8,160,128]{2,1,0:T(8,128)(2,1)S(1)}, u32[]{:S(2)}) copy-start(bf16[8,160,128]{2,1,0:T(8,128)(2,1)S(1)} %get-tuple-element.62.refs_4_) | copy-start | bytes 983044
  63.2 14.1 %copy-start.9 = (bf16[8,160,128]{2,1,0:T(8,128)(2,1)}, bf16[8,160,128]{2,1,0:T(8,128)(2,1)S(1)}, u32[]{:S(2)}) copy-start(bf16[8,160,128]{2,1,0:T(8,128)(2,1)S(1)} %collective-permute-done.7.refs_6_) | copy-start | bytes 983044
  70.4 14.8 %collective-permute-start.8 = (bf16[80,5120]{1,0:T(8,128)(2,1)S(1)}, bf16[80,5120]{1,0:T(8,128)(2,1)S(1)}, u32[]{:S(2)}, u32[]{:S(2)}) collective-permute-start(bf16[80,5120]{1,0:T(8,128)(2,1)S(1)} %collective-permute-done.5.refs_1_), channel_id=1, source_target_pairs={{0,2},{1,15},{2,4},{3,1},{4,6},{5,3},{6,8},{7,5},{8,10},{9,7},{10,... | collective-permute-start | bytes 2457608 | tf_op jit(solution)/shard_map/ppermute | solution.py:261
  70.4 6.8 %collective-permute-start.10 = (bf16[8,160,128]{2,1,0:T(8,128)(2,1)S(1)}, bf16[8,160,128]{2,1,0:T(8,128)(2,1)S(1)}, u32[]{:S(2)}, u32[]{:S(2)}) collective-permute-start(bf16[8,160,128]{2,1,0:T(8,128)(2,1)S(1)} %get-tuple-element.62.refs_4_), channel_id=1, source_target_pairs={{0,1},{1,0},{2,3},{3,2},{4,5},{5,4},{6,7},{7,6},{8,9},{9,8},{10,11... | collective-permute-start | bytes 983048 | tf_op jit(solution)/shard_map/ppermute | solution.py:264
  77.3 10.6 %copy-start.10 = (bf16[8,160,128]{2,1,0:T(8,128)(2,1)}, bf16[8,160,128]{2,1,0:T(8,128)(2,1)S(1)}, u32[]{:S(2)}) copy-start(bf16[8,160,128]{2,1,0:T(8,128)(2,1)S(1)} %collective-permute-done.10.refs_7_) | copy-start | bytes 983044
  88.6 2.1 %copy-start.2 = (bf16[8,320,128]{2,1,0:T(8,128)(2,1)}, bf16[8,320,128]{2,1,0:T(8,128)(2,1)S(1)}, u32[]{:S(2)}) copy-start(bf16[8,320,128]{2,1,0:T(8,128)(2,1)S(1)} %get-tuple-element.76.refs_5_) | copy-start | bytes 1966084
  88.6 2.1 %collective-permute-start.11 = (bf16[8,320,128]{2,1,0:T(8,128)(2,1)S(1)}, bf16[8,320,128]{2,1,0:T(8,128)(2,1)S(1)}, u32[]{:S(2)}, u32[]{:S(2)}) collective-permute-start(bf16[8,320,128]{2,1,0:T(8,128)(2,1)S(1)} %get-tuple-element.76.refs_5_), channel_id=1, source_target_pairs={{0,1},{1,0},{2,3},{3,2},{4,5},{5,4},{6,7},{7,6},{8,9},{9,8},{10,11... | collective-permute-start | bytes 1966088 | tf_op jit(solution)/shard_map/ppermute | solution.py:264
  90.7 0.9 copy-start.8
  100.6 20.8 %all-to-all-start = ((f32[16,32,80]{2,1,0:T(8,128)}), f32[16,32,80]{2,1,0:T(8,128)S(1)}, u32[]{:S(2)}, u32[]{:S(2)}) async-start(f32[16,32,80]{2,1,0:T(8,128)} %bitcast.29), calls=%async_computation | async-start | bytes 524288 | tf_op jit(solution)/shard_map/all_to_all | solution.py:331
  (3 other events, 2.1 us)

commit v3 on v2

--- a/solution.py
+++ b/solution.py
@@ -83,15 +83,52 @@
     )(step, hidden, mod, out_t, noise, stream, embed, table)
 
 
-def project_kernel(*refs, sizes, fetch, keep, before):
+def project_first_kernel(x_ref, w_any, q_ref, kv_ref, w_ref, sems):
+    copies = [pltpu.make_async_copy(w_any.at[n], w_ref.at[n], sems.at[n]) for n in range(3)]
+    for copy in copies:
+        copy.start()
+    size = q_ref.shape[2]
+    for n in range(3):
+        copies[n].wait()
+        value = dot(x_ref[...], w_ref[n], NN).astype(jnp.bfloat16)
+        for sub in range(2):
+            part = value[:, sub * size : (sub + 1) * size]
+            if n == 0:
+                q_ref[sub] = part
+            else:
+                kv_ref[2 * (n - 1) + sub] = part
+
+
+def project_first(x, w, head_size):
+    rows, width = x.shape
+    vmem = pl.BlockSpec(memory_space=pltpu.VMEM)
+    return pl.pallas_call(
+        project_first_kernel,
+        in_specs=[vmem, pl.BlockSpec(memory_space=pl.ANY)],
+        out_specs=[vmem] * 2,
+        out_shape=[
+            jax.ShapeDtypeStruct((2, rows, head_size), jnp.bfloat16),
+            jax.ShapeDtypeStruct((4, rows, head_size), jnp.bfloat16),
+        ],
+        scratch_shapes=[pltpu.VMEM(w.shape, w.dtype), pltpu.SemaphoreType.DMA((3,))],
+        compiler_params=pltpu.CompilerParams(vmem_limit_bytes=58 * MIB),
+        cost_estimate=pl.CostEstimate(
+            flops=6 * rows * width * w.shape[2], bytes_accessed=2 * w.size, transcendentals=0
+        ),
+        name="project_first",
+    )(x, w)
+
+
+def project_kernel(*refs, sizes, fetch, keep, before, ready):
     refs = list(refs)
     x_refs = [refs.pop(0) for _ in sizes]
     w_any = [refs.pop(0) for _ in range(2 if fetch else 1)]
     q_before, kv_before = (refs.pop(0), refs.pop(0)) if before else (None, None)
+    q_done, kv_done = (refs.pop(0), refs.pop(0)) if ready else (None, None)
     q_ref, kv_ref = refs.pop(0), refs.pop(0)
     w_ref = refs.pop(0) if fetch else w_any[0]
     x_buf = refs.pop(0)
-    copies = []
+    copies, x_copies = [], []
     if fetch:
         sems = refs.pop(0)
         copies = [
@@ -100,30 +137,40 @@
         for copy in copies[:3]:
             copy.start()
     at = 0
-    for ref, size in zip(x_refs, sizes):
-        x_buf[pl.ds(at, size)] = ref[...]
+    for i, (ref, size) in enumerate(zip(x_refs, sizes)):
+        if fetch:
+            x_copies.append(pltpu.make_async_copy(ref, x_buf.at[pl.ds(at, size)], sems.at[6 + i]))
+            x_copies[-1].start()
+        else:
+            x_buf[pl.ds(at, size)] = ref[...]
         at += size
+    for copy in x_copies:
+        copy.wait()
     size = q_ref.shape[2]
     if before:
         q_ref[:, pl.ds(0, before)] = q_before[...]
         kv_ref[:, pl.ds(0, before)] = kv_before[...]
-    here = pl.ds(before, sum(sizes))
     for n in range(6):
         if fetch:
             copies[n].wait()
             if n + 3 < 6:
                 copies[n + 3].start()
-        value = dot(x_buf[...], w_ref[n], NN).astype(jnp.bfloat16)
         pair, kind = n // 3, n % 3
+        skip = sizes[0] if ready and pair == 0 else 0
+        here = pl.ds(before + skip, sum(sizes) - skip)
+        value = dot(x_buf[pl.ds(skip, sum(sizes) - skip)], w_ref[n], NN).astype(jnp.bfloat16)
         for sub in range(2):
             part = value[:, sub * size : (sub + 1) * size]
             if kind == 0:
                 q_ref[2 * pair + sub, here] = part
             else:
                 kv_ref[4 * pair + 2 * (kind - 1) + sub, here] = part
-
-
-def project(xs, weights, head_size, keep=False, earlier=()):
+    if ready:
+        q_ref[0:2, pl.ds(0, sizes[0])] = q_done[...]
+        kv_ref[0:4, pl.ds(0, sizes[0])] = kv_done[...]
+
+
+def project(xs, weights, head_size, keep=False, earlier=(), ready=()):
     fetch = len(weights) == 2
     sizes = tuple(x.shape[0] for x in xs)
     width = xs[0].shape[1]
@@ -141,12 +188,13 @@
     elif fetch:
         scratch.insert(0, pltpu.VMEM((6, width, columns), jnp.bfloat16))
     if fetch:
-        scratch.append(pltpu.SemaphoreType.DMA((6,)))
+        scratch.append(pltpu.SemaphoreType.DMA((6 + len(xs),)))
     return pl.pallas_call(
-        functools.partial(project_kernel, sizes=sizes, fetch=fetch, keep=keep, before=before),
-        in_specs=[vmem] * len(xs)
-        + [pl.BlockSpec(memory_space=pl.ANY) if fetch else vmem] * len(weights)
-        + [vmem] * len(earlier),
+        functools.partial(
+            project_kernel, sizes=sizes, fetch=fetch, keep=keep, before=before, ready=bool(ready)
+        ),
+        in_specs=[pl.BlockSpec(memory_space=pl.ANY) if fetch else vmem] * (len(xs) + len(weights))
+        + [vmem] * (len(earlier) + len(ready)),
         out_specs=[vmem] * len(out_shape),
         out_shape=out_shape,
         scratch_shapes=scratch,
@@ -157,7 +205,7 @@
             transcendentals=0,
         ),
         name="project_rows",
-    )(*xs, *weights, *earlier)
+    )(*xs, *weights, *earlier, *ready)
 
 
 def attend_kernel(place_ref, bias_ref, ha_ref, hb_ref, *refs, calls, rows, sizes, scale):
@@ -167,24 +215,27 @@
     out_ref, q_buf, kv_buf, mix, heads, sems = refs[3 * calls :]
     own = sum(sizes)
     size = q_buf.shape[2]
-    pairs = []
+    pairs = [[], []]
     at = 0
     for i, count in enumerate(sizes):
         here, there = pl.ds(at, count), pl.ds(own + at, count)
-        pairs += [
-            (q_refs[i], q_buf.at[:, here]),
-            (own_refs[i].at[pl.ds(0, 8)], kv_buf.at[:, here]),
-            (far_refs[i].at[pl.ds(4, 4)], kv_buf.at[pl.ds(0, 4), there]),
-            (far_refs[i].at[pl.ds(0, 4)], kv_buf.at[pl.ds(4, 4), there]),
-        ]
+        pairs[0].append((q_refs[i], q_buf.at[:, here]))
+        for pair in range(2):
+            mine, theirs = pl.ds(4 * pair, 4), pl.ds(4 - 4 * pair, 4)
+            pairs[pair].append((own_refs[i].at[mine], kv_buf.at[mine, here]))
+            pairs[pair].append((far_refs[i].at[theirs], kv_buf.at[mine, there]))
         at += count
-    copies = [pltpu.make_async_copy(a, b, sems.at[j]) for j, (a, b) in enumerate(pairs)]
-    for copy in copies:
+    copies = [
+        [pltpu.make_async_copy(a, b, sems.at[3 * calls * pair + j]) for j, (a, b) in enumerate(pairs[pair])]
+        for pair in range(2)
+    ]
+    for copy in copies[0] + copies[1]:
         copy.start()
-    for copy in copies:
-        copy.wait()
     bias = bias_ref[...]
     for n in range(4):
+        if n % 2 == 0:
+            for copy in copies[n // 2]:
+                copy.wait()
         key = 4 * (n // 2) + n % 2
         scores = dot(q_buf[n], kv_buf[key], NT) * scale + bias
         highest = jnp.max(scores, -1, keepdims=True)
@@ -219,9 +270,9 @@
             pltpu.VMEM((8, 2 * own, head_size), jnp.bfloat16),
             pltpu.VMEM((own, 4 * head_size), jnp.bfloat16),
             pltpu.VMEM((patch, 4 * head_size), jnp.bfloat16),
-            pltpu.SemaphoreType.DMA((4 * calls,)),
+            pltpu.SemaphoreType.DMA((5 * calls,)),
         ],
-        compiler_params=pltpu.CompilerParams(vmem_limit_bytes=58 * MIB),
+        compiler_params=pltpu.CompilerParams(vmem_limit_bytes=26 * MIB),
         cost_estimate=pl.CostEstimate(
             flops=32 * own * own * head_size, bytes_accessed=10**7, transcendentals=8 * own * own
         ),
@@ -292,11 +343,11 @@
 
     up, down = [normed], [normed]
     up.append(hop(up[-1], 1))
-    begun, _ = lax.optimization_barrier((ha, normed))
+    fetched, begun, _ = lax.optimization_barrier((wa, ha, normed))
+    wb = other_core(fetched)
     hb = other_core(begun)
-    later, fetched, hb = lax.optimization_barrier((normed, wa, hb))
+    later, *ready = lax.optimization_barrier((normed, *project_first(normed, wa, head_size)))
     down.append(hop(later, -1))
-    wb = other_core(fetched)
     bias = jnp.concatenate([bias_of(core_at), bias_of(1 - core_at)]).reshape(1, -1)
     up.append(hop(up[-1], 1))
 
@@ -305,16 +356,18 @@
     weights, earlier = [wa, wb], ()
     for k in range(half_way):
         nearer, further = down[k], up[k + 1]
-        if k + 1 < half_way:
+        if 0 < k < half_way - 1:
             nearer, down[k + 1] = lax.optimization_barrier((nearer, down[k + 1]))
         if k + 2 < half_way:
             down.append(hop(down[k + 1], -1))
         q, kv, *kept = project(
-            [nearer, further], weights, head_size, keep=k == half_way - 2, earlier=earlier
+            [nearer, further], weights, head_size, keep=k == half_way - 2, earlier=earlier, ready=() if k else ready
         )
         weights = kept or weights
         if k + 2 <= half_way:
-            up[k + 2], q, kv, fars, bias, place = lax.optimization_barrier((up[k + 2], q, kv, fars, bias, place))
+            up[k + 2], q, kv, fars, bias, place, hb = lax.optimization_barrier(
+                (up[k + 2], q, kv, fars, bias, place, hb)
+            )
         if k + 3 <= half_way:
             up.append(hop(up[k + 2], 1))
         if k == half_way - 2:

time: 122 us -> 116 us (0.951)
  waiting for transfers between devices: 46.1 us -> 40.5 us
  Pallas kernels: 36.4 us -> 41.8 us
  local copies, waits for them, and re-layouts: 8 us -> 5.01 us
  starting transfers between devices: 28 us -> 25.5 us
    pallas_call x0 -> x1, Pallas kernels: none -> 6 us  [project_first(): pl.pallas_call(project_first_kernel, in_specs=[vmem, pl.BlockSpec(memory_...]
    ppermute x7, waiting for transfers between devices: 32.2 us -> 28 us  [hop(): return lax.ppermute(block, 'seq', route)]
    all_to_all x1, starting transfers between devices: 10.3 us -> 7.2 us  [local(): lax.all_to_all(terms, ('group', 'seq'), 0, 0, axis_index_groups=same_core...]
    unnamed x28 -> x18, local copies, waits for them, and re-layouts: 7.32 us -> 4.92 us
    ppermute x5, waiting for transfers between devices: 3.51 us -> 2.09 us  [other_core(): return lax.ppermute(block, 'seq', [(i, i ^ 1) for i in range(seq_count)])]
  transfers between devices with their start and end apart: 13 -> 13, of which waited for: 7 -> 6; matrix products, arithmetic and copies ran while one was open for 2% -> 0% of each run, Pallas kernels for 16% -> 22%
where the time goes in v3:
time: 116 us; the launch traced here: 115 us
  Pallas kernels  41.8 us (36%)
  waiting for transfers between devices  40.5 us (35%)
  starting transfers between devices  25.5 us (22%)
  local copies, waits for them, and re-layouts  5.01 us (4%)
  between operations  1.56 us (1%)
    ppermute x7, waiting for transfers between devices, hop(): return lax.ppermute(block, 'seq', route)  28 us
    pallas_call x4, Pallas kernels, project(): pl.pallas_call(functools.partial(project_kernel, sizes=sizes, fetch=fetch...  22.3 us
    ppermute x7, starting transfers between devices, hop(): return lax.ppermute(block, 'seq', route)  13.9 us
    all_to_all x1, waiting for transfers between devices, local(): lax.all_to_all(terms, ('group', 'seq'), 0, 0, axis_index_groups=same_core...  10.4 us
    pallas_call x1, Pallas kernels, attend(): pl.pallas_call(functools.partial(attend_kernel, calls=calls, rows=rows, s...  8.6 us
    all_to_all x1, starting transfers between devices, local(): lax.all_to_all(terms, ('group', 'seq'), 0, 0, axis_index_groups=same_core...  7.2 us
    pallas_call x1, Pallas kernels, project_first(): pl.pallas_call(project_first_kernel, in_specs=[vmem, pl.BlockSpec(memory_...  6 us
    unnamed x18, local copies, waits for them, and re-layouts  4.92 us
  transfers between devices with their start and end apart: 13, of which 6 were waited for; matrix products, arithmetic and copies ran while one was open for 0% of the time, Pallas kernels for 22%

profile of v3, /device:TPU:16, one launch (start us, length us, event | category | flops | bytes accessed | tf_op | source)
XLA Modules:
  0.0 115.2 jit_solution(3966197693389977050)
XLA Ops:
  0.7 4.9 %own_rows.1.x_ref.refs_0_ = bf16[80,5120]{1,0:T(8,128)(2,1)} custom-call(s32[1]{0:T(128)S(6)} %copy.13.step_ref, bf16[80,5120]{1,0:T(8,128)(2,1)} %bitcast.27, f32[2,5120]{1,0:T(2,128)} %mod_any.1, bf16[64,5120]{1,0:T(8,128)(2,1)} %bitcast.29, bf16[64,80]{1,0:T(8,128)(2,1)} %bitcast.32, bf16[80,5120]{1,0:T(8,128)(2,1)} %bitcast.28, ...), custom_call_target="tpu_custom_call" | custom-call | flops 200000000 | bytes 5000000 | tf_op jit(solution)/shard_map/own_rows/pallas_call | solution.py:73
  5.6 2.0 %collective-permute-start = (bf16[80,5120]{1,0:T(8,128)(2,1)}, bf16[80,5120]{1,0:T(8,128)(2,1)S(1)}, u32[]{:S(2)}, u32[]{:S(2)}) collective-permute-start(bf16[80,5120]{1,0:T(8,128)(2,1)} %own_rows.1.x_ref.refs_0_), channel_id=1, source_target_pairs={{0,2},{1,15},{2,4},{3,1},{4,6},{5,3},{6,8},{7,5},{8,10},{9,7},{10,... | collective-permute-start | bytes 2457608 | tf_op jit(solution)/shard_map/ppermute | solution.py:312
  7.6 6.0 %project_first.1 = (bf16[2,80,128]{2,1,0:T(8,128)(2,1)}, bf16[4,80,128]{2,1,0:T(8,128)(2,1)}) custom-call(bf16[80,5120]{1,0:T(8,128)(2,1)} %own_rows.1.x_ref.refs_0_, bf16[3,5120,256]{2,1,0:T(8,128)(2,1)} %bitcast.19), custom_call_target="tpu_custom_call" | custom-call | flops 629145600 | bytes 7864320 | tf_op jit(solution)/shard_map/project_first/pallas_call | solution.py:105
  13.7 4.1 %collective-permute-start.5 = (bf16[80,5120]{1,0:T(8,128)(2,1)S(1)}, bf16[80,5120]{1,0:T(8,128)(2,1)S(1)}, u32[]{:S(2)}, u32[]{:S(2)}) collective-permute-start(bf16[80,5120]{1,0:T(8,128)(2,1)S(1)} %copy-done.1), channel_id=1, source_target_pairs={{0,14},{1,3},{2,0},{3,5},{4,2},{5,7},{6,4},{7,9},{8,6},{9,11},{10,... | collective-permute-start | bytes 2457608 | tf_op jit(solution)/shard_map/ppermute | solution.py:312
  17.7 4.8 %collective-permute-done.refs_1_ = bf16[80,5120]{1,0:T(8,128)(2,1)S(1)} collective-permute-done((bf16[80,5120]{1,0:T(8,128)(2,1)}, bf16[80,5120]{1,0:T(8,128)(2,1)S(1)}, u32[]{:S(2)}, u32[]{:S(2)}) %collective-permute-start) | collective-permute-done | bytes 819232 | tf_op jit(solution)/shard_map/ppermute | solution.py:312
  22.5 0.6 collective-permute-start.1
  23.1 3.7 %collective-permute-start.3 = (bf16[2,64,128]{2,1,0:T(8,128)(2,1)S(1)}, bf16[2,64,128]{2,1,0:T(8,128)(2,1)S(1)}, u32[]{:S(2)}, u32[]{:S(2)}) collective-permute-start(bf16[2,64,128]{2,1,0:T(8,128)(2,1)S(1)} %bitcast.25), channel_id=1, source_target_pairs={{0,1},{1,0},{2,3},{3,2},{4,5},{5,4},{6,7},{7,6},{8,9},{9,8},{10,11... | collective-permute-start | bytes 98312 | tf_op jit(solution)/shard_map/ppermute | solution.py:315
  27.7 4.7 %collective-permute-done.5.refs_0_ = bf16[80,5120]{1,0:T(8,128)(2,1)S(1)} collective-permute-done((bf16[80,5120]{1,0:T(8,128)(2,1)S(1)}, bf16[80,5120]{1,0:T(8,128)(2,1)S(1)}, u32[]{:S(2)}, u32[]{:S(2)}) %collective-permute-start.5) | collective-permute-done | bytes 819232 | tf_op jit(solution)/shard_map/ppermute | solution.py:312
  32.4 3.7 %collective-permute-start.6 = (bf16[80,5120]{1,0:T(8,128)(2,1)S(1)}, bf16[80,5120]{1,0:T(8,128)(2,1)S(1)}, u32[]{:S(2)}, u32[]{:S(2)}) collective-permute-start(bf16[80,5120]{1,0:T(8,128)(2,1)S(1)} %collective-permute-done.5.refs_0_), channel_id=1, source_target_pairs={{0,14},{1,3},{2,0},{3,5},{4,2},{5,7},{6,4},{7,9},{8,6},{9,11},{10,... | collective-permute-start | bytes 2457608 | tf_op jit(solution)/shard_map/ppermute | solution.py:312
  36.1 3.2 %copy-done = bf16[1,5120,3,256]{3,1,2,0:T(8,128)(2,1)S(1)} copy-done((bf16[1,5120,3,256]{3,1,2,0:T(8,128)(2,1)S(1)}, bf16[1,5120,3,256]{3,1,2,0:T(8,128)(2,1)}, u32[]{:S(2)}) %copy-start) | copy-done | bytes 7864344
  39.4 0.9 copy-done.2
  40.3 0.8 copy-done.3
  41.0 6.1 %project_rows.4 = (bf16[4,160,128]{2,1,0:T(8,128)(2,1)S(1)}, bf16[8,160,128]{2,1,0:T(8,128)(2,1)S(1)}) custom-call(bf16[80,5120]{1,0:T(8,128)(2,1)S(1)} %copy-done.1, bf16[80,5120]{1,0:T(8,128)(2,1)S(1)} %collective-permute-done.refs_1_, bf16[3,5120,256]{2,1,0:T(8,128)(2,1)S(1)} %bitcast.20, bf16[3,5120,256]{2,1,0:T(8,128)(2,1)} %collective-permute-done.2.refs_3_, ...), custom_call_target="tpu_custom_call" | custom-call | flops 2516582400 | bytes 15728640 | tf_op jit(solution)/shard_map/project_rows/pallas_call | solution.py:192
  47.6 3.5 %collective-permute-start.9 = (bf16[80,5120]{1,0:T(8,128)(2,1)S(1)}, bf16[80,5120]{1,0:T(8,128)(2,1)S(1)}, u32[]{:S(2)}, u32[]{:S(2)}) collective-permute-start(bf16[80,5120]{1,0:T(8,128)(2,1)S(1)} %collective-permute-done.6.refs_0_), channel_id=1, source_target_pairs={{0,14},{1,3},{2,0},{3,5},{4,2},{5,7},{6,4},{7,9},{8,6},{9,11},{10,... | collective-permute-start | bytes 2457608 | tf_op jit(solution)/shard_map/ppermute | solution.py:312
  51.1 6.7 %project_rows.5 = (bf16[4,160,128]{2,1,0:T(8,128)(2,1)S(1)}, bf16[8,160,128]{2,1,0:T(8,128)(2,1)S(1)}) custom-call(bf16[80,5120]{1,0:T(8,128)(2,1)S(1)} %collective-permute-done.5.refs_0_, bf16[80,5120]{1,0:T(8,128)(2,1)S(1)} %collective-permute-done.1.refs_1_, bf16[3,5120,256]{2,1,0:T(8,128)(2,1)S(1)} %bitcast.21, ...), custom_call_target="tpu_custom_call" | custom-call | flops 2516582400 | bytes 15728640 | tf_op jit(solution)/shard_map/project_rows/pallas_call | solution.py:192
  57.9 11.7 %collective-permute-done.4.refs_1_ = bf16[80,5120]{1,0:T(8,128)(2,1)S(1)} collective-permute-done((bf16[80,5120]{1,0:T(8,128)(2,1)S(1)}, bf16[80,5120]{1,0:T(8,128)(2,1)S(1)}, u32[]{:S(2)}, u32[]{:S(2)}) %collective-permute-start.4) | collective-permute-done | bytes 819232 | tf_op jit(solution)/shard_map/ppermute | solution.py:312
  69.7 6.8 %project_rows.6 = (bf16[4,160,128]{2,1,0:T(8,128)(2,1)S(1)}, bf16[8,160,128]{2,1,0:T(8,128)(2,1)S(1)}, bf16[6,5120,256]{2,1,0:T(8,128)(2,1)S(1)}) custom-call(bf16[80,5120]{1,0:T(8,128)(2,1)S(1)} %collective-permute-done.6.refs_0_, bf16[80,5120]{1,0:T(8,128)(2,1)S(1)} %collective-permute-done.4.refs_1_, bf16[3,5120,256]{2,1,0:T(8,128)(2,1)S(1)} %bitcast.24, ...), custom_call_target="tpu_custom_call" | custom-call | flops 2516582400 | bytes 15728640 | tf_op jit(solution)/shard_map/project_rows/pallas_call | solution.py:192
  76.4 6.7 %collective-permute-done.8.refs_1_ = bf16[80,5120]{1,0:T(8,128)(2,1)S(1)} collective-permute-done((bf16[80,5120]{1,0:T(8,128)(2,1)S(1)}, bf16[80,5120]{1,0:T(8,128)(2,1)S(1)}, u32[]{:S(2)}, u32[]{:S(2)}) %collective-permute-start.8) | collective-permute-done | bytes 819232 | tf_op jit(solution)/shard_map/ppermute | solution.py:312
  83.2 2.7 %project_rows.7 = (bf16[4,320,128]{2,1,0:T(8,128)(2,1)S(1)}, bf16[8,320,128]{2,1,0:T(8,128)(2,1)S(1)}) custom-call(bf16[80,5120]{1,0:T(8,128)(2,1)S(1)} %collective-permute-done.9.refs_0_, bf16[80,5120]{1,0:T(8,128)(2,1)S(1)} %collective-permute-done.8.refs_1_, bf16[6,5120,256]{2,1,0:T(8,128)(2,1)S(1)} %get-tuple-element.80.refs_2_, ...), custom_call_target="tpu_custom_call" | custom-call | flops 2516582400 | bytes 1638400 | tf_op jit(solution)/shard_map/project_rows/pallas_call | solution.py:192
  86.2 2.1 %collective-permute-done.11.refs_8_ = bf16[8,320,128]{2,1,0:T(8,128)(2,1)S(1)} collective-permute-done((bf16[8,320,128]{2,1,0:T(8,128)(2,1)S(1)}, bf16[8,320,128]{2,1,0:T(8,128)(2,1)S(1)}, u32[]{:S(2)}, u32[]{:S(2)}) %collective-permute-start.11) | collective-permute-done | bytes 655392 | tf_op jit(solution)/shard_map/ppermute | solution.py:315
  88.3 8.6 %attend.1 = f32[2,8,32,80]{3,2,1,0:T(8,128)} custom-call(s32[8]{0:T(128)S(1)} %get-tuple-element.73.place_ref, f32[1,1280]{1,0:T(1,128)S(1)} %reshape.56.bias_ref, bf16[2,64,128]{2,1,0:T(8,128)(2,1)S(1)} %bitcast.26, bf16[2,64,128]{2,1,0:T(8,128)(2,1)S(1)} %collective-permute-done.3.hb_ref, bf16[4,160,128]{2,1,0:T(8,128)(2,1)S(1)} %get-tuple-element.76.refs_0_, ...), custom_call_target="tpu_custom_call" | custom-call | flops 1677721600 | bytes 10000000 | tf_op jit(solution)/shard_map/attend/pallas_call | solution.py:262
  96.9 7.2 %all-to-all-start = ((f32[16,32,80]{2,1,0:T(8,128)}), f32[16,32,80]{2,1,0:T(8,128)S(1)}, u32[]{:S(2)}, u32[]{:S(2)}) async-start(f32[16,32,80]{2,1,0:T(8,128)} %bitcast.12), calls=%async_computation | async-start | bytes 524288 | tf_op jit(solution)/shard_map/all_to_all | solution.py:384
  104.1 10.4 %all-to-all-done = f32[16,32,80]{2,1,0:T(8,128)S(1)} async-done(((f32[16,32,80]{2,1,0:T(8,128)}), f32[16,32,80]{2,1,0:T(8,128)S(1)}, u32[]{:S(2)}, u32[]{:S(2)}) %all-to-all-start) | async-done | bytes 163872 | tf_op jit(solution)/shard_map/all_to_all | solution.py:384
  114.6 0.6 bitcast_select_fusion
  (35 shorter events, 1.0 us)
Async XLA Ops:
  0.0 27.5 %copy-start.5 = (s32[8]{0:T(128)S(1)}, s32[8]{0:T(128)}, u32[]{:S(2)}) copy-start(s32[8]{0:T(128)} %constant.62.clone) | copy-start | bytes 100
  0.0 27.5 %copy-start.6 = (s32[8]{0:T(128)S(1)}, s32[8]{0:T(128)}, u32[]{:S(2)}) copy-start(s32[8]{0:T(128)} %constant.72) | copy-start | bytes 100
  0.0 23.1 %copy-start.4 = (bf16[1,2,128,64]{2,3,1,0:T(8,128)(2,1)S(1)}, bf16[1,2,128,64]{2,3,1,0:T(8,128)(2,1)}, u32[]{:S(2)}) copy-start(bf16[1,2,128,64]{2,3,1,0:T(8,128)(2,1)} %param.19) | copy-start | bytes 98308
  5.5 8.1 %copy-start.1 = (bf16[80,5120]{1,0:T(8,128)(2,1)S(1)}, bf16[80,5120]{1,0:T(8,128)(2,1)}, u32[]{:S(2)}) copy-start(bf16[80,5120]{1,0:T(8,128)(2,1)} %own_rows.1.x_ref.refs_0_) | copy-start | bytes 2457604
  5.5 30.6 %collective-permute-start.2 = (bf16[3,5120,256]{2,1,0:T(8,128)(2,1)}, bf16[3,5120,256]{2,1,0:T(8,128)(2,1)}, u32[]{:S(2)}, u32[]{:S(2)}) collective-permute-start(bf16[3,5120,256]{2,1,0:T(8,128)(2,1)} %bitcast.18), channel_id=1, source_target_pairs={{0,1},{1,0},{2,3},{3,2},{4,5},{5,4},{6,7},{7,6},{8,9},{9,8},{10,11... | collective-permute-start | bytes 23592968 | tf_op jit(solution)/shard_map/ppermute | solution.py:315
  5.6 16.9 %collective-permute-start = (bf16[80,5120]{1,0:T(8,128)(2,1)}, bf16[80,5120]{1,0:T(8,128)(2,1)S(1)}, u32[]{:S(2)}, u32[]{:S(2)}) collective-permute-start(bf16[80,5120]{1,0:T(8,128)(2,1)} %own_rows.1.x_ref.refs_0_), channel_id=1, source_target_pairs={{0,2},{1,15},{2,4},{3,1},{4,6},{5,3},{6,8},{7,5},{8,10},{9,7},{10,... | collective-permute-start | bytes 2457608 | tf_op jit(solution)/shard_map/ppermute | solution.py:312
  13.7 18.8 %collective-permute-start.5 = (bf16[80,5120]{1,0:T(8,128)(2,1)S(1)}, bf16[80,5120]{1,0:T(8,128)(2,1)S(1)}, u32[]{:S(2)}, u32[]{:S(2)}) collective-permute-start(bf16[80,5120]{1,0:T(8,128)(2,1)S(1)} %copy-done.1), channel_id=1, source_target_pairs={{0,14},{1,3},{2,0},{3,5},{4,2},{5,7},{6,4},{7,9},{8,6},{9,11},{10,... | collective-permute-start | bytes 2457608 | tf_op jit(solution)/shard_map/ppermute | solution.py:312
  22.5 24.7 %collective-permute-start.1 = (bf16[80,5120]{1,0:T(8,128)(2,1)S(1)}, bf16[80,5120]{1,0:T(8,128)(2,1)S(1)}, u32[]{:S(2)}, u32[]{:S(2)}) collective-permute-start(bf16[80,5120]{1,0:T(8,128)(2,1)S(1)} %collective-permute-done.refs_1_), channel_id=1, source_target_pairs={{0,2},{1,15},{2,4},{3,1},{4,6},{5,3},{6,8},{7,5},{8,10},{9,7},{10,... | collective-permute-start | bytes 2457608 | tf_op jit(solution)/shard_map/ppermute | solution.py:312
  23.1 24.1 %collective-permute-start.3 = (bf16[2,64,128]{2,1,0:T(8,128)(2,1)S(1)}, bf16[2,64,128]{2,1,0:T(8,128)(2,1)S(1)}, u32[]{:S(2)}, u32[]{:S(2)}) collective-permute-start(bf16[2,64,128]{2,1,0:T(8,128)(2,1)S(1)} %bitcast.25), channel_id=1, source_target_pairs={{0,1},{1,0},{2,3},{3,2},{4,5},{5,4},{6,7},{7,6},{8,9},{9,8},{10,11... | collective-permute-start | bytes 98312 | tf_op jit(solution)/shard_map/ppermute | solution.py:315
  32.4 15.2 %collective-permute-start.6 = (bf16[80,5120]{1,0:T(8,128)(2,1)S(1)}, bf16[80,5120]{1,0:T(8,128)(2,1)S(1)}, u32[]{:S(2)}, u32[]{:S(2)}) collective-permute-start(bf16[80,5120]{1,0:T(8,128)(2,1)S(1)} %collective-permute-done.5.refs_0_), channel_id=1, source_target_pairs={{0,14},{1,3},{2,0},{3,5},{4,2},{5,7},{6,4},{7,9},{8,6},{9,11},{10,... | collective-permute-start | bytes 2457608 | tf_op jit(solution)/shard_map/ppermute | solution.py:312
  36.1 3.2 %copy-start = (bf16[1,5120,3,256]{3,1,2,0:T(8,128)(2,1)S(1)}, bf16[1,5120,3,256]{3,1,2,0:T(8,128)(2,1)}, u32[]{:S(2)}) copy-start(bf16[1,5120,3,256]{3,1,2,0:T(8,128)(2,1)} %param.18) | copy-start | bytes 23592964
  39.4 0.9 copy-start.2
  40.3 0.8 copy-start.3
  47.2 22.4 %slice-start = ((s8[7864320]{0:T(1024)(128)(4,1)}), s8[4194304]{0:T(1024)(128)(4,1)S(1)}, s32[]{:S(2)}) async-start(s8[7864320]{0:T(1024)(128)(4,1)} %bitcast.22), calls=%async_computation.1 | async-start | bytes 8388608
  47.2 22.4 %slice-start.1 = ((s8[7864320]{0:T(1024)(128)(4,1)}), s8[3670016]{0:T(1024)(128)(4,1)S(1)}, s32[]{:S(2)}) async-start(s8[7864320]{0:T(1024)(128)(4,1)} %bitcast.22), calls=%async_computation.2 | async-start | bytes 7340032
  47.2 22.4 %collective-permute-start.4 = (bf16[80,5120]{1,0:T(8,128)(2,1)S(1)}, bf16[80,5120]{1,0:T(8,128)(2,1)S(1)}, u32[]{:S(2)}, u32[]{:S(2)}) collective-permute-start(bf16[80,5120]{1,0:T(8,128)(2,1)S(1)} %collective-permute-done.1.refs_1_), channel_id=1, source_target_pairs={{0,2},{1,15},{2,4},{3,1},{4,6},{5,3},{6,8},{7,5},{8,10},{9,7},{10,... | collective-permute-start | bytes 2457608 | tf_op jit(solution)/shard_map/ppermute | solution.py:312
  47.3 10.6 %collective-permute-start.7 = (bf16[8,160,128]{2,1,0:T(8,128)(2,1)S(1)}, bf16[8,160,128]{2,1,0:T(8,128)(2,1)S(1)}, u32[]{:S(2)}, u32[]{:S(2)}) collective-permute-start(bf16[8,160,128]{2,1,0:T(8,128)(2,1)S(1)} %get-tuple-element.59.refs_3_), channel_id=1, source_target_pairs={{0,1},{1,0},{2,3},{3,2},{4,5},{5,4},{6,7},{7,6},{8,9},{9,8},{10,11... | collective-permute-start | bytes 983048 | tf_op jit(solution)/shard_map/ppermute | solution.py:315
  47.6 22.0 %collective-permute-start.9 = (bf16[80,5120]{1,0:T(8,128)(2,1)S(1)}, bf16[80,5120]{1,0:T(8,128)(2,1)S(1)}, u32[]{:S(2)}, u32[]{:S(2)}) collective-permute-start(bf16[80,5120]{1,0:T(8,128)(2,1)S(1)} %collective-permute-done.6.refs_0_), channel_id=1, source_target_pairs={{0,14},{1,3},{2,0},{3,5},{4,2},{5,7},{6,4},{7,9},{8,6},{9,11},{10,... | collective-permute-start | bytes 2457608 | tf_op jit(solution)/shard_map/ppermute | solution.py:312
  69.6 13.6 %collective-permute-start.8 = (bf16[80,5120]{1,0:T(8,128)(2,1)S(1)}, bf16[80,5120]{1,0:T(8,128)(2,1)S(1)}, u32[]{:S(2)}, u32[]{:S(2)}) collective-permute-start(bf16[80,5120]{1,0:T(8,128)(2,1)S(1)} %collective-permute-done.4.refs_1_), channel_id=1, source_target_pairs={{0,2},{1,15},{2,4},{3,1},{4,6},{5,3},{6,8},{7,5},{8,10},{9,7},{10,... | collective-permute-start | bytes 2457608 | tf_op jit(solution)/shard_map/ppermute | solution.py:312
  69.6 6.8 %collective-permute-start.10 = (bf16[8,160,128]{2,1,0:T(8,128)(2,1)S(1)}, bf16[8,160,128]{2,1,0:T(8,128)(2,1)S(1)}, u32[]{:S(2)}, u32[]{:S(2)}) collective-permute-start(bf16[8,160,128]{2,1,0:T(8,128)(2,1)S(1)} %get-tuple-element.69.refs_4_), channel_id=1, source_target_pairs={{0,1},{1,0},{2,3},{3,2},{4,5},{5,4},{6,7},{7,6},{8,9},{9,8},{10,11... | collective-permute-start | bytes 983048 | tf_op jit(solution)/shard_map/ppermute | solution.py:315
  85.9 2.4 %collective-permute-start.11 = (bf16[8,320,128]{2,1,0:T(8,128)(2,1)S(1)}, bf16[8,320,128]{2,1,0:T(8,128)(2,1)S(1)}, u32[]{:S(2)}, u32[]{:S(2)}) collective-permute-start(bf16[8,320,128]{2,1,0:T(8,128)(2,1)S(1)} %get-tuple-element.84.refs_5_), channel_id=1, source_target_pairs={{0,1},{1,0},{2,3},{3,2},{4,5},{5,4},{6,7},{7,6},{8,9},{9,8},{10,11... | collective-permute-start | bytes 1966088 | tf_op jit(solution)/shard_map/ppermute | solution.py:315
  96.9 17.7 %all-to-all-start = ((f32[16,32,80]{2,1,0:T(8,128)}), f32[16,32,80]{2,1,0:T(8,128)S(1)}, u32[]{:S(2)}, u32[]{:S(2)}) async-start(f32[16,32,80]{2,1,0:T(8,128)} %bitcast.12), calls=%async_computation | async-start | bytes 524288 | tf_op jit(solution)/shard_map/all_to_all | solution.py:384

commit v4 on v3

--- a/solution.py
+++ b/solution.py
@@ -355,19 +355,22 @@
     qs, owns, fars = [], [], []
     weights, earlier = [wa, wb], ()
     for k in range(half_way):
-        nearer, further = down[k], up[k + 1]
-        if 0 < k < half_way - 1:
-            nearer, down[k + 1] = lax.optimization_barrier((nearer, down[k + 1]))
-        if k + 2 < half_way:
-            down.append(hop(down[k + 1], -1))
         q, kv, *kept = project(
-            [nearer, further], weights, head_size, keep=k == half_way - 2, earlier=earlier, ready=() if k else ready
+            [down[k], up[k + 1]],
+            weights,
+            head_size,
+            keep=k == half_way - 2,
+            earlier=earlier,
+            ready=() if k else ready,
         )
         weights = kept or weights
-        if k + 2 <= half_way:
-            up[k + 2], q, kv, fars, bias, place, hb = lax.optimization_barrier(
-                (up[k + 2], q, kv, fars, bias, place, hb)
+        if k + 2 < half_way:
+            down[k + 1], q, kv, fars, bias, place, hb = lax.optimization_barrier(
+                (down[k + 1], q, kv, fars, bias, place, hb)
             )
+            down.append(hop(down[k + 1], -1))
+        elif k + 2 == half_way:
+            down[k + 1], q, kv, fars = lax.optimization_barrier((down[k + 1], q, kv, fars))
         if k + 3 <= half_way:
             up.append(hop(up[k + 2], 1))
         if k == half_way - 2:

time: 116 us -> 113 us (0.974)
  starting transfers between devices: 25.5 us -> 22.8 us
    ppermute x7, starting transfers between devices: 13.9 us -> 9.45 us  [hop(): return lax.ppermute(block, 'seq', route)]
  transfers between devices with their start and end apart: 13 -> 13, of which waited for: 6 -> 8; matrix products, arithmetic and copies ran while one was open for 0% -> 0% of each run, Pallas kernels for 22% -> 23%
where the time goes in v4:
time: 113 us
  Pallas kernels  41.8 us (37%)
  waiting for transfers between devices  41.1 us (36%)
  starting transfers between devices  22.8 us (20%)
  local copies, waits for them, and re-layouts  5 us (4%)
  between operations  1.53 us (1%)
    ppermute x7, waiting for transfers between devices, hop(): return lax.ppermute(block, 'seq', route)  28.5 us
    pallas_call x4, Pallas kernels, project(): pl.pallas_call(functools.partial(project_kernel, sizes=sizes, fetch=fetch...  22.3 us
    all_to_all x1, waiting for transfers between devices, local(): lax.all_to_all(terms, ('group', 'seq'), 0, 0, axis_index_groups=same_core...  10.4 us
    ppermute x7, starting transfers between devices, hop(): return lax.ppermute(block, 'seq', route)  9.45 us
    pallas_call x1, Pallas kernels, attend(): pl.pallas_call(functools.partial(attend_kernel, calls=calls, rows=rows, s...  8.6 us
    all_to_all x1, starting transfers between devices, local(): lax.all_to_all(terms, ('group', 'seq'), 0, 0, axis_index_groups=same_core...  8.2 us
    pallas_call x1, Pallas kernels, project_first(): pl.pallas_call(project_first_kernel, in_specs=[vmem, pl.BlockSpec(memory_...  6 us
    ppermute x5, starting transfers between devices, other_core(): return lax.ppermute(block, 'seq', [(i, i ^ 1) for i in range(seq_count)])  5.19 us
  transfers between devices with their start and end apart: 13, of which 8 were waited for; matrix products, arithmetic and copies ran while one was open for 0% of the time, Pallas kernels for 23%

profile of v4, /device:TPU:16, one launch (start us, length us, event | category | flops | bytes accessed | tf_op | source)
XLA Modules:
  0.0 113.0 jit_solution(16105668816721567510)
XLA Ops:
  0.7 4.9 %own_rows.1.x_ref.refs_0_ = bf16[80,5120]{1,0:T(8,128)(2,1)} custom-call(s32[1]{0:T(128)S(6)} %copy.13.step_ref, bf16[80,5120]{1,0:T(8,128)(2,1)} %bitcast.27, f32[2,5120]{1,0:T(2,128)} %mod_any.1, bf16[64,5120]{1,0:T(8,128)(2,1)} %bitcast.29, bf16[64,80]{1,0:T(8,128)(2,1)} %bitcast.32, bf16[80,5120]{1,0:T(8,128)(2,1)} %bitcast.28, ...), custom_call_target="tpu_custom_call" | custom-call | flops 200000000 | bytes 5000000 | tf_op jit(solution)/shard_map/own_rows/pallas_call | solution.py:73
  5.6 2.0 %collective-permute-start.1 = (bf16[80,5120]{1,0:T(8,128)(2,1)}, bf16[80,5120]{1,0:T(8,128)(2,1)S(1)}, u32[]{:S(2)}, u32[]{:S(2)}) collective-permute-start(bf16[80,5120]{1,0:T(8,128)(2,1)} %own_rows.1.x_ref.refs_0_), channel_id=1, source_target_pairs={{0,2},{1,15},{2,4},{3,1},{4,6},{5,3},{6,8},{7,5},{8,10},{9,7},{10,... | collective-permute-start | bytes 2457608 | tf_op jit(solution)/shard_map/ppermute | solution.py:312
  7.6 6.0 %project_first.1 = (bf16[2,80,128]{2,1,0:T(8,128)(2,1)}, bf16[4,80,128]{2,1,0:T(8,128)(2,1)}) custom-call(bf16[80,5120]{1,0:T(8,128)(2,1)} %own_rows.1.x_ref.refs_0_, bf16[3,5120,256]{2,1,0:T(8,128)(2,1)} %bitcast.19), custom_call_target="tpu_custom_call" | custom-call | flops 629145600 | bytes 7864320 | tf_op jit(solution)/shard_map/project_first/pallas_call | solution.py:105
  13.7 4.1 %collective-permute-start = (bf16[80,5120]{1,0:T(8,128)(2,1)S(1)}, bf16[80,5120]{1,0:T(8,128)(2,1)S(1)}, u32[]{:S(2)}, u32[]{:S(2)}) collective-permute-start(bf16[80,5120]{1,0:T(8,128)(2,1)S(1)} %copy-done.1), channel_id=1, source_target_pairs={{0,14},{1,3},{2,0},{3,5},{4,2},{5,7},{6,4},{7,9},{8,6},{9,11},{10,... | collective-permute-start | bytes 2457608 | tf_op jit(solution)/shard_map/ppermute | solution.py:312
  17.7 4.8 %collective-permute-done.1.refs_1_ = bf16[80,5120]{1,0:T(8,128)(2,1)S(1)} collective-permute-done((bf16[80,5120]{1,0:T(8,128)(2,1)}, bf16[80,5120]{1,0:T(8,128)(2,1)S(1)}, u32[]{:S(2)}, u32[]{:S(2)}) %collective-permute-start.1) | collective-permute-done | bytes 819232 | tf_op jit(solution)/shard_map/ppermute | solution.py:312
  23.1 3.7 %collective-permute-start.3 = (bf16[2,64,128]{2,1,0:T(8,128)(2,1)S(1)}, bf16[2,64,128]{2,1,0:T(8,128)(2,1)S(1)}, u32[]{:S(2)}, u32[]{:S(2)}) collective-permute-start(bf16[2,64,128]{2,1,0:T(8,128)(2,1)S(1)} %bitcast.25), channel_id=1, source_target_pairs={{0,1},{1,0},{2,3},{3,2},{4,5},{5,4},{6,7},{7,6},{8,9},{9,8},{10,11... | collective-permute-start | bytes 98312 | tf_op jit(solution)/shard_map/ppermute | solution.py:315
  27.7 3.2 %copy-done = bf16[1,5120,3,256]{3,1,2,0:T(8,128)(2,1)S(1)} copy-done((bf16[1,5120,3,256]{3,1,2,0:T(8,128)(2,1)S(1)}, bf16[1,5120,3,256]{3,1,2,0:T(8,128)(2,1)}, u32[]{:S(2)}) %copy-start) | copy-done | bytes 7864344
  31.0 0.9 copy-done.2
  31.9 0.8 copy-done.3
  32.6 6.1 %project_rows.4 = (bf16[4,160,128]{2,1,0:T(8,128)(2,1)S(1)}, bf16[8,160,128]{2,1,0:T(8,128)(2,1)S(1)}) custom-call(bf16[80,5120]{1,0:T(8,128)(2,1)S(1)} %copy-done.1, bf16[80,5120]{1,0:T(8,128)(2,1)S(1)} %collective-permute-done.1.refs_1_, bf16[3,5120,256]{2,1,0:T(8,128)(2,1)S(1)} %bitcast.20, bf16[3,5120,256]{2,1,0:T(8,128)(2,1)} %collective-permute-done.2.refs_3_, ...), custom_call_target="tpu_custom_call" | custom-call | flops 2516582400 | bytes 15728640 | tf_op jit(solution)/shard_map/project_rows/pallas_call | solution.py:192
  39.7 1.3 %collective-permute-start.8 = (bf16[80,5120]{1,0:T(8,128)(2,1)S(1)}, bf16[80,5120]{1,0:T(8,128)(2,1)S(1)}, u32[]{:S(2)}, u32[]{:S(2)}) collective-permute-start(bf16[80,5120]{1,0:T(8,128)(2,1)S(1)} %collective-permute-done.5.refs_1_), channel_id=1, source_target_pairs={{0,2},{1,15},{2,4},{3,1},{4,6},{5,3},{6,8},{7,5},{8,10},{9,7},{10,... | collective-permute-start | bytes 2457608 | tf_op jit(solution)/shard_map/ppermute | solution.py:312
  40.9 0.9 collective-permute-start.6
  41.9 6.7 %project_rows.5 = (bf16[4,160,128]{2,1,0:T(8,128)(2,1)S(1)}, bf16[8,160,128]{2,1,0:T(8,128)(2,1)S(1)}) custom-call(bf16[80,5120]{1,0:T(8,128)(2,1)S(1)} %collective-permute-done.refs_0_, bf16[80,5120]{1,0:T(8,128)(2,1)S(1)} %collective-permute-done.5.refs_1_, bf16[3,5120,256]{2,1,0:T(8,128)(2,1)S(1)} %bitcast.21, ...), custom_call_target="tpu_custom_call" | custom-call | flops 2516582400 | bytes 15728640 | tf_op jit(solution)/shard_map/project_rows/pallas_call | solution.py:192
  48.7 10.5 %collective-permute-done.4.refs_0_ = bf16[80,5120]{1,0:T(8,128)(2,1)S(1)} collective-permute-done((bf16[80,5120]{1,0:T(8,128)(2,1)S(1)}, bf16[80,5120]{1,0:T(8,128)(2,1)S(1)}, u32[]{:S(2)}, u32[]{:S(2)}) %collective-permute-start.4) | collective-permute-done | bytes 819232 | tf_op jit(solution)/shard_map/ppermute | solution.py:312
  59.4 0.8 collective-permute-done.8.refs_1_
  60.3 0.9 collective-permute-start.10
  61.3 6.7 %project_rows.6 = (bf16[4,160,128]{2,1,0:T(8,128)(2,1)S(1)}, bf16[8,160,128]{2,1,0:T(8,128)(2,1)S(1)}, bf16[6,5120,256]{2,1,0:T(8,128)(2,1)S(1)}) custom-call(bf16[80,5120]{1,0:T(8,128)(2,1)S(1)} %collective-permute-done.4.refs_0_, bf16[80,5120]{1,0:T(8,128)(2,1)S(1)} %collective-permute-done.8.refs_1_, bf16[3,5120,256]{2,1,0:T(8,128)(2,1)S(1)} %bitcast.24, ...), custom_call_target="tpu_custom_call" | custom-call | flops 2516582400 | bytes 15728640 | tf_op jit(solution)/shard_map/project_rows/pallas_call | solution.py:192
  68.0 11.7 %collective-permute-done.7.refs_0_ = bf16[80,5120]{1,0:T(8,128)(2,1)S(1)} collective-permute-done((bf16[80,5120]{1,0:T(8,128)(2,1)S(1)}, bf16[80,5120]{1,0:T(8,128)(2,1)S(1)}, u32[]{:S(2)}, u32[]{:S(2)}) %collective-permute-start.7) | collective-permute-done | bytes 819232 | tf_op jit(solution)/shard_map/ppermute | solution.py:312
  80.0 2.7 %project_rows.7 = (bf16[4,320,128]{2,1,0:T(8,128)(2,1)S(1)}, bf16[8,320,128]{2,1,0:T(8,128)(2,1)S(1)}) custom-call(bf16[80,5120]{1,0:T(8,128)(2,1)S(1)} %collective-permute-done.7.refs_0_, bf16[80,5120]{1,0:T(8,128)(2,1)S(1)} %collective-permute-done.10.refs_1_, bf16[6,5120,256]{2,1,0:T(8,128)(2,1)S(1)} %get-tuple-element.66.refs_2_, ...), custom_call_target="tpu_custom_call" | custom-call | flops 2516582400 | bytes 1638400 | tf_op jit(solution)/shard_map/project_rows/pallas_call | solution.py:192
  83.0 2.1 %collective-permute-done.11.refs_8_ = bf16[8,320,128]{2,1,0:T(8,128)(2,1)S(1)} collective-permute-done((bf16[8,320,128]{2,1,0:T(8,128)(2,1)S(1)}, bf16[8,320,128]{2,1,0:T(8,128)(2,1)S(1)}, u32[]{:S(2)}, u32[]{:S(2)}) %collective-permute-start.11) | collective-permute-done | bytes 655392 | tf_op jit(solution)/shard_map/ppermute | solution.py:315
  85.1 8.6 %attend.1 = f32[2,8,32,80]{3,2,1,0:T(8,128)} custom-call(s32[8]{0:T(128)S(1)} %get-tuple-element.55.place_ref, f32[1,1280]{1,0:T(1,128)S(1)} %reshape.56.bias_ref, bf16[2,64,128]{2,1,0:T(8,128)(2,1)S(1)} %bitcast.26, bf16[2,64,128]{2,1,0:T(8,128)(2,1)S(1)} %collective-permute-done.3.hb_ref, bf16[4,160,128]{2,1,0:T(8,128)(2,1)S(1)} %get-tuple-element.58.refs_0_, ...), custom_call_target="tpu_custom_call" | custom-call | flops 1677721600 | bytes 10000000 | tf_op jit(solution)/shard_map/attend/pallas_call | solution.py:262
  93.7 8.2 %all-to-all-start = ((f32[16,32,80]{2,1,0:T(8,128)}), f32[16,32,80]{2,1,0:T(8,128)S(1)}, u32[]{:S(2)}, u32[]{:S(2)}) async-start(f32[16,32,80]{2,1,0:T(8,128)} %bitcast.12), calls=%async_computation | async-start | bytes 524288 | tf_op jit(solution)/shard_map/all_to_all | solution.py:387
  101.9 10.4 %all-to-all-done = f32[16,32,80]{2,1,0:T(8,128)S(1)} async-done(((f32[16,32,80]{2,1,0:T(8,128)}), f32[16,32,80]{2,1,0:T(8,128)S(1)}, u32[]{:S(2)}, u32[]{:S(2)}) %all-to-all-start) | async-done | bytes 163872 | tf_op jit(solution)/shard_map/all_to_all | solution.py:387
  112.4 0.6 bitcast_select_fusion
  (35 shorter events, 2.6 us)
Async XLA Ops:
  0.0 27.5 %copy-start.5 = (s32[8]{0:T(128)S(1)}, s32[8]{0:T(128)}, u32[]{:S(2)}) copy-start(s32[8]{0:T(128)} %constant.62.clone) | copy-start | bytes 100
  0.0 27.5 %copy-start.6 = (s32[8]{0:T(128)S(1)}, s32[8]{0:T(128)}, u32[]{:S(2)}) copy-start(s32[8]{0:T(128)} %constant.72) | copy-start | bytes 100
  0.0 23.1 %copy-start.4 = (bf16[1,2,128,64]{2,3,1,0:T(8,128)(2,1)S(1)}, bf16[1,2,128,64]{2,3,1,0:T(8,128)(2,1)}, u32[]{:S(2)}) copy-start(bf16[1,2,128,64]{2,3,1,0:T(8,128)(2,1)} %param.19) | copy-start | bytes 98308
  5.5 8.1 %copy-start.1 = (bf16[80,5120]{1,0:T(8,128)(2,1)S(1)}, bf16[80,5120]{1,0:T(8,128)(2,1)}, u32[]{:S(2)}) copy-start(bf16[80,5120]{1,0:T(8,128)(2,1)} %own_rows.1.x_ref.refs_0_) | copy-start | bytes 2457604
  5.5 22.2 %collective-permute-start.2 = (bf16[3,5120,256]{2,1,0:T(8,128)(2,1)}, bf16[3,5120,256]{2,1,0:T(8,128)(2,1)}, u32[]{:S(2)}, u32[]{:S(2)}) collective-permute-start(bf16[3,5120,256]{2,1,0:T(8,128)(2,1)} %bitcast.18), channel_id=1, source_target_pairs={{0,1},{1,0},{2,3},{3,2},{4,5},{5,4},{6,7},{7,6},{8,9},{9,8},{10,11... | collective-permute-start | bytes 23592968 | tf_op jit(solution)/shard_map/ppermute | solution.py:315
  5.6 16.9 %collective-permute-start.1 = (bf16[80,5120]{1,0:T(8,128)(2,1)}, bf16[80,5120]{1,0:T(8,128)(2,1)S(1)}, u32[]{:S(2)}, u32[]{:S(2)}) collective-permute-start(bf16[80,5120]{1,0:T(8,128)(2,1)} %own_rows.1.x_ref.refs_0_), channel_id=1, source_target_pairs={{0,2},{1,15},{2,4},{3,1},{4,6},{5,3},{6,8},{7,5},{8,10},{9,7},{10,... | collective-permute-start | bytes 2457608 | tf_op jit(solution)/shard_map/ppermute | solution.py:312
  13.7 25.1 %collective-permute-start = (bf16[80,5120]{1,0:T(8,128)(2,1)S(1)}, bf16[80,5120]{1,0:T(8,128)(2,1)S(1)}, u32[]{:S(2)}, u32[]{:S(2)}) collective-permute-start(bf16[80,5120]{1,0:T(8,128)(2,1)S(1)} %copy-done.1), channel_id=1, source_target_pairs={{0,14},{1,3},{2,0},{3,5},{4,2},{5,7},{6,4},{7,9},{8,6},{9,11},{10,... | collective-permute-start | bytes 2457608 | tf_op jit(solution)/shard_map/ppermute | solution.py:312
  22.5 17.1 %collective-permute-start.5 = (bf16[80,5120]{1,0:T(8,128)(2,1)S(1)}, bf16[80,5120]{1,0:T(8,128)(2,1)S(1)}, u32[]{:S(2)}, u32[]{:S(2)}) collective-permute-start(bf16[80,5120]{1,0:T(8,128)(2,1)S(1)} %collective-permute-done.1.refs_1_), channel_id=1, source_target_pairs={{0,2},{1,15},{2,4},{3,1},{4,6},{5,3},{6,8},{7,5},{8,10},{9,7},{10,... | collective-permute-start | bytes 2457608 | tf_op jit(solution)/shard_map/ppermute | solution.py:312
  23.1 15.7 %collective-permute-start.3 = (bf16[2,64,128]{2,1,0:T(8,128)(2,1)S(1)}, bf16[2,64,128]{2,1,0:T(8,128)(2,1)S(1)}, u32[]{:S(2)}, u32[]{:S(2)}) collective-permute-start(bf16[2,64,128]{2,1,0:T(8,128)(2,1)S(1)} %bitcast.25), channel_id=1, source_target_pairs={{0,1},{1,0},{2,3},{3,2},{4,5},{5,4},{6,7},{7,6},{8,9},{9,8},{10,11... | collective-permute-start | bytes 98312 | tf_op jit(solution)/shard_map/ppermute | solution.py:315
  27.7 3.2 %copy-start = (bf16[1,5120,3,256]{3,1,2,0:T(8,128)(2,1)S(1)}, bf16[1,5120,3,256]{3,1,2,0:T(8,128)(2,1)}, u32[]{:S(2)}) copy-start(bf16[1,5120,3,256]{3,1,2,0:T(8,128)(2,1)} %param.18) | copy-start | bytes 23592964
  31.0 0.9 copy-start.2
  31.9 0.8 copy-start.3
  38.8 22.5 %slice-start = ((s8[7864320]{0:T(1024)(128)(4,1)}), s8[4194304]{0:T(1024)(128)(4,1)S(1)}, s32[]{:S(2)}) async-start(s8[7864320]{0:T(1024)(128)(4,1)} %bitcast.22), calls=%async_computation.1 | async-start | bytes 8388608
  38.8 22.5 %slice-start.1 = ((s8[7864320]{0:T(1024)(128)(4,1)}), s8[3670016]{0:T(1024)(128)(4,1)S(1)}, s32[]{:S(2)}) async-start(s8[7864320]{0:T(1024)(128)(4,1)} %bitcast.22), calls=%async_computation.2 | async-start | bytes 7340032
  38.8 20.3 %collective-permute-start.4 = (bf16[80,5120]{1,0:T(8,128)(2,1)S(1)}, bf16[80,5120]{1,0:T(8,128)(2,1)S(1)}, u32[]{:S(2)}, u32[]{:S(2)}) collective-permute-start(bf16[80,5120]{1,0:T(8,128)(2,1)S(1)} %collective-permute-done.refs_0_), channel_id=1, source_target_pairs={{0,14},{1,3},{2,0},{3,5},{4,2},{5,7},{6,4},{7,9},{8,6},{9,11},{10,... | collective-permute-start | bytes 2457608 | tf_op jit(solution)/shard_map/ppermute | solution.py:312
  39.7 20.6 %collective-permute-start.8 = (bf16[80,5120]{1,0:T(8,128)(2,1)S(1)}, bf16[80,5120]{1,0:T(8,128)(2,1)S(1)}, u32[]{:S(2)}, u32[]{:S(2)}) collective-permute-start(bf16[80,5120]{1,0:T(8,128)(2,1)S(1)} %collective-permute-done.5.refs_1_), channel_id=1, source_target_pairs={{0,2},{1,15},{2,4},{3,1},{4,6},{5,3},{6,8},{7,5},{8,10},{9,7},{10,... | collective-permute-start | bytes 2457608 | tf_op jit(solution)/shard_map/ppermute | solution.py:312
  40.9 7.7 %collective-permute-start.6 = (bf16[8,160,128]{2,1,0:T(8,128)(2,1)S(1)}, bf16[8,160,128]{2,1,0:T(8,128)(2,1)S(1)}, u32[]{:S(2)}, u32[]{:S(2)}) collective-permute-start(bf16[8,160,128]{2,1,0:T(8,128)(2,1)S(1)} %get-tuple-element.51.refs_3_), channel_id=1, source_target_pairs={{0,1},{1,0},{2,3},{3,2},{4,5},{5,4},{6,7},{7,6},{8,9},{9,8},{10,11... | collective-permute-start | bytes 983048 | tf_op jit(solution)/shard_map/ppermute | solution.py:315
  59.2 20.6 %collective-permute-start.7 = (bf16[80,5120]{1,0:T(8,128)(2,1)S(1)}, bf16[80,5120]{1,0:T(8,128)(2,1)S(1)}, u32[]{:S(2)}, u32[]{:S(2)}) collective-permute-start(bf16[80,5120]{1,0:T(8,128)(2,1)S(1)} %collective-permute-done.4.refs_0_), channel_id=1, source_target_pairs={{0,14},{1,3},{2,0},{3,5},{4,2},{5,7},{6,4},{7,9},{8,6},{9,11},{10,... | collective-permute-start | bytes 2457608 | tf_op jit(solution)/shard_map/ppermute | solution.py:312
  60.3 19.7 %collective-permute-start.10 = (bf16[80,5120]{1,0:T(8,128)(2,1)S(1)}, bf16[80,5120]{1,0:T(8,128)(2,1)S(1)}, u32[]{:S(2)}, u32[]{:S(2)}) collective-permute-start(bf16[80,5120]{1,0:T(8,128)(2,1)S(1)} %collective-permute-done.8.refs_1_), channel_id=1, source_target_pairs={{0,2},{1,15},{2,4},{3,1},{4,6},{5,3},{6,8},{7,5},{8,10},{9,7},{10,... | collective-permute-start | bytes 2457608 | tf_op jit(solution)/shard_map/ppermute | solution.py:312
  61.2 6.8 %collective-permute-start.9 = (bf16[8,160,128]{2,1,0:T(8,128)(2,1)S(1)}, bf16[8,160,128]{2,1,0:T(8,128)(2,1)S(1)}, u32[]{:S(2)}, u32[]{:S(2)}) collective-permute-start(bf16[8,160,128]{2,1,0:T(8,128)(2,1)S(1)} %get-tuple-element.64.refs_4_), channel_id=1, source_target_pairs={{0,1},{1,0},{2,3},{3,2},{4,5},{5,4},{6,7},{7,6},{8,9},{9,8},{10,11... | collective-permute-start | bytes 983048 | tf_op jit(solution)/shard_map/ppermute | solution.py:315
  82.7 2.4 %collective-permute-start.11 = (bf16[8,320,128]{2,1,0:T(8,128)(2,1)S(1)}, bf16[8,320,128]{2,1,0:T(8,128)(2,1)S(1)}, u32[]{:S(2)}, u32[]{:S(2)}) collective-permute-start(bf16[8,320,128]{2,1,0:T(8,128)(2,1)S(1)} %get-tuple-element.70.refs_5_), channel_id=1, source_target_pairs={{0,1},{1,0},{2,3},{3,2},{4,5},{5,4},{6,7},{7,6},{8,9},{9,8},{10,11... | collective-permute-start | bytes 1966088 | tf_op jit(solution)/shard_map/ppermute | solution.py:315
  93.7 18.7 %all-to-all-start = ((f32[16,32,80]{2,1,0:T(8,128)}), f32[16,32,80]{2,1,0:T(8,128)S(1)}, u32[]{:S(2)}, u32[]{:S(2)}) async-start(f32[16,32,80]{2,1,0:T(8,128)} %bitcast.12), calls=%async_computation | async-start | bytes 524288 | tf_op jit(solution)/shard_map/all_to_all | solution.py:387

commit v5 on v4

--- a/solution.py
+++ b/solution.py
@@ -343,9 +343,8 @@
 
     up, down = [normed], [normed]
     up.append(hop(up[-1], 1))
-    fetched, begun, _ = lax.optimization_barrier((wa, ha, normed))
+    fetched, _ = lax.optimization_barrier((wa, normed))
     wb = other_core(fetched)
-    hb = other_core(begun)
     later, *ready = lax.optimization_barrier((normed, *project_first(normed, wa, head_size)))
     down.append(hop(later, -1))
     bias = jnp.concatenate([bias_of(core_at), bias_of(1 - core_at)]).reshape(1, -1)
@@ -364,13 +363,16 @@
             ready=() if k else ready,
         )
         weights = kept or weights
+        if k == 0:
+            begun, kv = lax.optimization_barrier((ha, kv))
+            hb = other_core(begun)
         if k + 2 < half_way:
-            down[k + 1], q, kv, fars, bias, place, hb = lax.optimization_barrier(
-                (down[k + 1], q, kv, fars, bias, place, hb)
+            down[k + 1], q, kv, fars, bias, place = lax.optimization_barrier(
+                (down[k + 1], q, kv, fars, bias, place)
             )
             down.append(hop(down[k + 1], -1))
         elif k + 2 == half_way:
-            down[k + 1], q, kv, fars = lax.optimization_barrier((down[k + 1], q, kv, fars))
+            down[k + 1], q, kv, fars, hb = lax.optimization_barrier((down[k + 1], q, kv, fars, hb))
         if k + 3 <= half_way:
             up.append(hop(up[k + 2], 1))
         if k == half_way - 2:

time: 113 us -> 110 us (0.973)
  waiting for transfers between devices: 41.1 us -> 37.8 us
    ppermute x7, starting transfers between devices: 9.45 us -> 14.3 us  [hop(): return lax.ppermute(block, 'seq', route)]
    ppermute x7, waiting for transfers between devices: 28.5 us -> 25.2 us  [hop(): return lax.ppermute(block, 'seq', route)]
    all_to_all x1, starting transfers between devices: 8.2 us -> 4.96 us  [local(): lax.all_to_all(terms, ('group', 'seq'), 0, 0, axis_index_groups=same_core...]
    ppermute x5, starting transfers between devices: 5.19 us -> 3.63 us  [other_core(): return lax.ppermute(block, 'seq', [(i, i ^ 1) for i in range(seq_count)])]
where the time goes in v5:
time: 110 us
  Pallas kernels  41.8 us (38%)
  waiting for transfers between devices  37.8 us (34%)
  starting transfers between devices  22.8 us (21%)
  local copies, waits for them, and re-layouts  5.01 us (5%)
  between operations  1.57 us (1%)
    ppermute x7, waiting for transfers between devices, hop(): return lax.ppermute(block, 'seq', route)  25.2 us
    pallas_call x4, Pallas kernels, project(): pl.pallas_call(functools.partial(project_kernel, sizes=sizes, fetch=fetch...  22.3 us
    ppermute x7, starting transfers between devices, hop(): return lax.ppermute(block, 'seq', route)  14.3 us
    all_to_all x1, waiting for transfers between devices, local(): lax.all_to_all(terms, ('group', 'seq'), 0, 0, axis_index_groups=same_core...  10.4 us
    pallas_call x1, Pallas kernels, attend(): pl.pallas_call(functools.partial(attend_kernel, calls=calls, rows=rows, s...  8.6 us
    pallas_call x1, Pallas kernels, project_first(): pl.pallas_call(project_first_kernel, in_specs=[vmem, pl.BlockSpec(memory_...  6.01 us
    all_to_all x1, starting transfers between devices, local(): lax.all_to_all(terms, ('group', 'seq'), 0, 0, axis_index_groups=same_core...  4.96 us
    unnamed x18, local copies, waits for them, and re-layouts  4.92 us
  transfers between devices with their start and end apart: 13, of which 8 were waited for; matrix products, arithmetic and copies ran while one was open for 0% of the time, Pallas kernels for 23%

profile of v5, /device:TPU:16, one launch (start us, length us, event | category | flops | bytes accessed | tf_op | source)
XLA Modules:
  0.0 109.7 jit_solution(7998392498898447905)
XLA Ops:
  0.7 4.9 %own_rows.1.x_ref.refs_0_ = bf16[80,5120]{1,0:T(8,128)(2,1)} custom-call(s32[1]{0:T(128)S(6)} %copy.13.step_ref, bf16[80,5120]{1,0:T(8,128)(2,1)} %bitcast.27, f32[2,5120]{1,0:T(2,128)} %mod_any.1, bf16[64,5120]{1,0:T(8,128)(2,1)} %bitcast.29, bf16[64,80]{1,0:T(8,128)(2,1)} %bitcast.32, bf16[80,5120]{1,0:T(8,128)(2,1)} %bitcast.28, ...), custom_call_target="tpu_custom_call" | custom-call | flops 200000000 | bytes 5000000 | tf_op jit(solution)/shard_map/own_rows/pallas_call | solution.py:73
  5.7 2.0 %collective-permute-start.1 = (bf16[80,5120]{1,0:T(8,128)(2,1)}, bf16[80,5120]{1,0:T(8,128)(2,1)S(1)}, u32[]{:S(2)}, u32[]{:S(2)}) collective-permute-start(bf16[80,5120]{1,0:T(8,128)(2,1)} %own_rows.1.x_ref.refs_0_), channel_id=1, source_target_pairs={{0,2},{1,15},{2,4},{3,1},{4,6},{5,3},{6,8},{7,5},{8,10},{9,7},{10,... | collective-permute-start | bytes 2457608 | tf_op jit(solution)/shard_map/ppermute | solution.py:312
  7.7 6.0 %project_first.1 = (bf16[2,80,128]{2,1,0:T(8,128)(2,1)}, bf16[4,80,128]{2,1,0:T(8,128)(2,1)}) custom-call(bf16[80,5120]{1,0:T(8,128)(2,1)} %own_rows.1.x_ref.refs_0_, bf16[3,5120,256]{2,1,0:T(8,128)(2,1)} %bitcast.19), custom_call_target="tpu_custom_call" | custom-call | flops 629145600 | bytes 7864320 | tf_op jit(solution)/shard_map/project_first/pallas_call | solution.py:105
  13.7 4.1 %collective-permute-start = (bf16[80,5120]{1,0:T(8,128)(2,1)S(1)}, bf16[80,5120]{1,0:T(8,128)(2,1)S(1)}, u32[]{:S(2)}, u32[]{:S(2)}) collective-permute-start(bf16[80,5120]{1,0:T(8,128)(2,1)S(1)} %copy-done.1), channel_id=1, source_target_pairs={{0,14},{1,3},{2,0},{3,5},{4,2},{5,7},{6,4},{7,9},{8,6},{9,11},{10,... | collective-permute-start | bytes 2457608 | tf_op jit(solution)/shard_map/ppermute | solution.py:312
  17.7 4.8 %collective-permute-done.1.refs_1_ = bf16[80,5120]{1,0:T(8,128)(2,1)S(1)} collective-permute-done((bf16[80,5120]{1,0:T(8,128)(2,1)}, bf16[80,5120]{1,0:T(8,128)(2,1)S(1)}, u32[]{:S(2)}, u32[]{:S(2)}) %collective-permute-start.1) | collective-permute-done | bytes 819232 | tf_op jit(solution)/shard_map/ppermute | solution.py:312
  24.0 3.2 %copy-done = bf16[1,5120,3,256]{3,1,2,0:T(8,128)(2,1)S(1)} copy-done((bf16[1,5120,3,256]{3,1,2,0:T(8,128)(2,1)S(1)}, bf16[1,5120,3,256]{3,1,2,0:T(8,128)(2,1)}, u32[]{:S(2)}) %copy-start) | copy-done | bytes 7864344
  27.2 0.9 copy-done.2
  28.9 6.1 %project_rows.4 = (bf16[4,160,128]{2,1,0:T(8,128)(2,1)S(1)}, bf16[8,160,128]{2,1,0:T(8,128)(2,1)S(1)}) custom-call(bf16[80,5120]{1,0:T(8,128)(2,1)S(1)} %copy-done.1, bf16[80,5120]{1,0:T(8,128)(2,1)S(1)} %collective-permute-done.1.refs_1_, bf16[3,5120,256]{2,1,0:T(8,128)(2,1)S(1)} %bitcast.20, bf16[3,5120,256]{2,1,0:T(8,128)(2,1)} %collective-permute-done.2.refs_3_, ...), custom_call_target="tpu_custom_call" | custom-call | flops 2516582400 | bytes 15728640 | tf_op jit(solution)/shard_map/project_rows/pallas_call | solution.py:192
  35.1 3.7 %collective-permute-start.3 = (bf16[80,5120]{1,0:T(8,128)(2,1)S(1)}, bf16[80,5120]{1,0:T(8,128)(2,1)S(1)}, u32[]{:S(2)}, u32[]{:S(2)}) collective-permute-start(bf16[80,5120]{1,0:T(8,128)(2,1)S(1)} %collective-permute-done.refs_0_), channel_id=1, source_target_pairs={{0,14},{1,3},{2,0},{3,5},{4,2},{5,7},{6,4},{7,9},{8,6},{9,11},{10,... | collective-permute-start | bytes 2457608 | tf_op jit(solution)/shard_map/ppermute | solution.py:312
  38.8 0.8 collective-permute-done.4.refs_1_
  39.7 2.2 %collective-permute-start.5 = (bf16[8,160,128]{2,1,0:T(8,128)(2,1)S(1)}, bf16[8,160,128]{2,1,0:T(8,128)(2,1)S(1)}, u32[]{:S(2)}, u32[]{:S(2)}) collective-permute-start(bf16[8,160,128]{2,1,0:T(8,128)(2,1)S(1)} %get-tuple-element.51.refs_3_), channel_id=1, source_target_pairs={{0,1},{1,0},{2,3},{3,2},{4,5},{5,4},{6,7},{7,6},{8,9},{9,8},{10,11... | collective-permute-start | bytes 983048 | tf_op jit(solution)/shard_map/ppermute | solution.py:315
  41.9 6.7 %project_rows.5 = (bf16[4,160,128]{2,1,0:T(8,128)(2,1)S(1)}, bf16[8,160,128]{2,1,0:T(8,128)(2,1)S(1)}) custom-call(bf16[80,5120]{1,0:T(8,128)(2,1)S(1)} %collective-permute-done.refs_0_, bf16[80,5120]{1,0:T(8,128)(2,1)S(1)} %collective-permute-done.4.refs_1_, bf16[3,5120,256]{2,1,0:T(8,128)(2,1)S(1)} %bitcast.21, ...), custom_call_target="tpu_custom_call" | custom-call | flops 2516582400 | bytes 15728640 | tf_op jit(solution)/shard_map/project_rows/pallas_call | solution.py:192
  48.7 6.4 %collective-permute-done.3.refs_0_ = bf16[80,5120]{1,0:T(8,128)(2,1)S(1)} collective-permute-done((bf16[80,5120]{1,0:T(8,128)(2,1)S(1)}, bf16[80,5120]{1,0:T(8,128)(2,1)S(1)}, u32[]{:S(2)}, u32[]{:S(2)}) %collective-permute-start.3) | collective-permute-done | bytes 819232 | tf_op jit(solution)/shard_map/ppermute | solution.py:312
  55.0 3.9 %collective-permute-start.6 = (bf16[80,5120]{1,0:T(8,128)(2,1)S(1)}, bf16[80,5120]{1,0:T(8,128)(2,1)S(1)}, u32[]{:S(2)}, u32[]{:S(2)}) collective-permute-start(bf16[80,5120]{1,0:T(8,128)(2,1)S(1)} %collective-permute-done.3.refs_0_), channel_id=1, source_target_pairs={{0,14},{1,3},{2,0},{3,5},{4,2},{5,7},{6,4},{7,9},{8,6},{9,11},{10,... | collective-permute-start | bytes 2457608 | tf_op jit(solution)/shard_map/ppermute | solution.py:312
  58.9 1.4 %collective-permute-done.7.refs_1_ = bf16[80,5120]{1,0:T(8,128)(2,1)S(1)} collective-permute-done((bf16[80,5120]{1,0:T(8,128)(2,1)S(1)}, bf16[80,5120]{1,0:T(8,128)(2,1)S(1)}, u32[]{:S(2)}, u32[]{:S(2)}) %collective-permute-start.7) | collective-permute-done | bytes 819232 | tf_op jit(solution)/shard_map/ppermute | solution.py:312
  60.3 1.0 collective-permute-start.8
  61.3 6.8 %project_rows.6 = (bf16[4,160,128]{2,1,0:T(8,128)(2,1)S(1)}, bf16[8,160,128]{2,1,0:T(8,128)(2,1)S(1)}, bf16[6,5120,256]{2,1,0:T(8,128)(2,1)S(1)}) custom-call(bf16[80,5120]{1,0:T(8,128)(2,1)S(1)} %collective-permute-done.3.refs_0_, bf16[80,5120]{1,0:T(8,128)(2,1)S(1)} %collective-permute-done.7.refs_1_, bf16[3,5120,256]{2,1,0:T(8,128)(2,1)S(1)} %bitcast.24, ...), custom_call_target="tpu_custom_call" | custom-call | flops 2516582400 | bytes 15728640 | tf_op jit(solution)/shard_map/project_rows/pallas_call | solution.py:192
  68.1 7.7 %collective-permute-done.6.refs_0_ = bf16[80,5120]{1,0:T(8,128)(2,1)S(1)} collective-permute-done((bf16[80,5120]{1,0:T(8,128)(2,1)S(1)}, bf16[80,5120]{1,0:T(8,128)(2,1)S(1)}, u32[]{:S(2)}, u32[]{:S(2)}) %collective-permute-start.6) | collective-permute-done | bytes 819232 | tf_op jit(solution)/shard_map/ppermute | solution.py:312
  75.8 4.1 %collective-permute-done.10.refs_1_ = bf16[80,5120]{1,0:T(8,128)(2,1)S(1)} collective-permute-done((bf16[80,5120]{1,0:T(8,128)(2,1)S(1)}, bf16[80,5120]{1,0:T(8,128)(2,1)S(1)}, u32[]{:S(2)}, u32[]{:S(2)}) %collective-permute-start.10) | collective-permute-done | bytes 819232 | tf_op jit(solution)/shard_map/ppermute | solution.py:312
  80.0 2.7 %project_rows.7 = (bf16[4,320,128]{2,1,0:T(8,128)(2,1)S(1)}, bf16[8,320,128]{2,1,0:T(8,128)(2,1)S(1)}) custom-call(bf16[80,5120]{1,0:T(8,128)(2,1)S(1)} %collective-permute-done.6.refs_0_, bf16[80,5120]{1,0:T(8,128)(2,1)S(1)} %collective-permute-done.10.refs_1_, bf16[6,5120,256]{2,1,0:T(8,128)(2,1)S(1)} %get-tuple-element.66.refs_2_, ...), custom_call_target="tpu_custom_call" | custom-call | flops 2516582400 | bytes 1638400 | tf_op jit(solution)/shard_map/project_rows/pallas_call | solution.py:192
  83.0 2.1 %collective-permute-done.11.refs_8_ = bf16[8,320,128]{2,1,0:T(8,128)(2,1)S(1)} collective-permute-done((bf16[8,320,128]{2,1,0:T(8,128)(2,1)S(1)}, bf16[8,320,128]{2,1,0:T(8,128)(2,1)S(1)}, u32[]{:S(2)}, u32[]{:S(2)}) %collective-permute-start.11) | collective-permute-done | bytes 655392 | tf_op jit(solution)/shard_map/ppermute | solution.py:315
  85.1 8.6 %attend.1 = f32[2,8,32,80]{3,2,1,0:T(8,128)} custom-call(s32[8]{0:T(128)S(1)} %get-tuple-element.54.place_ref, f32[1,1280]{1,0:T(1,128)S(1)} %reshape.56.bias_ref, bf16[2,64,128]{2,1,0:T(8,128)(2,1)S(1)} %bitcast.26, bf16[2,64,128]{2,1,0:T(8,128)(2,1)S(1)} %collective-permute-done.9.hb_ref, bf16[4,160,128]{2,1,0:T(8,128)(2,1)S(1)} %get-tuple-element.63.refs_0_, ...), custom_call_target="tpu_custom_call" | custom-call | flops 1677721600 | bytes 10000000 | tf_op jit(solution)/shard_map/attend/pallas_call | solution.py:262
  93.7 5.0 %all-to-all-start = ((f32[16,32,80]{2,1,0:T(8,128)}), f32[16,32,80]{2,1,0:T(8,128)S(1)}, u32[]{:S(2)}, u32[]{:S(2)}) async-start(f32[16,32,80]{2,1,0:T(8,128)} %bitcast.12), calls=%async_computation | async-start | bytes 524288 | tf_op jit(solution)/shard_map/all_to_all | solution.py:389
  98.7 10.4 %all-to-all-done = f32[16,32,80]{2,1,0:T(8,128)S(1)} async-done(((f32[16,32,80]{2,1,0:T(8,128)}), f32[16,32,80]{2,1,0:T(8,128)S(1)}, u32[]{:S(2)}, u32[]{:S(2)}) %all-to-all-start) | async-done | bytes 163872 | tf_op jit(solution)/shard_map/all_to_all | solution.py:389
  (35 shorter events, 2.6 us)
Async XLA Ops:
  0.0 23.8 %copy-start.5 = (s32[8]{0:T(128)S(1)}, s32[8]{0:T(128)}, u32[]{:S(2)}) copy-start(s32[8]{0:T(128)} %constant.62.clone) | copy-start | bytes 100
  0.0 23.8 %copy-start.6 = (s32[8]{0:T(128)S(1)}, s32[8]{0:T(128)}, u32[]{:S(2)}) copy-start(s32[8]{0:T(128)} %constant.72) | copy-start | bytes 100
  5.5 8.1 %copy-start.1 = (bf16[80,5120]{1,0:T(8,128)(2,1)S(1)}, bf16[80,5120]{1,0:T(8,128)(2,1)}, u32[]{:S(2)}) copy-start(bf16[80,5120]{1,0:T(8,128)(2,1)} %own_rows.1.x_ref.refs_0_) | copy-start | bytes 2457604
  5.6 18.4 %collective-permute-start.2 = (bf16[3,5120,256]{2,1,0:T(8,128)(2,1)}, bf16[3,5120,256]{2,1,0:T(8,128)(2,1)}, u32[]{:S(2)}, u32[]{:S(2)}) collective-permute-start(bf16[3,5120,256]{2,1,0:T(8,128)(2,1)} %bitcast.18), channel_id=1, source_target_pairs={{0,1},{1,0},{2,3},{3,2},{4,5},{5,4},{6,7},{7,6},{8,9},{9,8},{10,11... | collective-permute-start | bytes 23592968 | tf_op jit(solution)/shard_map/ppermute | solution.py:315
  5.7 16.9 %collective-permute-start.1 = (bf16[80,5120]{1,0:T(8,128)(2,1)}, bf16[80,5120]{1,0:T(8,128)(2,1)S(1)}, u32[]{:S(2)}, u32[]{:S(2)}) collective-permute-start(bf16[80,5120]{1,0:T(8,128)(2,1)} %own_rows.1.x_ref.refs_0_), channel_id=1, source_target_pairs={{0,2},{1,15},{2,4},{3,1},{4,6},{5,3},{6,8},{7,5},{8,10},{9,7},{10,... | collective-permute-start | bytes 2457608 | tf_op jit(solution)/shard_map/ppermute | solution.py:312
  13.7 21.4 %collective-permute-start = (bf16[80,5120]{1,0:T(8,128)(2,1)S(1)}, bf16[80,5120]{1,0:T(8,128)(2,1)S(1)}, u32[]{:S(2)}, u32[]{:S(2)}) collective-permute-start(bf16[80,5120]{1,0:T(8,128)(2,1)S(1)} %copy-done.1), channel_id=1, source_target_pairs={{0,14},{1,3},{2,0},{3,5},{4,2},{5,7},{6,4},{7,9},{8,6},{9,11},{10,... | collective-permute-start | bytes 2457608 | tf_op jit(solution)/shard_map/ppermute | solution.py:312
  22.5 17.1 %collective-permute-start.4 = (bf16[80,5120]{1,0:T(8,128)(2,1)S(1)}, bf16[80,5120]{1,0:T(8,128)(2,1)S(1)}, u32[]{:S(2)}, u32[]{:S(2)}) collective-permute-start(bf16[80,5120]{1,0:T(8,128)(2,1)S(1)} %collective-permute-done.1.refs_1_), channel_id=1, source_target_pairs={{0,2},{1,15},{2,4},{3,1},{4,6},{5,3},{6,8},{7,5},{8,10},{9,7},{10,... | collective-permute-start | bytes 2457608 | tf_op jit(solution)/shard_map/ppermute | solution.py:312
  24.0 3.2 %copy-start = (bf16[1,5120,3,256]{3,1,2,0:T(8,128)(2,1)S(1)}, bf16[1,5120,3,256]{3,1,2,0:T(8,128)(2,1)}, u32[]{:S(2)}) copy-start(bf16[1,5120,3,256]{3,1,2,0:T(8,128)(2,1)} %param.18) | copy-start | bytes 23592964
  27.2 0.9 copy-start.2
  28.1 0.8 copy-start.3
  35.1 26.2 %slice-start = ((s8[7864320]{0:T(1024)(128)(4,1)}), s8[4194304]{0:T(1024)(128)(4,1)S(1)}, s32[]{:S(2)}) async-start(s8[7864320]{0:T(1024)(128)(4,1)} %bitcast.22), calls=%async_computation.1 | async-start | bytes 8388608
  35.1 26.2 %copy-start.4 = (bf16[1,2,128,64]{2,3,1,0:T(8,128)(2,1)S(1)}, bf16[1,2,128,64]{2,3,1,0:T(8,128)(2,1)}, u32[]{:S(2)}) copy-start(bf16[1,2,128,64]{2,3,1,0:T(8,128)(2,1)} %param.19) | copy-start | bytes 98308
  35.1 26.2 %slice-start.1 = ((s8[7864320]{0:T(1024)(128)(4,1)}), s8[3670016]{0:T(1024)(128)(4,1)S(1)}, s32[]{:S(2)}) async-start(s8[7864320]{0:T(1024)(128)(4,1)} %bitcast.22), calls=%async_computation.2 | async-start | bytes 7340032
  35.1 20.0 %collective-permute-start.3 = (bf16[80,5120]{1,0:T(8,128)(2,1)S(1)}, bf16[80,5120]{1,0:T(8,128)(2,1)S(1)}, u32[]{:S(2)}, u32[]{:S(2)}) collective-permute-start(bf16[80,5120]{1,0:T(8,128)(2,1)S(1)} %collective-permute-done.refs_0_), channel_id=1, source_target_pairs={{0,14},{1,3},{2,0},{3,5},{4,2},{5,7},{6,4},{7,9},{8,6},{9,11},{10,... | collective-permute-start | bytes 2457608 | tf_op jit(solution)/shard_map/ppermute | solution.py:312
  39.7 20.6 %collective-permute-start.7 = (bf16[80,5120]{1,0:T(8,128)(2,1)S(1)}, bf16[80,5120]{1,0:T(8,128)(2,1)S(1)}, u32[]{:S(2)}, u32[]{:S(2)}) collective-permute-start(bf16[80,5120]{1,0:T(8,128)(2,1)S(1)} %collective-permute-done.4.refs_1_), channel_id=1, source_target_pairs={{0,2},{1,15},{2,4},{3,1},{4,6},{5,3},{6,8},{7,5},{8,10},{9,7},{10,... | collective-permute-start | bytes 2457608 | tf_op jit(solution)/shard_map/ppermute | solution.py:312
  39.7 9.0 %collective-permute-start.5 = (bf16[8,160,128]{2,1,0:T(8,128)(2,1)S(1)}, bf16[8,160,128]{2,1,0:T(8,128)(2,1)S(1)}, u32[]{:S(2)}, u32[]{:S(2)}) collective-permute-start(bf16[8,160,128]{2,1,0:T(8,128)(2,1)S(1)} %get-tuple-element.51.refs_3_), channel_id=1, source_target_pairs={{0,1},{1,0},{2,3},{3,2},{4,5},{5,4},{6,7},{7,6},{8,9},{9,8},{10,11... | collective-permute-start | bytes 983048 | tf_op jit(solution)/shard_map/ppermute | solution.py:315
  55.0 20.8 %collective-permute-start.6 = (bf16[80,5120]{1,0:T(8,128)(2,1)S(1)}, bf16[80,5120]{1,0:T(8,128)(2,1)S(1)}, u32[]{:S(2)}, u32[]{:S(2)}) collective-permute-start(bf16[80,5120]{1,0:T(8,128)(2,1)S(1)} %collective-permute-done.3.refs_0_), channel_id=1, source_target_pairs={{0,14},{1,3},{2,0},{3,5},{4,2},{5,7},{6,4},{7,9},{8,6},{9,11},{10,... | collective-permute-start | bytes 2457608 | tf_op jit(solution)/shard_map/ppermute | solution.py:312
  60.3 19.7 %collective-permute-start.10 = (bf16[80,5120]{1,0:T(8,128)(2,1)S(1)}, bf16[80,5120]{1,0:T(8,128)(2,1)S(1)}, u32[]{:S(2)}, u32[]{:S(2)}) collective-permute-start(bf16[80,5120]{1,0:T(8,128)(2,1)S(1)} %collective-permute-done.7.refs_1_), channel_id=1, source_target_pairs={{0,2},{1,15},{2,4},{3,1},{4,6},{5,3},{6,8},{7,5},{8,10},{9,7},{10,... | collective-permute-start | bytes 2457608 | tf_op jit(solution)/shard_map/ppermute | solution.py:312
  60.3 7.8 %collective-permute-start.8 = (bf16[8,160,128]{2,1,0:T(8,128)(2,1)S(1)}, bf16[8,160,128]{2,1,0:T(8,128)(2,1)S(1)}, u32[]{:S(2)}, u32[]{:S(2)}) collective-permute-start(bf16[8,160,128]{2,1,0:T(8,128)(2,1)S(1)} %get-tuple-element.60.refs_4_), channel_id=1, source_target_pairs={{0,1},{1,0},{2,3},{3,2},{4,5},{5,4},{6,7},{7,6},{8,9},{9,8},{10,11... | collective-permute-start | bytes 983048 | tf_op jit(solution)/shard_map/ppermute | solution.py:315
  61.3 6.8 %collective-permute-start.9 = (bf16[2,64,128]{2,1,0:T(8,128)(2,1)S(1)}, bf16[2,64,128]{2,1,0:T(8,128)(2,1)S(1)}, u32[]{:S(2)}, u32[]{:S(2)}) collective-permute-start(bf16[2,64,128]{2,1,0:T(8,128)(2,1)S(1)} %bitcast.25), channel_id=1, source_target_pairs={{0,1},{1,0},{2,3},{3,2},{4,5},{5,4},{6,7},{7,6},{8,9},{9,8},{10,11... | collective-permute-start | bytes 98312 | tf_op jit(solution)/shard_map/ppermute | solution.py:315
  82.7 2.4 %collective-permute-start.11 = (bf16[8,320,128]{2,1,0:T(8,128)(2,1)S(1)}, bf16[8,320,128]{2,1,0:T(8,128)(2,1)S(1)}, u32[]{:S(2)}, u32[]{:S(2)}) collective-permute-start(bf16[8,320,128]{2,1,0:T(8,128)(2,1)S(1)} %get-tuple-element.70.refs_5_), channel_id=1, source_target_pairs={{0,1},{1,0},{2,3},{3,2},{4,5},{5,4},{6,7},{7,6},{8,9},{9,8},{10,11... | collective-permute-start | bytes 1966088 | tf_op jit(solution)/shard_map/ppermute | solution.py:315
  93.7 15.4 %all-to-all-start = ((f32[16,32,80]{2,1,0:T(8,128)}), f32[16,32,80]{2,1,0:T(8,128)S(1)}, u32[]{:S(2)}, u32[]{:S(2)}) async-start(f32[16,32,80]{2,1,0:T(8,128)} %bitcast.12), calls=%async_computation | async-start | bytes 524288 | tf_op jit(solution)/shard_map/all_to_all | solution.py:389

commit v6 on v3

--- a/solution.py
+++ b/solution.py
@@ -99,7 +99,7 @@
                 kv_ref[2 * (n - 1) + sub] = part
 
 
-def project_first(x, w, head_size):
+def project_first(x, w, head_size, weight=1):
     rows, width = x.shape
     vmem = pl.BlockSpec(memory_space=pltpu.VMEM)
     return pl.pallas_call(
@@ -113,7 +113,7 @@
         scratch_shapes=[pltpu.VMEM(w.shape, w.dtype), pltpu.SemaphoreType.DMA((3,))],
         compiler_params=pltpu.CompilerParams(vmem_limit_bytes=58 * MIB),
         cost_estimate=pl.CostEstimate(
-            flops=6 * rows * width * w.shape[2], bytes_accessed=2 * w.size, transcendentals=0
+            flops=weight * 6 * rows * width * w.shape[2], bytes_accessed=weight * 2 * w.size, transcendentals=0
         ),
         name="project_first",
     )(x, w)
@@ -124,7 +124,7 @@
     x_refs = [refs.pop(0) for _ in sizes]
     w_any = [refs.pop(0) for _ in range(2 if fetch else 1)]
     q_before, kv_before = (refs.pop(0), refs.pop(0)) if before else (None, None)
-    q_done, kv_done = (refs.pop(0), refs.pop(0)) if ready else (None, None)
+    done = [(refs.pop(0), refs.pop(0)) for _ in range(ready)]
     q_ref, kv_ref = refs.pop(0), refs.pop(0)
     w_ref = refs.pop(0) if fetch else w_any[0]
     x_buf = refs.pop(0)
@@ -156,7 +156,7 @@
             if n + 3 < 6:
                 copies[n + 3].start()
         pair, kind = n // 3, n % 3
-        skip = sizes[0] if ready and pair == 0 else 0
+        skip = sum(sizes[:ready]) if pair == 0 else 0
         here = pl.ds(before + skip, sum(sizes) - skip)
         value = dot(x_buf[pl.ds(skip, sum(sizes) - skip)], w_ref[n], NN).astype(jnp.bfloat16)
         for sub in range(2):
@@ -165,9 +165,9 @@
                 q_ref[2 * pair + sub, here] = part
             else:
                 kv_ref[4 * pair + 2 * (kind - 1) + sub, here] = part
-    if ready:
-        q_ref[0:2, pl.ds(0, sizes[0])] = q_done[...]
-        kv_ref[0:4, pl.ds(0, sizes[0])] = kv_done[...]
+    for i, (q_done, kv_done) in enumerate(done):
+        q_ref[0:2, pl.ds(sum(sizes[:i]), sizes[i])] = q_done[...]
+        kv_ref[0:4, pl.ds(sum(sizes[:i]), sizes[i])] = kv_done[...]
 
 
 def project(xs, weights, head_size, keep=False, earlier=(), ready=()):
@@ -191,7 +191,7 @@
         scratch.append(pltpu.SemaphoreType.DMA((6 + len(xs),)))
     return pl.pallas_call(
         functools.partial(
-            project_kernel, sizes=sizes, fetch=fetch, keep=keep, before=before, ready=bool(ready)
+            project_kernel, sizes=sizes, fetch=fetch, keep=keep, before=before, ready=len(ready) // 2
         ),
         in_specs=[pl.BlockSpec(memory_space=pl.ANY) if fetch else vmem] * (len(xs) + len(weights))
         + [vmem] * (len(earlier) + len(ready)),
@@ -314,10 +314,7 @@
     def other_core(block):
         return lax.ppermute(block, "seq", [(i, i ^ 1) for i in range(seq_count)])
 
-    half_way = chips // 2
-    apart = [0, -1]
-    for k in range(1, half_way):
-        apart += [k, -k - 1]
+    apart = [0, -1, 1, -2, 2, -3, 3, -4]
     apart = jnp.asarray(apart, jnp.int32)
 
     def places(core):
@@ -343,39 +340,32 @@
 
     up, down = [normed], [normed]
     up.append(hop(up[-1], 1))
-    fetched, begun, _ = lax.optimization_barrier((wa, ha, normed))
+    fetched, _ = lax.optimization_barrier((wa, normed))
     wb = other_core(fetched)
-    hb = other_core(begun)
     later, *ready = lax.optimization_barrier((normed, *project_first(normed, wa, head_size)))
     down.append(hop(later, -1))
     bias = jnp.concatenate([bias_of(core_at), bias_of(1 - core_at)]).reshape(1, -1)
     up.append(hop(up[-1], 1))
 
     place = places(core_at)
-    qs, owns, fars = [], [], []
-    weights, earlier = [wa, wb], ()
-    for k in range(half_way):
-        nearer, further = down[k], up[k + 1]
-        if 0 < k < half_way - 1:
-            nearer, down[k + 1] = lax.optimization_barrier((nearer, down[k + 1]))
-        if k + 2 < half_way:
-            down.append(hop(down[k + 1], -1))
-        q, kv, *kept = project(
-            [nearer, further], weights, head_size, keep=k == half_way - 2, earlier=earlier, ready=() if k else ready
-        )
-        weights = kept or weights
-        if k + 2 <= half_way:
-            up[k + 2], q, kv, fars, bias, place, hb = lax.optimization_barrier(
-                (up[k + 2], q, kv, fars, bias, place, hb)
-            )
-        if k + 3 <= half_way:
-            up.append(hop(up[k + 2], 1))
-        if k == half_way - 2:
-            earlier = (q, kv)
-        else:
-            qs.append(q)
-            owns.append(kv)
-            fars.append(other_core(kv))
+    more = project_first(up[1], wa, head_size, weight=3)
+    down[1], bias, place, *more = lax.optimization_barrier((down[1], bias, place, *more))
+    down.append(hop(down[1], -1))
+    up.append(hop(up[2], 1))
+
+    q, kv = project([normed, up[1], down[1], up[2]], [wa, wb], head_size, ready=[*ready, *more])
+    begun, kv = lax.optimization_barrier((ha, kv))
+    hb = other_core(begun)
+    down[2], q, kv = lax.optimization_barrier((down[2], q, kv))
+    down.append(hop(down[2], -1))
+    up.append(hop(up[3], 1))
+    qs, owns, fars = [q], [kv], [other_core(kv)]
+    *earlier, kept = project([down[2], up[3]], [wa, wb], head_size, keep=True)
+    down[3], earlier, fars, hb = lax.optimization_barrier((down[3], earlier, fars, hb))
+    q, kv = project([down[3], up[4]], [kept], head_size, earlier=earlier)
+    qs.append(q)
+    owns.append(kv)
+    fars.append(other_core(kv))
     terms = attend(place, bias, ha, hb, qs, owns, fars, rows, groups, scale)
 
     half = terms.shape[2]

time: 116 us -> 110 us (0.948)
  starting transfers between devices: 25.5 us -> 20 us
  waiting for transfers between devices: 40.5 us -> 37.3 us
  Pallas kernels: 41.8 us -> 43.6 us
    pallas_call x1 -> x2, Pallas kernels: 6 us -> 12 us  [project_first(): pl.pallas_call(project_first_kernel, in_specs=[vmem, pl.BlockSpec(memory_...]
    pallas_call x4 -> x3, Pallas kernels: 22.3 us -> 18.5 us  [project(): pl.pallas_call(functools.partial(project_kernel, sizes=sizes, fetch=fetch...]
    ppermute x7, waiting for transfers between devices: 28 us -> 24.7 us  [hop(): return lax.ppermute(block, 'seq', route)]
    ppermute x5 -> x4, starting transfers between devices: 4.43 us -> 1.48 us  [other_core(): return lax.ppermute(block, 'seq', [(i, i ^ 1) for i in range(seq_count)])]
    all_to_all x1, starting transfers between devices: 7.2 us -> 4.59 us  [local(): lax.all_to_all(terms, ('group', 'seq'), 0, 0, axis_index_groups=same_core...]
    unnamed x18 -> x24, local copies, waits for them, and re-layouts: 4.92 us -> 6.07 us
  transfers between devices with their start and end apart: 13 -> 12, of which waited for: 6 -> 7; matrix products, arithmetic and copies ran while one was open for 0% -> 0% of each run, Pallas kernels for 22% -> 25%
where the time goes in v6:
time: 110 us; the launch traced here: 109 us
  Pallas kernels  43.6 us (40%)
  waiting for transfers between devices  37.3 us (34%)
  starting transfers between devices  20 us (18%)
  local copies, waits for them, and re-layouts  6.15 us (6%)
  between operations  1.55 us (1%)
    ppermute x7, waiting for transfers between devices, hop(): return lax.ppermute(block, 'seq', route)  24.7 us
    pallas_call x3, Pallas kernels, project(): pl.pallas_call(functools.partial(project_kernel, sizes=sizes, fetch=fetch...  18.5 us
    ppermute x7, starting transfers between devices, hop(): return lax.ppermute(block, 'seq', route)  13.9 us
    pallas_call x2, Pallas kernels, project_first(): pl.pallas_call(project_first_kernel, in_specs=[vmem, pl.BlockSpec(memory_...  12 us
    all_to_all x1, waiting for transfers between devices, local(): lax.all_to_all(terms, ('group', 'seq'), 0, 0, axis_index_groups=same_core...  10.5 us
    pallas_call x1, Pallas kernels, attend(): pl.pallas_call(functools.partial(attend_kernel, calls=calls, rows=rows, s...  8.22 us
    unnamed x24, local copies, waits for them, and re-layouts  6.07 us
    pallas_call x1, Pallas kernels, own_rows(): pl.pallas_call(functools.partial(own_rows_kernel, levels=levels, cuts=cut...  4.85 us
  transfers between devices with their start and end apart: 12, of which 7 were waited for; matrix products, arithmetic and copies ran while one was open for 0% of the time, Pallas kernels for 25%

profile of v6, /device:TPU:16, one launch (start us, length us, event | category | flops | bytes accessed | tf_op | source)
XLA Modules:
  0.0 109.3 jit_solution(16526146751313683395)
XLA Ops:
  0.7 4.9 %own_rows.1.x_ref.refs_0_ = bf16[80,5120]{1,0:T(8,128)(2,1)} custom-call(s32[1]{0:T(128)S(6)} %copy.13.step_ref, bf16[80,5120]{1,0:T(8,128)(2,1)} %bitcast.25, f32[2,5120]{1,0:T(2,128)} %mod_any.1, bf16[64,5120]{1,0:T(8,128)(2,1)} %bitcast.27, bf16[64,80]{1,0:T(8,128)(2,1)} %bitcast.30, bf16[80,5120]{1,0:T(8,128)(2,1)} %bitcast.26, ...), custom_call_target="tpu_custom_call" | custom-call | flops 200000000 | bytes 5000000 | tf_op jit(solution)/shard_map/own_rows/pallas_call | solution.py:73
  5.7 2.0 %collective-permute-start.1 = (bf16[80,5120]{1,0:T(8,128)(2,1)}, bf16[80,5120]{1,0:T(8,128)(2,1)S(1)}, u32[]{:S(2)}, u32[]{:S(2)}) collective-permute-start(bf16[80,5120]{1,0:T(8,128)(2,1)} %own_rows.1.x_ref.refs_0_), channel_id=1, source_target_pairs={{0,2},{1,15},{2,4},{3,1},{4,6},{5,3},{6,8},{7,5},{8,10},{9,7},{10,... | collective-permute-start | bytes 2457608 | tf_op jit(solution)/shard_map/ppermute | solution.py:312
  7.7 6.0 %project_first.2 = (bf16[2,80,128]{2,1,0:T(8,128)(2,1)}, bf16[4,80,128]{2,1,0:T(8,128)(2,1)}) custom-call(bf16[80,5120]{1,0:T(8,128)(2,1)} %own_rows.1.x_ref.refs_0_, bf16[3,5120,256]{2,1,0:T(8,128)(2,1)} %bitcast.19), custom_call_target="tpu_custom_call" | custom-call | flops 629145600 | bytes 7864320 | tf_op jit(solution)/shard_map/project_first/pallas_call | solution.py:105
  13.7 4.1 %collective-permute-start = (bf16[80,5120]{1,0:T(8,128)(2,1)S(1)}, bf16[80,5120]{1,0:T(8,128)(2,1)S(1)}, u32[]{:S(2)}, u32[]{:S(2)}) collective-permute-start(bf16[80,5120]{1,0:T(8,128)(2,1)S(1)} %copy-done.2), channel_id=1, source_target_pairs={{0,14},{1,3},{2,0},{3,5},{4,2},{5,7},{6,4},{7,9},{8,6},{9,11},{10,... | collective-permute-start | bytes 2457608 | tf_op jit(solution)/shard_map/ppermute | solution.py:312
  17.8 4.8 %collective-permute-done.1.x_ref.refs_1_ = bf16[80,5120]{1,0:T(8,128)(2,1)S(1)} collective-permute-done((bf16[80,5120]{1,0:T(8,128)(2,1)}, bf16[80,5120]{1,0:T(8,128)(2,1)S(1)}, u32[]{:S(2)}, u32[]{:S(2)}) %collective-permute-start.1) | collective-permute-done | bytes 819232 | tf_op jit(solution)/shard_map/ppermute | solution.py:312
  24.0 6.0 %project_first.3 = (bf16[2,80,128]{2,1,0:T(8,128)(2,1)}, bf16[4,80,128]{2,1,0:T(8,128)(2,1)}) custom-call(bf16[80,5120]{1,0:T(8,128)(2,1)} %copy-done.3, bf16[3,5120,256]{2,1,0:T(8,128)(2,1)} %bitcast.20), custom_call_target="tpu_custom_call" | custom-call | flops 1887436800 | bytes 23592960 | tf_op jit(solution)/shard_map/project_first/pallas_call | solution.py:105
  30.0 2.5 %collective-permute-done.refs_2_ = bf16[80,5120]{1,0:T(8,128)(2,1)S(1)} collective-permute-done((bf16[80,5120]{1,0:T(8,128)(2,1)S(1)}, bf16[80,5120]{1,0:T(8,128)(2,1)S(1)}, u32[]{:S(2)}, u32[]{:S(2)}) %collective-permute-start) | collective-permute-done | bytes 819232 | tf_op jit(solution)/shard_map/ppermute | solution.py:312
  32.5 3.7 %collective-permute-start.2 = (bf16[80,5120]{1,0:T(8,128)(2,1)S(1)}, bf16[80,5120]{1,0:T(8,128)(2,1)S(1)}, u32[]{:S(2)}, u32[]{:S(2)}) collective-permute-start(bf16[80,5120]{1,0:T(8,128)(2,1)S(1)} %collective-permute-done.refs_2_), channel_id=1, source_target_pairs={{0,14},{1,3},{2,0},{3,5},{4,2},{5,7},{6,4},{7,9},{8,6},{9,11},{10,... | collective-permute-start | bytes 2457608 | tf_op jit(solution)/shard_map/ppermute | solution.py:312
  36.2 5.5 %collective-permute-done.3.refs_3_ = bf16[80,5120]{1,0:T(8,128)(2,1)S(1)} collective-permute-done((bf16[80,5120]{1,0:T(8,128)(2,1)S(1)}, bf16[80,5120]{1,0:T(8,128)(2,1)S(1)}, u32[]{:S(2)}, u32[]{:S(2)}) %collective-permute-start.3) | collective-permute-done | bytes 819232 | tf_op jit(solution)/shard_map/ppermute | solution.py:312
  41.7 3.2 %copy-done = bf16[1,5120,3,256]{3,1,2,0:T(8,128)(2,1)S(1)} copy-done((bf16[1,5120,3,256]{3,1,2,0:T(8,128)(2,1)S(1)}, bf16[1,5120,3,256]{3,1,2,0:T(8,128)(2,1)}, u32[]{:S(2)}) %copy-start) | copy-done | bytes 7864344
  45.0 1.1 %copy-done.4 = bf16[80,5120]{1,0:T(8,128)(2,1)S(1)} copy-done((bf16[80,5120]{1,0:T(8,128)(2,1)S(1)}, bf16[80,5120]{1,0:T(8,128)(2,1)}, u32[]{:S(2)}) %copy-start.4) | copy-done | bytes 819224
  46.1 0.9 copy-done.6
  47.0 0.8 copy-done.8
  47.8 9.1 %project_rows.3 = (bf16[4,320,128]{2,1,0:T(8,128)(2,1)S(1)}, bf16[8,320,128]{2,1,0:T(8,128)(2,1)S(1)}) custom-call(bf16[80,5120]{1,0:T(8,128)(2,1)S(1)} %copy-done.2, bf16[80,5120]{1,0:T(8,128)(2,1)S(1)} %copy-done.4, bf16[80,5120]{1,0:T(8,128)(2,1)S(1)} %collective-permute-done.refs_2_, bf16[80,5120]{1,0:T(8,128)(2,1)S(1)} %collective-permute-done.3.refs_3_, ...), custom_call_target="tpu_custom_call" | custom-call | flops 5033164800 | bytes 15728640 | tf_op jit(solution)/shard_map/project_rows/pallas_call | solution.py:192
  56.9 3.6 %collective-permute-start.5 = (bf16[80,5120]{1,0:T(8,128)(2,1)S(1)}, bf16[80,5120]{1,0:T(8,128)(2,1)S(1)}, u32[]{:S(2)}, u32[]{:S(2)}) collective-permute-start(bf16[80,5120]{1,0:T(8,128)(2,1)S(1)} %collective-permute-done.2.refs_0_), channel_id=1, source_target_pairs={{0,14},{1,3},{2,0},{3,5},{4,2},{5,7},{6,4},{7,9},{8,6},{9,11},{10,... | collective-permute-start | bytes 2457608 | tf_op jit(solution)/shard_map/ppermute | solution.py:312
  60.4 1.0 collective-permute-start.7
  61.5 6.8 %project_rows.4 = (bf16[4,160,128]{2,1,0:T(8,128)(2,1)S(1)}, bf16[8,160,128]{2,1,0:T(8,128)(2,1)S(1)}, bf16[6,5120,256]{2,1,0:T(8,128)(2,1)S(1)}) custom-call(bf16[80,5120]{1,0:T(8,128)(2,1)S(1)} %collective-permute-done.2.refs_0_, bf16[80,5120]{1,0:T(8,128)(2,1)S(1)} %collective-permute-done.6.refs_1_, bf16[3,5120,256]{2,1,0:T(8,128)(2,1)S(1)} %bitcast.22, ...), custom_call_target="tpu_custom_call" | custom-call | flops 2516582400 | bytes 15728640 | tf_op jit(solution)/shard_map/project_rows/pallas_call | solution.py:192
  68.3 10.5 %collective-permute-done.5.refs_0_ = bf16[80,5120]{1,0:T(8,128)(2,1)S(1)} collective-permute-done((bf16[80,5120]{1,0:T(8,128)(2,1)S(1)}, bf16[80,5120]{1,0:T(8,128)(2,1)S(1)}, u32[]{:S(2)}, u32[]{:S(2)}) %collective-permute-start.5) | collective-permute-done | bytes 819232 | tf_op jit(solution)/shard_map/ppermute | solution.py:312
  78.7 1.4 %collective-permute-done.9.refs_1_ = bf16[80,5120]{1,0:T(8,128)(2,1)S(1)} collective-permute-done((bf16[80,5120]{1,0:T(8,128)(2,1)S(1)}, bf16[80,5120]{1,0:T(8,128)(2,1)S(1)}, u32[]{:S(2)}, u32[]{:S(2)}) %collective-permute-start.9) | collective-permute-done | bytes 819232 | tf_op jit(solution)/shard_map/ppermute | solution.py:312
  80.1 2.7 %project_rows.5 = (bf16[4,320,128]{2,1,0:T(8,128)(2,1)S(1)}, bf16[8,320,128]{2,1,0:T(8,128)(2,1)S(1)}) custom-call(bf16[80,5120]{1,0:T(8,128)(2,1)S(1)} %collective-permute-done.5.refs_0_, bf16[80,5120]{1,0:T(8,128)(2,1)S(1)} %collective-permute-done.9.refs_1_, bf16[6,5120,256]{2,1,0:T(8,128)(2,1)S(1)} %get-tuple-element.59.refs_2_, ...), custom_call_target="tpu_custom_call" | custom-call | flops 2516582400 | bytes 1638400 | tf_op jit(solution)/shard_map/project_rows/pallas_call | solution.py:192
  83.2 2.1 %collective-permute-done.10.refs_5_ = bf16[8,320,128]{2,1,0:T(8,128)(2,1)S(1)} collective-permute-done((bf16[8,320,128]{2,1,0:T(8,128)(2,1)S(1)}, bf16[8,320,128]{2,1,0:T(8,128)(2,1)S(1)}, u32[]{:S(2)}, u32[]{:S(2)}) %collective-permute-start.10) | collective-permute-done | bytes 655392 | tf_op jit(solution)/shard_map/ppermute | solution.py:315
  85.3 8.2 %attend.1 = f32[2,8,32,80]{3,2,1,0:T(8,128)} custom-call(s32[8]{0:T(128)S(1)} %get-tuple-element.40.place_ref, f32[1,1280]{1,0:T(1,128)S(1)} %reshape.56.bias_ref, bf16[2,64,128]{2,1,0:T(8,128)(2,1)S(1)} %bitcast.24, bf16[2,64,128]{2,1,0:T(8,128)(2,1)S(1)} %collective-permute-done.8.hb_ref, bf16[4,320,128]{2,1,0:T(8,128)(2,1)S(1)} %get-tuple-element.57.refs_0_, ...), custom_call_target="tpu_custom_call" | custom-call | flops 1677721600 | bytes 10000000 | tf_op jit(solution)/shard_map/attend/pallas_call | solution.py:262
  93.5 4.6 %all-to-all-start = ((f32[16,32,80]{2,1,0:T(8,128)}), f32[16,32,80]{2,1,0:T(8,128)S(1)}, u32[]{:S(2)}, u32[]{:S(2)}) async-start(f32[16,32,80]{2,1,0:T(8,128)} %bitcast.13), calls=%async_computation | async-start | bytes 524288 | tf_op jit(solution)/shard_map/all_to_all | solution.py:374
  98.1 10.5 %all-to-all-done = f32[16,32,80]{2,1,0:T(8,128)S(1)} async-done(((f32[16,32,80]{2,1,0:T(8,128)}), f32[16,32,80]{2,1,0:T(8,128)S(1)}, u32[]{:S(2)}, u32[]{:S(2)}) %all-to-all-start) | async-done | bytes 163872 | tf_op jit(solution)/shard_map/all_to_all | solution.py:374
  (38 shorter events, 1.9 us)
Async XLA Ops:
  0.0 23.8 %copy-start.10 = (s32[8]{0:T(128)S(1)}, s32[8]{0:T(128)}, u32[]{:S(2)}) copy-start(s32[8]{0:T(128)} %constant.62.clone) | copy-start | bytes 100
  0.0 23.8 %copy-start.11 = (s32[8]{0:T(128)S(1)}, s32[8]{0:T(128)}, u32[]{:S(2)}) copy-start(s32[8]{0:T(128)} %constant.72) | copy-start | bytes 100
  5.5 8.1 %copy-start.2 = (bf16[80,5120]{1,0:T(8,128)(2,1)S(1)}, bf16[80,5120]{1,0:T(8,128)(2,1)}, u32[]{:S(2)}) copy-start(bf16[80,5120]{1,0:T(8,128)(2,1)} %own_rows.1.x_ref.refs_0_) | copy-start | bytes 2457604
  5.6 36.1 %collective-permute-start.4 = (bf16[3,5120,256]{2,1,0:T(8,128)(2,1)}, bf16[3,5120,256]{2,1,0:T(8,128)(2,1)}, u32[]{:S(2)}, u32[]{:S(2)}) collective-permute-start(bf16[3,5120,256]{2,1,0:T(8,128)(2,1)} %bitcast.18), channel_id=1, source_target_pairs={{0,1},{1,0},{2,3},{3,2},{4,5},{5,4},{6,7},{7,6},{8,9},{9,8},{10,11... | collective-permute-start | bytes 23592968 | tf_op jit(solution)/shard_map/ppermute | solution.py:315
  5.7 16.9 %collective-permute-start.1 = (bf16[80,5120]{1,0:T(8,128)(2,1)}, bf16[80,5120]{1,0:T(8,128)(2,1)S(1)}, u32[]{:S(2)}, u32[]{:S(2)}) collective-permute-start(bf16[80,5120]{1,0:T(8,128)(2,1)} %own_rows.1.x_ref.refs_0_), channel_id=1, source_target_pairs={{0,2},{1,15},{2,4},{3,1},{4,6},{5,3},{6,8},{7,5},{8,10},{9,7},{10,... | collective-permute-start | bytes 2457608 | tf_op jit(solution)/shard_map/ppermute | solution.py:312
  13.7 28.0 %copy-start.5 = (bf16[4,80,128]{2,1,0:T(8,128)(2,1)S(1)}, bf16[4,80,128]{2,1,0:T(8,128)(2,1)}, u32[]{:S(2)}) copy-start(bf16[4,80,128]{2,1,0:T(8,128)(2,1)} %get-tuple-element.45.refs_7_) | copy-start | bytes 245764
  13.7 28.0 %copy-start.7 = (bf16[2,80,128]{2,1,0:T(8,128)(2,1)S(1)}, bf16[2,80,128]{2,1,0:T(8,128)(2,1)}, u32[]{:S(2)}) copy-start(bf16[2,80,128]{2,1,0:T(8,128)(2,1)} %get-tuple-element.44.refs_6_) | copy-start | bytes 122884
  13.7 18.8 %collective-permute-start = (bf16[80,5120]{1,0:T(8,128)(2,1)S(1)}, bf16[80,5120]{1,0:T(8,128)(2,1)S(1)}, u32[]{:S(2)}, u32[]{:S(2)}) collective-permute-start(bf16[80,5120]{1,0:T(8,128)(2,1)S(1)} %copy-done.2), channel_id=1, source_target_pairs={{0,14},{1,3},{2,0},{3,5},{4,2},{5,7},{6,4},{7,9},{8,6},{9,11},{10,... | collective-permute-start | bytes 2457608 | tf_op jit(solution)/shard_map/ppermute | solution.py:312
  22.5 1.4 %copy-start.3 = (bf16[80,5120]{1,0:T(8,128)(2,1)}, bf16[80,5120]{1,0:T(8,128)(2,1)S(1)}, u32[]{:S(2)}) copy-start(bf16[80,5120]{1,0:T(8,128)(2,1)S(1)} %collective-permute-done.1.x_ref.refs_1_) | copy-start | bytes 2457604
  22.5 19.2 %collective-permute-start.3 = (bf16[80,5120]{1,0:T(8,128)(2,1)S(1)}, bf16[80,5120]{1,0:T(8,128)(2,1)S(1)}, u32[]{:S(2)}, u32[]{:S(2)}) collective-permute-start(bf16[80,5120]{1,0:T(8,128)(2,1)S(1)} %collective-permute-done.1.x_ref.refs_1_), channel_id=1, source_target_pairs={{0,2},{1,15},{2,4},{3,1},{4,6},{5,3},{6,8},{7,5},{8,10},{9,7},{10,... | collective-permute-start | bytes 2457608 | tf_op jit(solution)/shard_map/ppermute | solution.py:312
  32.5 24.4 %collective-permute-start.2 = (bf16[80,5120]{1,0:T(8,128)(2,1)S(1)}, bf16[80,5120]{1,0:T(8,128)(2,1)S(1)}, u32[]{:S(2)}, u32[]{:S(2)}) collective-permute-start(bf16[80,5120]{1,0:T(8,128)(2,1)S(1)} %collective-permute-done.refs_2_), channel_id=1, source_target_pairs={{0,14},{1,3},{2,0},{3,5},{4,2},{5,7},{6,4},{7,9},{8,6},{9,11},{10,... | collective-permute-start | bytes 2457608 | tf_op jit(solution)/shard_map/ppermute | solution.py:312
  41.7 18.7 %collective-permute-start.6 = (bf16[80,5120]{1,0:T(8,128)(2,1)S(1)}, bf16[80,5120]{1,0:T(8,128)(2,1)S(1)}, u32[]{:S(2)}, u32[]{:S(2)}) collective-permute-start(bf16[80,5120]{1,0:T(8,128)(2,1)S(1)} %collective-permute-done.3.refs_3_), channel_id=1, source_target_pairs={{0,2},{1,15},{2,4},{3,1},{4,6},{5,3},{6,8},{7,5},{8,10},{9,7},{10,... | collective-permute-start | bytes 2457608 | tf_op jit(solution)/shard_map/ppermute | solution.py:312
  41.7 3.2 %copy-start = (bf16[1,5120,3,256]{3,1,2,0:T(8,128)(2,1)S(1)}, bf16[1,5120,3,256]{3,1,2,0:T(8,128)(2,1)}, u32[]{:S(2)}) copy-start(bf16[1,5120,3,256]{3,1,2,0:T(8,128)(2,1)} %param.18) | copy-start | bytes 23592964
  45.0 1.1 %copy-start.4 = (bf16[80,5120]{1,0:T(8,128)(2,1)S(1)}, bf16[80,5120]{1,0:T(8,128)(2,1)}, u32[]{:S(2)}) copy-start(bf16[80,5120]{1,0:T(8,128)(2,1)} %copy-done.3) | copy-start | bytes 2457604
  46.1 0.9 copy-start.6
  47.0 0.8 copy-start.8
  47.8 13.7 %copy-start.9 = (bf16[1,2,128,64]{2,3,1,0:T(8,128)(2,1)S(1)}, bf16[1,2,128,64]{2,3,1,0:T(8,128)(2,1)}, u32[]{:S(2)}) copy-start(bf16[1,2,128,64]{2,3,1,0:T(8,128)(2,1)} %param.19) | copy-start | bytes 98308
  47.8 13.7 %copy-start.1 = (bf16[1,5120,3,256]{3,1,2,0:T(8,128)(2,1)S(1)}, bf16[1,5120,3,256]{3,1,2,0:T(8,128)(2,1)}, u32[]{:S(2)}) copy-start(bf16[1,5120,3,256]{3,1,2,0:T(8,128)(2,1)} %param.18) | copy-start | bytes 23592964
  56.9 21.9 %collective-permute-start.5 = (bf16[80,5120]{1,0:T(8,128)(2,1)S(1)}, bf16[80,5120]{1,0:T(8,128)(2,1)S(1)}, u32[]{:S(2)}, u32[]{:S(2)}) collective-permute-start(bf16[80,5120]{1,0:T(8,128)(2,1)S(1)} %collective-permute-done.2.refs_0_), channel_id=1, source_target_pairs={{0,14},{1,3},{2,0},{3,5},{4,2},{5,7},{6,4},{7,9},{8,6},{9,11},{10,... | collective-permute-start | bytes 2457608 | tf_op jit(solution)/shard_map/ppermute | solution.py:312
  60.4 19.7 %collective-permute-start.9 = (bf16[80,5120]{1,0:T(8,128)(2,1)S(1)}, bf16[80,5120]{1,0:T(8,128)(2,1)S(1)}, u32[]{:S(2)}, u32[]{:S(2)}) collective-permute-start(bf16[80,5120]{1,0:T(8,128)(2,1)S(1)} %collective-permute-done.6.refs_1_), channel_id=1, source_target_pairs={{0,2},{1,15},{2,4},{3,1},{4,6},{5,3},{6,8},{7,5},{8,10},{9,7},{10,... | collective-permute-start | bytes 2457608 | tf_op jit(solution)/shard_map/ppermute | solution.py:312
  60.4 7.8 %collective-permute-start.7 = (bf16[8,320,128]{2,1,0:T(8,128)(2,1)S(1)}, bf16[8,320,128]{2,1,0:T(8,128)(2,1)S(1)}, u32[]{:S(2)}, u32[]{:S(2)}) collective-permute-start(bf16[8,320,128]{2,1,0:T(8,128)(2,1)S(1)} %get-tuple-element.54.refs_2_), channel_id=1, source_target_pairs={{0,1},{1,0},{2,3},{3,2},{4,5},{5,4},{6,7},{7,6},{8,9},{9,8},{10,11... | collective-permute-start | bytes 1966088 | tf_op jit(solution)/shard_map/ppermute | solution.py:315
  61.5 6.8 %collective-permute-start.8 = (bf16[2,64,128]{2,1,0:T(8,128)(2,1)S(1)}, bf16[2,64,128]{2,1,0:T(8,128)(2,1)S(1)}, u32[]{:S(2)}, u32[]{:S(2)}) collective-permute-start(bf16[2,64,128]{2,1,0:T(8,128)(2,1)S(1)} %bitcast.23), channel_id=1, source_target_pairs={{0,1},{1,0},{2,3},{3,2},{4,5},{5,4},{6,7},{7,6},{8,9},{9,8},{10,11... | collective-permute-start | bytes 98312 | tf_op jit(solution)/shard_map/ppermute | solution.py:315
  82.9 2.4 %collective-permute-start.10 = (bf16[8,320,128]{2,1,0:T(8,128)(2,1)S(1)}, bf16[8,320,128]{2,1,0:T(8,128)(2,1)S(1)}, u32[]{:S(2)}, u32[]{:S(2)}) collective-permute-start(bf16[8,320,128]{2,1,0:T(8,128)(2,1)S(1)} %get-tuple-element.63.refs_3_), channel_id=1, source_target_pairs={{0,1},{1,0},{2,3},{3,2},{4,5},{5,4},{6,7},{7,6},{8,9},{9,8},{10,11... | collective-permute-start | bytes 1966088 | tf_op jit(solution)/shard_map/ppermute | solution.py:315
  93.5 15.1 %all-to-all-start = ((f32[16,32,80]{2,1,0:T(8,128)}), f32[16,32,80]{2,1,0:T(8,128)S(1)}, u32[]{:S(2)}, u32[]{:S(2)}) async-start(f32[16,32,80]{2,1,0:T(8,128)} %bitcast.13), calls=%async_computation | async-start | bytes 524288 | tf_op jit(solution)/shard_map/all_to_all | solution.py:374

commit v7 on v6

--- a/solution.py
+++ b/solution.py
@@ -198,7 +198,7 @@
         out_specs=[vmem] * len(out_shape),
         out_shape=out_shape,
         scratch_shapes=scratch,
-        compiler_params=pltpu.CompilerParams(vmem_limit_bytes=(10 if keep or not fetch else 40) * MIB),
+        compiler_params=pltpu.CompilerParams(vmem_limit_bytes=(10 if keep or not fetch else 58) * MIB),
         cost_estimate=pl.CostEstimate(
             flops=2 * total * width * 6 * columns,
             bytes_accessed=12 * width * columns if fetch else 2 * total * width,

time: 110 us -> 109 us (level)
  Pallas kernels: 43.6 us -> 48.6 us
  waiting for transfers between devices: 37.3 us -> 33.6 us
  local copies, waits for them, and re-layouts: 6.15 us -> 4.22 us
    pallas_call x3, Pallas kernels: 18.5 us -> 23.6 us  [project(): pl.pallas_call(functools.partial(project_kernel, sizes=sizes, fetch=fetch...]
    ppermute x7, waiting for transfers between devices: 24.7 us -> 21.1 us  [hop(): return lax.ppermute(block, 'seq', route)]
    unnamed x24 -> x20, local copies, waits for them, and re-layouts: 6.07 us -> 4.13 us
  transfers between devices with their start and end apart: 12 -> 12, of which waited for: 7 -> 7; matrix products, arithmetic and copies ran while one was open for 0% -> 0% of each run, Pallas kernels for 25% -> 30%
where the time goes in v7:
time: 109 us
  Pallas kernels  48.6 us (45%)
  waiting for transfers between devices  33.6 us (31%)
  starting transfers between devices  20.2 us (19%)
  local copies, waits for them, and re-layouts  4.22 us (4%)
  between operations  1.53 us (1%)
    pallas_call x3, Pallas kernels, project(): pl.pallas_call(functools.partial(project_kernel, sizes=sizes, fetch=fetch...  23.6 us
    ppermute x7, waiting for transfers between devices, hop(): return lax.ppermute(block, 'seq', route)  21.1 us
    ppermute x7, starting transfers between devices, hop(): return lax.ppermute(block, 'seq', route)  14 us
    pallas_call x2, Pallas kernels, project_first(): pl.pallas_call(project_first_kernel, in_specs=[vmem, pl.BlockSpec(memory_...  12 us
    all_to_all x1, waiting for transfers between devices, local(): lax.all_to_all(terms, ('group', 'seq'), 0, 0, axis_index_groups=same_core...  10.4 us
    pallas_call x1, Pallas kernels, attend(): pl.pallas_call(functools.partial(attend_kernel, calls=calls, rows=rows, s...  8.22 us
    all_to_all x1, starting transfers between devices, local(): lax.all_to_all(terms, ('group', 'seq'), 0, 0, axis_index_groups=same_core...  5.28 us
    pallas_call x1, Pallas kernels, own_rows(): pl.pallas_call(functools.partial(own_rows_kernel, levels=levels, cuts=cut...  4.87 us
  transfers between devices with their start and end apart: 12, of which 7 were waited for; matrix products, arithmetic and copies ran while one was open for 0% of the time, Pallas kernels for 30%

profile of v7, /device:TPU:16, one launch (start us, length us, event | category | flops | bytes accessed | tf_op | source)
XLA Modules:
  0.0 109.0 jit_solution(2540801901934216560)
XLA Ops:
  0.7 4.9 %own_rows.1.x_ref.refs_0_ = bf16[80,5120]{1,0:T(8,128)(2,1)} custom-call(s32[1]{0:T(128)S(6)} %copy.13.step_ref, bf16[80,5120]{1,0:T(8,128)(2,1)} %bitcast.25, f32[2,5120]{1,0:T(2,128)} %mod_any.1, bf16[64,5120]{1,0:T(8,128)(2,1)} %bitcast.27, bf16[64,80]{1,0:T(8,128)(2,1)} %bitcast.30, bf16[80,5120]{1,0:T(8,128)(2,1)} %bitcast.26, ...), custom_call_target="tpu_custom_call" | custom-call | flops 200000000 | bytes 5000000 | tf_op jit(solution)/shard_map/own_rows/pallas_call | solution.py:73
  5.7 2.0 %collective-permute-start.1 = (bf16[80,5120]{1,0:T(8,128)(2,1)}, bf16[80,5120]{1,0:T(8,128)(2,1)S(1)}, u32[]{:S(2)}, u32[]{:S(2)}) collective-permute-start(bf16[80,5120]{1,0:T(8,128)(2,1)} %own_rows.1.x_ref.refs_0_), channel_id=1, source_target_pairs={{0,2},{1,15},{2,4},{3,1},{4,6},{5,3},{6,8},{7,5},{8,10},{9,7},{10,... | collective-permute-start | bytes 2457608 | tf_op jit(solution)/shard_map/ppermute | solution.py:312
  7.7 6.0 %project_first.2 = (bf16[2,80,128]{2,1,0:T(8,128)(2,1)}, bf16[4,80,128]{2,1,0:T(8,128)(2,1)}) custom-call(bf16[80,5120]{1,0:T(8,128)(2,1)} %own_rows.1.x_ref.refs_0_, bf16[3,5120,256]{2,1,0:T(8,128)(2,1)} %bitcast.19), custom_call_target="tpu_custom_call" | custom-call | flops 629145600 | bytes 7864320 | tf_op jit(solution)/shard_map/project_first/pallas_call | solution.py:105
  13.7 4.1 %collective-permute-start = (bf16[80,5120]{1,0:T(8,128)(2,1)S(1)}, bf16[80,5120]{1,0:T(8,128)(2,1)S(1)}, u32[]{:S(2)}, u32[]{:S(2)}) collective-permute-start(bf16[80,5120]{1,0:T(8,128)(2,1)S(1)} %copy-done.4), channel_id=1, source_target_pairs={{0,14},{1,3},{2,0},{3,5},{4,2},{5,7},{6,4},{7,9},{8,6},{9,11},{10,... | collective-permute-start | bytes 2457608 | tf_op jit(solution)/shard_map/ppermute | solution.py:312
  17.7 4.8 %collective-permute-done.1.x_ref.refs_1_ = bf16[80,5120]{1,0:T(8,128)(2,1)S(1)} collective-permute-done((bf16[80,5120]{1,0:T(8,128)(2,1)}, bf16[80,5120]{1,0:T(8,128)(2,1)S(1)}, u32[]{:S(2)}, u32[]{:S(2)}) %collective-permute-start.1) | collective-permute-done | bytes 819232 | tf_op jit(solution)/shard_map/ppermute | solution.py:312
  22.6 0.6 collective-permute-start.3
  24.0 6.0 %project_first.3 = (bf16[2,80,128]{2,1,0:T(8,128)(2,1)}, bf16[4,80,128]{2,1,0:T(8,128)(2,1)}) custom-call(bf16[80,5120]{1,0:T(8,128)(2,1)} %copy-done.5, bf16[3,5120,256]{2,1,0:T(8,128)(2,1)} %bitcast.20), custom_call_target="tpu_custom_call" | custom-call | flops 1887436800 | bytes 23592960 | tf_op jit(solution)/shard_map/project_first/pallas_call | solution.py:105
  30.0 2.5 %collective-permute-done.refs_2_ = bf16[80,5120]{1,0:T(8,128)(2,1)S(1)} collective-permute-done((bf16[80,5120]{1,0:T(8,128)(2,1)S(1)}, bf16[80,5120]{1,0:T(8,128)(2,1)S(1)}, u32[]{:S(2)}, u32[]{:S(2)}) %collective-permute-start) | collective-permute-done | bytes 819232 | tf_op jit(solution)/shard_map/ppermute | solution.py:312
  32.5 3.7 %collective-permute-start.2 = (bf16[80,5120]{1,0:T(8,128)(2,1)S(1)}, bf16[80,5120]{1,0:T(8,128)(2,1)S(1)}, u32[]{:S(2)}, u32[]{:S(2)}) collective-permute-start(bf16[80,5120]{1,0:T(8,128)(2,1)S(1)} %collective-permute-done.refs_2_), channel_id=1, source_target_pairs={{0,14},{1,3},{2,0},{3,5},{4,2},{5,7},{6,4},{7,9},{8,6},{9,11},{10,... | collective-permute-start | bytes 2457608 | tf_op jit(solution)/shard_map/ppermute | solution.py:312
  36.2 5.5 %collective-permute-done.3.refs_3_ = bf16[80,5120]{1,0:T(8,128)(2,1)S(1)} collective-permute-done((bf16[80,5120]{1,0:T(8,128)(2,1)S(1)}, bf16[80,5120]{1,0:T(8,128)(2,1)S(1)}, u32[]{:S(2)}, u32[]{:S(2)}) %collective-permute-start.3) | collective-permute-done | bytes 819232 | tf_op jit(solution)/shard_map/ppermute | solution.py:312
  41.7 0.9 copy-done.6
  42.6 14.1 %project_rows.3 = (bf16[4,320,128]{2,1,0:T(8,128)(2,1)}, bf16[8,320,128]{2,1,0:T(8,128)(2,1)}) custom-call(bf16[80,5120]{1,0:T(8,128)(2,1)} %own_rows.1.x_ref.refs_0_, bf16[80,5120]{1,0:T(8,128)(2,1)} %copy-done.5, bf16[80,5120]{1,0:T(8,128)(2,1)} %copy-done.7, bf16[80,5120]{1,0:T(8,128)(2,1)} %copy-done.6, bf16[3,5120,256]{2,1,0:T(8,128)(2,1)} %bitcast.21, ...), custom_call_target="tpu_custom_call" | custom-call | flops 5033164800 | bytes 15728640 | tf_op jit(solution)/shard_map/project_rows/pallas_call | solution.py:192
  56.7 3.6 %collective-permute-start.5 = (bf16[80,5120]{1,0:T(8,128)(2,1)S(1)}, bf16[80,5120]{1,0:T(8,128)(2,1)S(1)}, u32[]{:S(2)}, u32[]{:S(2)}) collective-permute-start(bf16[80,5120]{1,0:T(8,128)(2,1)S(1)} %collective-permute-done.2.refs_0_), channel_id=1, source_target_pairs={{0,14},{1,3},{2,0},{3,5},{4,2},{5,7},{6,4},{7,9},{8,6},{9,11},{10,... | collective-permute-start | bytes 2457608 | tf_op jit(solution)/shard_map/ppermute | solution.py:312
  60.5 0.4 collective-permute-start.8
  60.9 3.2 %copy-done = bf16[1,5120,3,256]{3,1,2,0:T(8,128)(2,1)S(1)} copy-done((bf16[1,5120,3,256]{3,1,2,0:T(8,128)(2,1)S(1)}, bf16[1,5120,3,256]{3,1,2,0:T(8,128)(2,1)}, u32[]{:S(2)}) %copy-start) | copy-done | bytes 7864344
  64.1 6.7 %project_rows.4 = (bf16[4,160,128]{2,1,0:T(8,128)(2,1)S(1)}, bf16[8,160,128]{2,1,0:T(8,128)(2,1)S(1)}, bf16[6,5120,256]{2,1,0:T(8,128)(2,1)S(1)}) custom-call(bf16[80,5120]{1,0:T(8,128)(2,1)S(1)} %collective-permute-done.2.refs_0_, bf16[80,5120]{1,0:T(8,128)(2,1)S(1)} %collective-permute-done.6.refs_1_, bf16[3,5120,256]{2,1,0:T(8,128)(2,1)S(1)} %bitcast.22, ...), custom_call_target="tpu_custom_call" | custom-call | flops 2516582400 | bytes 15728640 | tf_op jit(solution)/shard_map/project_rows/pallas_call | solution.py:192
  70.9 7.6 %collective-permute-done.5.refs_0_ = bf16[80,5120]{1,0:T(8,128)(2,1)S(1)} collective-permute-done((bf16[80,5120]{1,0:T(8,128)(2,1)S(1)}, bf16[80,5120]{1,0:T(8,128)(2,1)S(1)}, u32[]{:S(2)}, u32[]{:S(2)}) %collective-permute-start.5) | collective-permute-done | bytes 819232 | tf_op jit(solution)/shard_map/ppermute | solution.py:312
  78.4 0.7 collective-permute-done.9.refs_1_
  79.2 2.7 %project_rows.5 = (bf16[4,320,128]{2,1,0:T(8,128)(2,1)S(1)}, bf16[8,320,128]{2,1,0:T(8,128)(2,1)S(1)}) custom-call(bf16[80,5120]{1,0:T(8,128)(2,1)S(1)} %collective-permute-done.5.refs_0_, bf16[80,5120]{1,0:T(8,128)(2,1)S(1)} %collective-permute-done.9.refs_1_, bf16[6,5120,256]{2,1,0:T(8,128)(2,1)S(1)} %get-tuple-element.59.refs_2_, ...), custom_call_target="tpu_custom_call" | custom-call | flops 2516582400 | bytes 1638400 | tf_op jit(solution)/shard_map/project_rows/pallas_call | solution.py:192
  82.3 2.1 %collective-permute-done.10.refs_5_ = bf16[8,320,128]{2,1,0:T(8,128)(2,1)S(1)} collective-permute-done((bf16[8,320,128]{2,1,0:T(8,128)(2,1)S(1)}, bf16[8,320,128]{2,1,0:T(8,128)(2,1)S(1)}, u32[]{:S(2)}, u32[]{:S(2)}) %collective-permute-start.10) | collective-permute-done | bytes 655392 | tf_op jit(solution)/shard_map/ppermute | solution.py:315
  84.3 8.2 %attend.1 = f32[2,8,32,80]{3,2,1,0:T(8,128)} custom-call(s32[8]{0:T(128)S(1)} %get-tuple-element.40.place_ref, f32[1,1280]{1,0:T(1,128)S(1)} %reshape.56.bias_ref, bf16[2,64,128]{2,1,0:T(8,128)(2,1)S(1)} %bitcast.24, bf16[2,64,128]{2,1,0:T(8,128)(2,1)S(1)} %collective-permute-done.8.hb_ref, bf16[4,320,128]{2,1,0:T(8,128)(2,1)S(1)} %copy-done.2, ...), custom_call_target="tpu_custom_call" | custom-call | flops 1677721600 | bytes 10000000 | tf_op jit(solution)/shard_map/attend/pallas_call | solution.py:262
  92.6 5.3 %all-to-all-start = ((f32[16,32,80]{2,1,0:T(8,128)}), f32[16,32,80]{2,1,0:T(8,128)S(1)}, u32[]{:S(2)}, u32[]{:S(2)}) async-start(f32[16,32,80]{2,1,0:T(8,128)} %bitcast.13), calls=%async_computation | async-start | bytes 524288 | tf_op jit(solution)/shard_map/all_to_all | solution.py:374
  97.9 10.4 %all-to-all-done = f32[16,32,80]{2,1,0:T(8,128)S(1)} async-done(((f32[16,32,80]{2,1,0:T(8,128)}), f32[16,32,80]{2,1,0:T(8,128)S(1)}, u32[]{:S(2)}, u32[]{:S(2)}) %all-to-all-start) | async-done | bytes 163872 | tf_op jit(solution)/shard_map/all_to_all | solution.py:374
  108.3 0.6 bitcast_select_fusion
  (34 shorter events, 0.9 us)
Async XLA Ops:
  0.0 23.8 %copy-start.8 = (s32[8]{0:T(128)S(1)}, s32[8]{0:T(128)}, u32[]{:S(2)}) copy-start(s32[8]{0:T(128)} %constant.62.clone) | copy-start | bytes 100
  0.0 23.8 %copy-start.9 = (s32[8]{0:T(128)S(1)}, s32[8]{0:T(128)}, u32[]{:S(2)}) copy-start(s32[8]{0:T(128)} %constant.72) | copy-start | bytes 100
  5.6 8.1 %copy-start.4 = (bf16[80,5120]{1,0:T(8,128)(2,1)S(1)}, bf16[80,5120]{1,0:T(8,128)(2,1)}, u32[]{:S(2)}) copy-start(bf16[80,5120]{1,0:T(8,128)(2,1)} %own_rows.1.x_ref.refs_0_) | copy-start | bytes 2457604
  5.6 36.1 %collective-permute-start.4 = (bf16[3,5120,256]{2,1,0:T(8,128)(2,1)}, bf16[3,5120,256]{2,1,0:T(8,128)(2,1)}, u32[]{:S(2)}, u32[]{:S(2)}) collective-permute-start(bf16[3,5120,256]{2,1,0:T(8,128)(2,1)} %bitcast.18), channel_id=1, source_target_pairs={{0,1},{1,0},{2,3},{3,2},{4,5},{5,4},{6,7},{7,6},{8,9},{9,8},{10,11... | collective-permute-start | bytes 23592968 | tf_op jit(solution)/shard_map/ppermute | solution.py:315
  5.7 16.9 %collective-permute-start.1 = (bf16[80,5120]{1,0:T(8,128)(2,1)}, bf16[80,5120]{1,0:T(8,128)(2,1)S(1)}, u32[]{:S(2)}, u32[]{:S(2)}) collective-permute-start(bf16[80,5120]{1,0:T(8,128)(2,1)} %own_rows.1.x_ref.refs_0_), channel_id=1, source_target_pairs={{0,2},{1,15},{2,4},{3,1},{4,6},{5,3},{6,8},{7,5},{8,10},{9,7},{10,... | collective-permute-start | bytes 2457608 | tf_op jit(solution)/shard_map/ppermute | solution.py:312
  13.7 18.8 %collective-permute-start = (bf16[80,5120]{1,0:T(8,128)(2,1)S(1)}, bf16[80,5120]{1,0:T(8,128)(2,1)S(1)}, u32[]{:S(2)}, u32[]{:S(2)}) collective-permute-start(bf16[80,5120]{1,0:T(8,128)(2,1)S(1)} %copy-done.4), channel_id=1, source_target_pairs={{0,14},{1,3},{2,0},{3,5},{4,2},{5,7},{6,4},{7,9},{8,6},{9,11},{10,... | collective-permute-start | bytes 2457608 | tf_op jit(solution)/shard_map/ppermute | solution.py:312
  22.6 1.4 %copy-start.5 = (bf16[80,5120]{1,0:T(8,128)(2,1)}, bf16[80,5120]{1,0:T(8,128)(2,1)S(1)}, u32[]{:S(2)}) copy-start(bf16[80,5120]{1,0:T(8,128)(2,1)S(1)} %collective-permute-done.1.x_ref.refs_1_) | copy-start | bytes 2457604
  22.6 19.1 %collective-permute-start.3 = (bf16[80,5120]{1,0:T(8,128)(2,1)S(1)}, bf16[80,5120]{1,0:T(8,128)(2,1)S(1)}, u32[]{:S(2)}, u32[]{:S(2)}) collective-permute-start(bf16[80,5120]{1,0:T(8,128)(2,1)S(1)} %collective-permute-done.1.x_ref.refs_1_), channel_id=1, source_target_pairs={{0,2},{1,15},{2,4},{3,1},{4,6},{5,3},{6,8},{7,5},{8,10},{9,7},{10,... | collective-permute-start | bytes 2457608 | tf_op jit(solution)/shard_map/ppermute | solution.py:312
  32.5 9.2 %copy-start.7 = (bf16[80,5120]{1,0:T(8,128)(2,1)}, bf16[80,5120]{1,0:T(8,128)(2,1)S(1)}, u32[]{:S(2)}) copy-start(bf16[80,5120]{1,0:T(8,128)(2,1)S(1)} %collective-permute-done.refs_2_) | copy-start | bytes 2457604
  32.5 28.0 %copy-start.3 = (bf16[1,2,128,64]{2,3,1,0:T(8,128)(2,1)S(1)}, bf16[1,2,128,64]{2,3,1,0:T(8,128)(2,1)}, u32[]{:S(2)}) copy-start(bf16[1,2,128,64]{2,3,1,0:T(8,128)(2,1)} %param.19) | copy-start | bytes 98308
  32.5 24.2 %collective-permute-start.2 = (bf16[80,5120]{1,0:T(8,128)(2,1)S(1)}, bf16[80,5120]{1,0:T(8,128)(2,1)S(1)}, u32[]{:S(2)}, u32[]{:S(2)}) collective-permute-start(bf16[80,5120]{1,0:T(8,128)(2,1)S(1)} %collective-permute-done.refs_2_), channel_id=1, source_target_pairs={{0,14},{1,3},{2,0},{3,5},{4,2},{5,7},{6,4},{7,9},{8,6},{9,11},{10,... | collective-permute-start | bytes 2457608 | tf_op jit(solution)/shard_map/ppermute | solution.py:312
  41.7 0.9 copy-start.6
  41.7 18.7 %collective-permute-start.6 = (bf16[80,5120]{1,0:T(8,128)(2,1)S(1)}, bf16[80,5120]{1,0:T(8,128)(2,1)S(1)}, u32[]{:S(2)}, u32[]{:S(2)}) collective-permute-start(bf16[80,5120]{1,0:T(8,128)(2,1)S(1)} %collective-permute-done.3.refs_3_), channel_id=1, source_target_pairs={{0,2},{1,15},{2,4},{3,1},{4,6},{5,3},{6,8},{7,5},{8,10},{9,7},{10,... | collective-permute-start | bytes 2457608 | tf_op jit(solution)/shard_map/ppermute | solution.py:312
  56.7 21.7 %collective-permute-start.5 = (bf16[80,5120]{1,0:T(8,128)(2,1)S(1)}, bf16[80,5120]{1,0:T(8,128)(2,1)S(1)}, u32[]{:S(2)}, u32[]{:S(2)}) collective-permute-start(bf16[80,5120]{1,0:T(8,128)(2,1)S(1)} %collective-permute-done.2.refs_0_), channel_id=1, source_target_pairs={{0,14},{1,3},{2,0},{3,5},{4,2},{5,7},{6,4},{7,9},{8,6},{9,11},{10,... | collective-permute-start | bytes 2457608 | tf_op jit(solution)/shard_map/ppermute | solution.py:312
  60.3 18.8 %collective-permute-start.9 = (bf16[80,5120]{1,0:T(8,128)(2,1)S(1)}, bf16[80,5120]{1,0:T(8,128)(2,1)S(1)}, u32[]{:S(2)}, u32[]{:S(2)}) collective-permute-start(bf16[80,5120]{1,0:T(8,128)(2,1)S(1)} %collective-permute-done.6.refs_1_), channel_id=1, source_target_pairs={{0,2},{1,15},{2,4},{3,1},{4,6},{5,3},{6,8},{7,5},{8,10},{9,7},{10,... | collective-permute-start | bytes 2457608 | tf_op jit(solution)/shard_map/ppermute | solution.py:312
  60.3 10.5 %collective-permute-start.7 = (bf16[8,320,128]{2,1,0:T(8,128)(2,1)}, bf16[8,320,128]{2,1,0:T(8,128)(2,1)S(1)}, u32[]{:S(2)}, u32[]{:S(2)}) collective-permute-start(bf16[8,320,128]{2,1,0:T(8,128)(2,1)} %get-tuple-element.54.refs_2_), channel_id=1, source_target_pairs={{0,1},{1,0},{2,3},{3,2},{4,5},{5,4},{6,7},{7,6},{8,9},{9,8},{10,11... | collective-permute-start | bytes 1966088 | tf_op jit(solution)/shard_map/ppermute | solution.py:315
  60.5 10.3 %collective-permute-start.8 = (bf16[2,64,128]{2,1,0:T(8,128)(2,1)S(1)}, bf16[2,64,128]{2,1,0:T(8,128)(2,1)S(1)}, u32[]{:S(2)}, u32[]{:S(2)}) collective-permute-start(bf16[2,64,128]{2,1,0:T(8,128)(2,1)S(1)} %bitcast.23), channel_id=1, source_target_pairs={{0,1},{1,0},{2,3},{3,2},{4,5},{5,4},{6,7},{7,6},{8,9},{9,8},{10,11... | collective-permute-start | bytes 98312 | tf_op jit(solution)/shard_map/ppermute | solution.py:315
  60.9 3.2 %copy-start = (bf16[1,5120,3,256]{3,1,2,0:T(8,128)(2,1)S(1)}, bf16[1,5120,3,256]{3,1,2,0:T(8,128)(2,1)}, u32[]{:S(2)}) copy-start(bf16[1,5120,3,256]{3,1,2,0:T(8,128)(2,1)} %param.18) | copy-start | bytes 23592964
  79.2 5.2 %copy-start.1 = (bf16[8,320,128]{2,1,0:T(8,128)(2,1)S(1)}, bf16[8,320,128]{2,1,0:T(8,128)(2,1)}, u32[]{:S(2)}) copy-start(bf16[8,320,128]{2,1,0:T(8,128)(2,1)} %get-tuple-element.54.refs_2_) | copy-start | bytes 1966084
  79.2 5.2 %copy-start.2 = (bf16[4,320,128]{2,1,0:T(8,128)(2,1)S(1)}, bf16[4,320,128]{2,1,0:T(8,128)(2,1)}, u32[]{:S(2)}) copy-start(bf16[4,320,128]{2,1,0:T(8,128)(2,1)} %get-tuple-element.57.refs_0_) | copy-start | bytes 983044
  81.9 2.4 %collective-permute-start.10 = (bf16[8,320,128]{2,1,0:T(8,128)(2,1)S(1)}, bf16[8,320,128]{2,1,0:T(8,128)(2,1)S(1)}, u32[]{:S(2)}, u32[]{:S(2)}) collective-permute-start(bf16[8,320,128]{2,1,0:T(8,128)(2,1)S(1)} %get-tuple-element.63.refs_3_), channel_id=1, source_target_pairs={{0,1},{1,0},{2,3},{3,2},{4,5},{5,4},{6,7},{7,6},{8,9},{9,8},{10,11... | collective-permute-start | bytes 1966088 | tf_op jit(solution)/shard_map/ppermute | solution.py:315
  92.6 15.7 %all-to-all-start = ((f32[16,32,80]{2,1,0:T(8,128)}), f32[16,32,80]{2,1,0:T(8,128)S(1)}, u32[]{:S(2)}, u32[]{:S(2)}) async-start(f32[16,32,80]{2,1,0:T(8,128)} %bitcast.13), calls=%async_computation | async-start | bytes 524288 | tf_op jit(solution)/shard_map/all_to_all | solution.py:374
